TPU v7x, 128 devices: a whole 4x4x4 slice. The times are simulated.
128 devices in a mesh: group: 4 (over z), dev: 32 (over x, y, core).
Axes of the slice: x: 4, y: 4, z: 4, core: 2. Of those that a mesh axis runs over, the one named last changes fastest.
Arguments:
- blocks_in: float32 [3968, 8, 4096], P(('group', 'dev')), as said below
- counts: int32 [128], P(('group', 'dev')), may hold values from 1 to 31, as said below
Outputs:
- blocks_out: float32 [2048, 8, 4096], P(('group', 'dev'))
Inputs may be any that keep to these rules, and one draw needn't show every extreme that they name: `blocks_in`: every slot holds a state of positive density and pressure. Device i (in the order of group+dev) holds its live meshblocks in its first counts[i] slots, in curve order. The counts sum to 2048; for every device i, starts[i] - i * 16 lies in 0 .. 15.
All inputs are finite; a program needn't handle non-finite values.
Results may differ from a plain program's by a relative error of at most 0.0003.
Values sent between devices are 32-bit elements; how exact they have to be, the bound alone decides.
No kernel may reach another device: no remote copies, remote signals or barrier semaphores. Data moves between devices by JAX's collectives and lax.ppermute only.
A program may use at most 192 MiB of HBM per device.

v0:
```python
import jax
import jax.numpy as jnp
from jax import lax
from jax.sharding import PartitionSpec as P

BS = 16
BRICK_Y = 2
BRICK_Z = 8
BRICK_X = 1
BLK_DEV = 16


GAMMA = 5.0 / 3.0
COURANT = 0.25
DENSITY_FLOOR = 0.05
PRESSURE_FLOOR = 0.05


def with_halo(cells, sides, width):
    for axis, dim in sides:
        count = lax.axis_size(axis)
        head = lax.slice_in_dim(cells, 0, width, axis=dim)
        tail = lax.slice_in_dim(cells, cells.shape[dim] - width, cells.shape[dim], axis=dim)
        cells = jnp.concatenate(
            [
                lax.ppermute(tail, axis, [(i, (i + 1) % count) for i in range(count)]),
                cells,
                lax.ppermute(head, axis, [((i + 1) % count, i) for i in range(count)]),
            ],
            axis=dim,
        )
    return cells


def passed_along(value, axis, steps):
    count = lax.axis_size(axis)
    first, last = (max(0, -steps), min(count, count - steps))
    return lax.ppermute(value, axis, [(source, source + steps) for source in range(first, last)])


def trimmed(values, along, front, back):
    return lax.slice_in_dim(values, front, values.shape[along] - back, axis=along)


def primitive(state):
    density = jnp.maximum(state[0], DENSITY_FLOOR)
    velocity = state[1:4] / density
    magnetic = state[5:8]
    kinetic = 0.5 * density * jnp.sum(velocity * velocity, axis=0)
    magnetic_energy = 0.5 * jnp.sum(magnetic * magnetic, axis=0)
    pressure = jnp.maximum((GAMMA - 1.0) * (state[4] - kinetic - magnetic_energy), PRESSURE_FLOOR)
    return jnp.concatenate([density[None], velocity, pressure[None], magnetic], axis=0)


def conserved(prims):
    density = prims[0]
    velocity = prims[1:4]
    magnetic = prims[5:8]
    energy = (
        prims[4] / (GAMMA - 1.0)
        + 0.5 * density * jnp.sum(velocity * velocity, axis=0)
        + 0.5 * jnp.sum(magnetic * magnetic, axis=0)
    )
    return jnp.concatenate([density[None], density * velocity, energy[None], magnetic], axis=0)


def fast_speed(prims, normal):
    density = prims[0]
    sound = GAMMA * prims[4] / density
    alfven = jnp.sum(prims[5:8] * prims[5:8], axis=0) / density
    along_field = prims[5 + normal] * prims[5 + normal] / density
    total = sound + alfven
    root = jnp.sqrt(jnp.maximum(total * total - 4.0 * sound * along_field, 0.0))
    return jnp.sqrt(0.5 * (total + root))


def physical_flux(prims, state, normal):
    density = prims[0]
    velocity = prims[1:4]
    magnetic = prims[5:8]
    speed_normal = velocity[normal]
    field_normal = magnetic[normal]
    total_pressure = prims[4] + 0.5 * jnp.sum(magnetic * magnetic, axis=0)
    unit_normal = jnp.array(
        [1.0 if component == normal else 0.0 for component in range(3)], dtype=jnp.float32
    )
    unit_normal = unit_normal.reshape((3,) + (1,) * (velocity.ndim - 1))
    momentum_flux = (
        density * velocity * speed_normal - magnetic * field_normal + unit_normal * total_pressure
    )
    energy_flux = (state[4] + total_pressure) * speed_normal - field_normal * jnp.sum(
        velocity * magnetic, axis=0
    )
    induction = speed_normal * magnetic - velocity * field_normal
    return jnp.concatenate(
        [(density * speed_normal)[None], momentum_flux, energy_flux[None], induction], axis=0
    )


def hlle_flux(left, right, normal):
    state_left = conserved(left)
    state_right = conserved(right)
    flux_left = physical_flux(left, state_left, normal)
    flux_right = physical_flux(right, state_right, normal)
    fast_left = fast_speed(left, normal)
    fast_right = fast_speed(right, normal)
    upper = jnp.maximum(
        jnp.maximum(right[1 + normal] + fast_right, left[1 + normal] + fast_left), 0.0
    )
    lower = jnp.minimum(
        jnp.minimum(left[1 + normal] - fast_left, right[1 + normal] - fast_right), 0.0
    )
    return (upper * flux_left - lower * flux_right + upper * lower * (state_right - state_left)) / (
        upper - lower
    )


def minmod(first, second):
    return 0.5 * (jnp.sign(first) + jnp.sign(second)) * jnp.minimum(jnp.abs(first), jnp.abs(second))


def divergence(prims, along, normal):
    backward = trimmed(prims, along, 1, 1) - trimmed(prims, along, 0, 2)
    forward = trimmed(prims, along, 2, 0) - trimmed(prims, along, 1, 1)
    slope = minmod(backward, forward)
    left = trimmed(prims, along, 1, 2) + 0.5 * trimmed(slope, along, 0, 1)
    right = trimmed(prims, along, 2, 1) - 0.5 * trimmed(slope, along, 1, 0)
    flux = hlle_flux(left, right, normal)
    return trimmed(flux, along, 1, 0) - trimmed(flux, along, 0, 1)


def tendency(padded):
    prims = primitive(padded)
    across_x = trimmed(divergence(prims, 1, 0), 2, 2, 2)
    across_y = trimmed(divergence(prims, 2, 1), 1, 2, 2)
    wrapped = jnp.concatenate([prims[..., -2:], prims, prims[..., :2]], axis=3)
    across_z = trimmed(trimmed(divergence(wrapped, 3, 2), 1, 2, 2), 2, 2, 2)
    return -(across_x + across_y + across_z)


def signal_speed(state):
    prims = primitive(state)
    fastest = jnp.abs(prims[1]) + fast_speed(prims, 0)
    fastest = jnp.maximum(fastest, jnp.abs(prims[2]) + fast_speed(prims, 1))
    return jnp.maximum(fastest, jnp.abs(prims[3]) + fast_speed(prims, 2))


def global_speed(local_top):
    return lax.pmax(local_top, ("group", "dev"))


def with_ghosts(slab):
    return with_halo(slab, (("group", 1), ("dev", 2)), 2)


def body(blocks_in, counts):
    fields = blocks_in.shape[1]
    cells = blocks_in.shape[2]
    own_count = counts[0]
    every_count = lax.all_gather(counts, ("group", "dev"), axis=0, tiled=True)
    position = lax.axis_index(("group", "dev"))
    earlier = jnp.arange(every_count.shape[0], dtype=jnp.int32) < position
    start_here = jnp.sum(jnp.where(earlier, every_count, 0))
    surplus = start_here - position * BLK_DEV
    padded_slots = jnp.concatenate(
        [jnp.zeros((BLK_DEV, fields, cells), jnp.float32), blocks_in], axis=0
    )
    outgoing = lax.dynamic_slice_in_dim(padded_slots, own_count, BLK_DEV, 0)
    incoming = passed_along(outgoing, ("group", "dev"), 1)
    joined = jnp.concatenate([incoming, blocks_in], axis=0)
    mine = lax.dynamic_slice_in_dim(joined, BLK_DEV - surplus, BLK_DEV, 0)
    slab = mine.reshape(BRICK_X, BRICK_Y, BRICK_Z, fields, BS, BS, BS)
    slab = jnp.transpose(slab, (3, 0, 4, 1, 5, 2, 6)).reshape(
        fields, BRICK_X * BS, BRICK_Y * BS, BRICK_Z * BS
    )
    speed = global_speed(jnp.max(signal_speed(slab)))
    step = COURANT / speed
    first = slab + step * tendency(with_ghosts(slab))
    second = 0.5 * (slab + first + step * tendency(with_ghosts(first)))
    result = second.reshape(fields, BRICK_X, BS, BRICK_Y, BS, BRICK_Z, BS)
    return jnp.transpose(result, (1, 3, 5, 0, 2, 4, 6)).reshape(BLK_DEV, fields, cells)


def solution(mesh):
    in_specs = (P(("group", "dev"), None, None), P(("group", "dev")))
    out_specs = P(("group", "dev"), None, None)
    return jax.shard_map(body, mesh=mesh, in_specs=in_specs, out_specs=out_specs, check_vma=False)
```

profile of v0, /device:TPU:0, one launch (start us, length us, event | category | flops | bytes accessed | tf_op | source)
XLA Modules:
  0.0 553.9 jit_solution(638706342557418375)
XLA Ops:
  2.5 2.7 collective-permute-start
  5.2 83.7 %all-reduce.1 = s32[128]{0:T(128)S(1)} all-reduce(s32[128]{0:T(128)S(1)} %dynamic-update-slice), channel_id=1, replica_groups=mesh['group'=4,'dev'=32] {'group','dev'}, use_global_device_ids=true, to_apply=%add.1 | all-reduce | flops 128 | bytes 1024
  92.2 9.0 %reshape.280 = f32[1,2,8,8,16,16,16]{6,5,4,3,2,1,0:T(8,128)} reshape(f32[16,8,4096]{2,1,0:T(8,128)S(1)} %fusion.37) | data formatting | bytes 4194304 | tf_op jit(solution)/shard_map/reshape | solution.py:172
  101.2 8.6 %fusion.155 = (f32[1,1,16,2,16,8,16]{6,4,2,0,5,3,1:T(8,128)S(1)}, f32[16,2,16,8,16]{4,2,0,3,1:T(8,128)}, f32[1,1,16,2,16,8,16]{6,4,2,0,5,3,1:T(8,128)}, f32[1,1,...) fusion(f32[8,1,16,2,16,8,16]{6,4,2,0,5,3,1:T(8,128)} %bitcast.526), kind=kLoop, calls=%fused_computation.450 | loop fusion | flops 262144 | bytes 2883584 | tf_op jit(solution)/shard_map/slice | solution.py:51
  109.8 17.9 %copy.31 = f32[8,1,16,2,16,8,16]{6,5,4,3,2,0,1:T(8,128)} copy(f32[8,1,16,2,16,8,16]{6,4,2,0,5,3,1:T(8,128)} %bitcast.527) | data formatting | bytes 4194304 | tf_op jit(solution)/shard_map/transpose | solution.py:173
  129.5 2.8 copy.39
  133.5 2.8 copy.38
  137.6 2.8 copy.37
  141.7 2.8 copy.33
  145.0 10.3 %multiply_reduce_fusion = (f32[16,2,16,8,16]{4,2,0,3,1:T(8,128)}, f32[16,2,16,8,16]{4,2,0,3,1:T(8,128)}, f32[3,1,16,2,16,8,16]{6,4,2,0,5,3,1:T(8,128)}) fusion(f32[16,2,16,8,16]{4,2,0,3,1:T(8,128)} %get-tuple-element.118, f32[8,1,16,2,16,8,16]{6,4,2,0,5,3,1:T(8,128)} %bitcast.528), kind=kLoop, calls=%fused_computation.40 | loop fusion | flops 851968 | bytes 3145728 | tf_op jit(solution)/shard_map/reduce_sum | solution.py:49
  155.4 10.7 %reshape.281 = f32[8,16,32,128]{3,2,1,0:T(8,128)S(1)} reshape(f32[8,1,16,2,16,8,16]{6,5,4,3,2,0,1:T(8,128)} %copy.31) | data formatting | bytes 4194304 | tf_op jit(solution)/shard_map/reshape | solution.py:173
  166.1 4.9 copy.35
  171.0 2.8 reduce_sum.577
  174.5 2.8 collective-permute-start.2
  177.3 2.8 copy.36
  181.4 9.1 %copy.32 = f32[3,1,16,2,16,8,16]{6,5,4,3,2,0,1:T(8,128)} copy(f32[3,1,16,2,16,8,16]{6,4,2,0,5,3,1:T(8,128)} %get-tuple-element.123) | data formatting | bytes 1572864 | tf_op jit(solution)/shard_map/slice | solution.py:47
  190.4 4.3 slice.680
  197.5 5.1 collective-permute-start.4
  204.0 62.7 %pmax.7 = f32[]{:T(128)} all-reduce(f32[]{:T(128)} %fusion.122), channel_id=1, replica_groups=mesh['group'=4,'dev'=32] {'group','dev'}, use_global_device_ids=true, to_apply=%region_4.5 | all-reduce | flops 1 | bytes 8 | tf_op jit(solution)/shard_map/pmax | solution.py:149
  270.2 4.5 minimum_multiply_fusion.3
  275.7 9.8 %minimum_multiply_fusion.1 = f32[8,20,36,130]{3,2,1,0:T(8,128)} fusion(f32[8,20,36,2]{3,2,1,0:T(8,128)S(1)} %get-tuple-element.227, f32[3,20,36,128]{3,2,1,0:T(8,128)S(1)} %get-tuple-element.114, f32[1,20,36,128]{3,2,1,0:T(8,128)S(1)} %fusion.74, f32[3,20,36,128]{3,2,1,0:T(8,128)S(1)} %get-tuple-element.291, ...), kind=kLoop, calls=%fused_computation.37 | loop fusion | flops 17222400 | bytes 6036480 | tf_op jit(solution)/shard_map/mul | solution.py:119
  285.5 6.8 %pad_maximum_fusion.10 = (f32[8,20,36,130]{3,2,1,0:T(8,128)}, f32[8,20,36,130]{3,2,1,0:T(8,128)}) fusion(f32[8,20,36,2]{3,2,1,0:T(8,128)S(1)} %get-tuple-element.227, f32[3,20,36,128]{3,2,1,0:T(8,128)S(1)} %get-tuple-element.114, f32[1,20,36,128]{3,2,1,0:T(8,128)S(1)} %fusion.74, f32[3,20,36,128]{3,2,1,0:T(8,128)S(1)} %get-tuple-element.291, ...), kind=kLoop, calls=%fused_computation.18 | loop fusion | flops 5990400 | bytes 9031680 | tf_op jit(solution)/shard_map/concatenate | solution.py:136
  295.0 4.1 fusion.16
  305.7 2.5 multiply_add_fusion.10
  308.2 3.4 fusion.31
  311.6 2.8 fusion.163
  318.6 3.2 fusion.19
  321.8 3.1 fusion.160
  324.9 10.7 %fusion.3 = (f32[8,20,36,129]{3,2,1,0:T(8,128)S(1)}, f32[8,20,36,129]{3,2,1,0:T(8,128)S(1)}) fusion(f32[8,20,36,130]{3,2,1,0:T(8,128)} %minimum_multiply_fusion.1, f32[8,20,36,130]{3,2,1,0:T(8,128)} %get-tuple-element.224, f32[8,20,36,130]{3,2,1,0:T(8,128)} %get-tuple-element.225), kind=kLoop, calls=%fused_computation.12 | loop fusion | flops 2972160 | bytes 17832960 | tf_op jit(solution)/shard_map/sub | solution.py:127
  336.4 2.2 multiply_reduce_fusion.11
  338.7 2.2 fusion.57
  340.9 2.3 fusion.60
  343.2 3.3 multiply_bitcast_fusion.1
  348.2 7.4 %multiply_add_fusion.2 = (f32[3,20,36,129]{3,2,1,0:T(8,128)}, f32[3,20,36,129]{3,2,1,0:T(8,128)}, f32[3,20,36,129]{3,2,1,0:T(8,128)}, f32[3,20,36,129]{3,2,1,0:T...) fusion(f32[20,36,129]{2,1,0:T(8,128)S(1)} %get-tuple-element.134, ...), kind=kLoop, calls=%fused_computation.117 | loop fusion | flops 5015520 | bytes 14117772 | tf_op jit(solution)/shard_map/add | solution.py:89
  355.6 9.1 %fusion.6 = f32[8,20,36,129]{3,2,1,0:T(8,128)S(1)} fusion(f32[3,20,36,129]{3,2,1,0:T(8,128)} %get-tuple-element.287, f32[1,20,36,129]{3,2,1,0:T(8,128)} %get-tuple-element.111, f32[3,20,36,129]{3,2,1,0:T(8,128)} %get-tuple-element.288, f32[1,20,36,129]{3,2,1,0:T(8,128)} %get-tuple-element.160, f32[3,20,36,129]{3,2,1,0:T(8,128)} %get-tuple-element.126, ...), kind=kLoop, calls=%fused_computation.23 | loop fusion | flops 14117760 | bytes 16346880 | tf_op jit(solution)/shard_map/div | solution.py:113
  367.9 3.8 fusion.47
  375.0 6.2 %collective-permute-done.5 = f32[8,2,32,128]{3,2,1,0:T(8,128)S(1)} collective-permute-done((f32[8,2,32,128]{3,2,1,0:T(8,128)S(1)}, f32[8,2,32,128]{3,2,1,0:T(8,128)S(1)}, u32[]{:S(2)}, u32[]{:S(2)}) %collective-permute-start.5) | collective-permute-done | bytes 262176 | tf_op jit(solution)/shard_map/ppermute | solution.py:26
  381.4 5.2 collective-permute-start.8
  386.6 2.8 collective-permute-done.7
  392.1 4.5 minimum_multiply_fusion.2
  397.6 10.0 %minimum_multiply_fusion = f32[8,20,36,130]{3,2,1,0:T(8,128)} fusion(f32[8,20,36,2]{3,2,1,0:T(8,128)S(1)} %get-tuple-element.209, f32[3,20,36,128]{3,2,1,0:T(8,128)S(1)} %get-tuple-element.77, f32[1,20,36,128]{3,2,1,0:T(8,128)S(1)} %fusion.71, f32[3,20,36,128]{3,2,1,0:T(8,128)S(1)} %get-tuple-element.79, f32[1,20,36,128]{3,2,1,0:T(8,128)S(1)} %maximum_maximum_fusion.4, ...), kind=kLoop, calls=%fused_computation.36 | loop fusion | flops 17222400 | bytes 6036480 | tf_op jit(solution)/shard_map/mul | solution.py:119
  407.6 6.5 %pad_maximum_fusion.11 = (f32[8,20,36,130]{3,2,1,0:T(8,128)}, f32[8,20,36,130]{3,2,1,0:T(8,128)}) fusion(f32[8,20,36,2]{3,2,1,0:T(8,128)S(1)} %get-tuple-element.209, f32[3,20,36,128]{3,2,1,0:T(8,128)S(1)} %get-tuple-element.77, f32[1,20,36,128]{3,2,1,0:T(8,128)S(1)} %fusion.71, f32[3,20,36,128]{3,2,1,0:T(8,128)S(1)} %get-tuple-element.79, ...), kind=kLoop, calls=%fused_computation.27 | loop fusion | flops 5990400 | bytes 9031680 | tf_op jit(solution)/shard_map/concatenate | solution.py:136
  414.5 2.4 multiply_reduce_fusion.34
  416.9 2.1 multiply_reduce_fusion.33
  419.0 4.0 fusion.14
  431.8 3.9 multiply_add_fusion.8
  435.7 4.0 fusion.35
  439.8 2.7 fusion.162
  447.6 2.3 multiply_add_fusion.4
  449.9 4.1 fusion.23
  454.0 3.1 fusion.158
  457.1 13.2 %fusion.1 = (f32[8,20,36,129]{3,2,1,0:T(8,128)S(1)}, f32[8,20,36,129]{3,2,1,0:T(8,128)}) fusion(f32[8,20,36,130]{3,2,1,0:T(8,128)} %minimum_multiply_fusion, f32[8,20,36,130]{3,2,1,0:T(8,128)} %get-tuple-element.206, f32[8,20,36,130]{3,2,1,0:T(8,128)} %get-tuple-element.207), kind=kLoop, calls=%fused_computation.3 | loop fusion | flops 2972160 | bytes 17832960 | tf_op jit(solution)/shard_map/sub | solution.py:127
  471.1 2.1 copy-done
  473.1 2.3 multiply_reduce_fusion.5
  475.4 2.2 fusion.49
  477.5 2.1 fusion.52
  479.7 4.9 multiply_bitcast_fusion
  485.6 8.0 %multiply_add_fusion = (f32[3,20,36,129]{3,2,1,0:T(8,128)}, f32[3,20,36,129]{3,2,1,0:T(8,128)}, f32[3,20,36,129]{3,2,1,0:T(8,128)}, f32[3,20,36,129]{3,2,1,0:T(8...) fusion(f32[20,36,129]{2,1,0:T(8,128)} %get-tuple-element.130, f32[20,36,129]{2,1,0:T(8,128)} %get-tuple-element.147, ...), kind=kLoop, calls=%fused_computation.107 | loop fusion | flops 5015520 | bytes 14117772 | tf_op jit(solution)/shard_map/add | solution.py:89
  493.7 9.5 %fusion.10 = f32[8,20,36,129]{3,2,1,0:T(8,128)S(1)} fusion(f32[3,20,36,129]{3,2,1,0:T(8,128)} %get-tuple-element.278, f32[1,20,36,129]{3,2,1,0:T(8,128)} %get-tuple-element.74, f32[3,20,36,129]{3,2,1,0:T(8,128)} %get-tuple-element.279, f32[1,20,36,129]{3,2,1,0:T(8,128)} %get-tuple-element.142, f32[3,20,36,129]{3,2,1,0:T(8,128)} %get-tuple-element.124, ...), kind=kLoop, calls=%fused_computation.32 | loop fusion | flops 14117760 | bytes 16346880 | tf_op jit(solution)/shard_map/div | solution.py:113
  503.2 2.8 fusion.156
  506.0 7.4 %fusion.42 = f32[8,16,32,128]{3,2,1,0:T(8,128)} fusion(f32[8,20,36,128]{3,2,1,0:T(8,128)} %get-tuple-element.139, f32[8,20,36,128]{3,2,1,0:T(8,128)S(1)} %get-tuple-element.138, f32[8,20,32,128]{3,2,1,0:T(8,128)} %get-tuple-element.193, f32[8,20,32,128]{3,2,1,0:T(8,128)} %get-tuple-element.192, f32[8,16,36,128]{3,2,1,0:T(8,128)} %get-tuple-element.237, ...), kind=kLoop, calls=%fused_computation.130 | loop fusion | flops 5242880 | bytes 18874372 | tf_op jit(solution)/shard_map/mul | solution.py:179
  513.4 10.6 %reshape.282 = f32[8,1,16,2,16,8,16]{6,5,4,3,2,0,1:T(8,128)} reshape(f32[8,16,32,128]{3,2,1,0:T(8,128)} %fusion.42) | data formatting | bytes 4194304 | tf_op jit(solution)/shard_map/reshape | solution.py:180
  524.0 14.1 %copy.40 = f32[1,2,8,8,16,16,16]{6,5,4,3,2,1,0:T(8,128)} copy(f32[1,2,8,8,16,16,16]{6,2,5,1,4,3,0:T(8,128)} %bitcast.529) | data formatting | bytes 4194304 | tf_op jit(solution)/shard_map/transpose | solution.py:181
  538.1 15.2 %reshape.283 = f32[16,8,4096]{2,1,0:T(8,128)} reshape(f32[1,2,8,8,16,16,16]{6,5,4,3,2,1,0:T(8,128)} %copy.40) | data formatting | bytes 4194304 | tf_op jit(solution)/shard_map/reshape | solution.py:181
  (149 shorter events, 62.7 us)
Async XLA Ops:
  2.5 87.8 %collective-permute-start = (f32[16,8,4096]{2,1,0:T(8,128)S(1)}, f32[16,8,4096]{2,1,0:T(8,128)}, u32[]{:S(2)}, u32[]{:S(2)}) collective-permute-start(f32[16,8,4096]{2,1,0:T(8,128)S(1)} %pad_dynamic-slice_fusion.2), channel_id=1, source_target_pairs={{0,1},{1,2},{2,3},{3,4},{4,5},{5,6},{6,7},{7,8},{8,9},{9,10},{10,1... | collective-permute-start | bytes 6291464 | tf_op jit(solution)/shard_map/ppermute | solution.py:38
  166.1 7.7 %copy-start.1 = (f32[8,16,32,128]{3,2,1,0:T(8,128)}, f32[8,16,32,128]{3,2,1,0:T(8,128)S(1)}, u32[]{:S(2)}) copy-start(f32[8,16,32,128]{3,2,1,0:T(8,128)S(1)} %reshape.281) | copy-start | bytes 6291460
  174.5 22.1 %collective-permute-start.2 = (f32[8,2,32,128]{3,2,1,0:T(8,128)}, f32[8,2,32,128]{3,2,1,0:T(8,128)S(1)}, u32[]{:S(2)}, u32[]{:S(2)}) collective-permute-start(f32[8,2,32,128]{3,2,1,0:T(8,128)} %get-tuple-element.270), channel_id=1, source_target_pairs={{32,0},{64,32},{96,64},{0,96},{33,1},{65,33},{97,65},{1,97},{34,2}... | collective-permute-start | bytes 786440 | tf_op jit(solution)/shard_map/ppermute | solution.py:28
  177.3 17.6 %collective-permute-start.1 = (f32[8,2,32,128]{3,2,1,0:T(8,128)S(1)}, f32[8,2,32,128]{3,2,1,0:T(8,128)}, u32[]{:S(2)}, u32[]{:S(2)}) collective-permute-start(f32[8,2,32,128]{3,2,1,0:T(8,128)S(1)} %get-tuple-element.271), channel_id=1, source_target_pairs={{0,32},{32,64},{64,96},{96,0},{1,33},{33,65},{65,97},{97,1},{2,34}... | collective-permute-start | bytes 786440 | tf_op jit(solution)/shard_map/ppermute | solution.py:26
  194.8 1.7 copy-start.2
  194.9 7.7 %copy-start.27 = (f32[16,32,128]{2,1,0:T(8,128)S(1)}, f32[16,32,128]{2,1,0:T(8,128)}, u32[]{:S(2)}) copy-start(f32[16,32,128]{2,1,0:T(8,128)} %mul.2246) | copy-start | bytes 786436
  194.9 7.7 %copy-start.28 = (f32[16,32,128]{2,1,0:T(8,128)S(1)}, f32[16,32,128]{2,1,0:T(8,128)}, u32[]{:S(2)}) copy-start(f32[16,32,128]{2,1,0:T(8,128)} %mul.2242) | copy-start | bytes 786436
  194.9 7.7 %copy-start.29 = (f32[16,32,128]{2,1,0:T(8,128)S(1)}, f32[16,32,128]{2,1,0:T(8,128)}, u32[]{:S(2)}) copy-start(f32[16,32,128]{2,1,0:T(8,128)} %mul.2238) | copy-start | bytes 786436
  194.9 7.7 %copy-start.30 = (f32[16,32,128]{2,1,0:T(8,128)S(1)}, f32[16,32,128]{2,1,0:T(8,128)}, u32[]{:S(2)}) copy-start(f32[16,32,128]{2,1,0:T(8,128)} %reduce_sum.577) | copy-start | bytes 786436
  194.9 7.6 %copy-start.31 = (f32[16,32,128]{2,1,0:T(8,128)S(1)}, f32[16,32,128]{2,1,0:T(8,128)}, u32[]{:S(2)}) copy-start(f32[16,32,128]{2,1,0:T(8,128)} %reduce_sum.579) | copy-start | bytes 786436
  197.5 70.0 %collective-permute-start.3 = (f32[8,20,2,128]{3,2,1,0:T(2,128)}, f32[8,20,2,128]{3,2,1,0:T(2,128)S(1)}, u32[]{:S(2)}, u32[]{:S(2)}) collective-permute-start(f32[8,20,2,128]{3,2,1,0:T(2,128)} %get-tuple-element.266), channel_id=1, source_target_pairs={{0,1},{1,2},{2,3},{3,4},{4,5},{5,6},{6,7},{7,8},{8,9},{9,10},{10,1... | collective-permute-start | bytes 491528 | tf_op jit(solution)/shard_map/ppermute | solution.py:26
  197.5 70.0 %collective-permute-start.4 = (f32[8,20,2,128]{3,2,1,0:T(2,128)}, f32[8,20,2,128]{3,2,1,0:T(2,128)S(1)}, u32[]{:S(2)}, u32[]{:S(2)}) collective-permute-start(f32[8,20,2,128]{3,2,1,0:T(2,128)} %get-tuple-element.267), channel_id=1, source_target_pairs={{1,0},{2,1},{3,2},{4,3},{5,4},{6,5},{7,6},{8,7},{9,8},{10,9},{11,1... | collective-permute-start | bytes 491528 | tf_op jit(solution)/shard_map/ppermute | solution.py:28
  299.5 1.0 copy-start.21
  299.5 1.1 copy-start.22
  299.5 1.2 copy-start.23
  299.9 2.0 copy-start.17
  299.9 2.0 copy-start.18
  303.1 2.6 copy-start.34
  305.7 2.5 copy-start.16
  315.5 2.3 copy-start.32
  343.2 4.4 copy-start.33
  346.5 1.4 copy-start.10
  346.5 1.7 copy-start.11
  364.7 1.6 copy-start.3
  364.7 2.4 copy-start.6
  364.7 3.2 copy-start.7
  371.7 9.5 %collective-permute-start.5 = (f32[8,2,32,128]{3,2,1,0:T(8,128)S(1)}, f32[8,2,32,128]{3,2,1,0:T(8,128)S(1)}, u32[]{:S(2)}, u32[]{:S(2)}) collective-permute-start(f32[8,2,32,128]{3,2,1,0:T(8,128)S(1)} %get-tuple-element.268), channel_id=1, source_target_pairs={{0,32},{32,64},{64,96},{96,0},{1,33},{33,65},{65,97},{97,1},{2,34}... | collective-permute-start | bytes 786440 | tf_op jit(solution)/shard_map/ppermute | solution.py:26
  373.5 7.6 %collective-permute-start.6 = (f32[8,2,32,128]{3,2,1,0:T(8,128)S(1)}, f32[8,2,32,128]{3,2,1,0:T(8,128)S(1)}, u32[]{:S(2)}, u32[]{:S(2)}) collective-permute-start(f32[8,2,32,128]{3,2,1,0:T(8,128)S(1)} %get-tuple-element.269), channel_id=1, source_target_pairs={{32,0},{64,32},{96,64},{0,96},{33,1},{65,33},{97,65},{1,97},{34,2}... | collective-permute-start | bytes 786440 | tf_op jit(solution)/shard_map/ppermute | solution.py:28
  381.3 8.1 %collective-permute-start.7 = (f32[8,20,2,128]{3,2,1,0:T(2,128)S(1)}, f32[8,20,2,128]{3,2,1,0:T(2,128)S(1)}, u32[]{:S(2)}, u32[]{:S(2)}) collective-permute-start(f32[8,20,2,128]{3,2,1,0:T(2,128)S(1)} %get-tuple-element.264), channel_id=1, source_target_pairs={{0,1},{1,2},{2,3},{3,4},{4,5},{5,6},{6,7},{7,8},{8,9},{9,10},{10,1... | collective-permute-start | bytes 491528 | tf_op jit(solution)/shard_map/ppermute | solution.py:26
  381.4 8.1 %collective-permute-start.8 = (f32[8,20,2,128]{3,2,1,0:T(2,128)S(1)}, f32[8,20,2,128]{3,2,1,0:T(2,128)S(1)}, u32[]{:S(2)}, u32[]{:S(2)}) collective-permute-start(f32[8,20,2,128]{3,2,1,0:T(2,128)S(1)} %get-tuple-element.265), channel_id=1, source_target_pairs={{1,0},{2,1},{3,2},{4,3},{5,4},{6,5},{7,6},{8,7},{9,8},{10,9},{11,1... | collective-permute-start | bytes 491528 | tf_op jit(solution)/shard_map/ppermute | solution.py:28
  414.5 2.4 copy-start.4
  424.4 1.9 copy-start.5
  424.4 2.0 copy-start.24
  424.4 2.1 copy-start.25
  424.4 2.2 copy-start.26
  425.6 2.2 copy-start.19
  425.6 2.2 copy-start.20
  428.9 2.8 copy-start.35
  431.8 3.9 copy-start.8
  431.8 3.9 copy-start.9
  439.8 2.8 copy-start.13
  439.8 2.8 copy-start.14
  439.8 2.8 copy-start.15
  442.5 1.4 copy-start.12
  470.3 2.9 copy-start
where the time goes:
time: 561 us; the launch traced here: 554 us
  other arithmetic  226 us (40%)
  local copies, waits for them, and re-layouts  150 us (27%)
  blocking collectives  146 us (26%)
  starting transfers between devices  19.1 us (3%)
  waiting for transfers between devices  9.03 us (2%)
    unnamed x1, blocking collectives  83.7 us
    pmax x1, blocking collectives, global_speed(): return lax.pmax(local_top, ('group', 'dev'))  62.7 us
    div x12, other arithmetic, hlle_flux(): (upper * flux_left - lower * flux_right + upper * lower * (state_right -...  38.5 us
    sub x6, other arithmetic, divergence(): right = trimmed(prims, along, 2, 1) - 0.5 * trimmed(slope, along, 1, 0)  32.8 us
    mul x6, other arithmetic, minmod(): 0.5 * (jnp.sign(first) + jnp.sign(second))  31.3 us
    add x6, other arithmetic, physical_flux(): density * velocity * speed_normal - magnetic * field_normal  25 us
    transpose x1, local copies, waits for them, and re-layouts, body(): jnp.transpose(slab, (3, 0, 4, 1, 5, 2, 6))  17.9 us
    sub x12, other arithmetic, physical_flux(): (state[4] + total_pressure) * speed_normal  17.4 us
  transfers between devices with their start and end apart: 9, of which 2 were waited for; matrix products, arithmetic and copies ran while one was open for 4% of the time, Pallas kernels for 0%

commit v1 on v0

v1 whole, which is shorter than its diff:
```python
import functools

import jax
import jax.numpy as jnp
from jax import lax
from jax.experimental import pallas as pl
from jax.experimental.pallas import tpu as pltpu
from jax.sharding import PartitionSpec as P

BS = 16
BLK_DEV = 16
FIELDS = 8
XS = 16
TS = 4
CHUNKS = 32
AXES = ("group", "dev")

GAMMA = 5.0 / 3.0
COURANT = 0.25
DENSITY_FLOOR = 0.05
PRESSURE_FLOOR = 0.05
TINY = 1e-37

GRID = (XS, TS, FIELDS, 8, 128)
XFACE = (2, TS, FIELDS, 8, 128)
YFACE = (2, 2, FIELDS, 8, 128)
LIMIT = 40 << 20


def iota(axis):
    return lax.broadcasted_iota(jnp.int32, (8, 128), axis)


def root(value):
    return value * lax.rsqrt(value)


def primitive(state):
    density = jnp.maximum(state[0], DENSITY_FLOOR)
    inverse = 1.0 / density
    velocity = [state[k] * inverse for k in (1, 2, 3)]
    magnetic = state[5:8]
    kinetic = 0.5 * density * (velocity[0] * velocity[0] + velocity[1] * velocity[1] + velocity[2] * velocity[2])
    field = 0.5 * (magnetic[0] * magnetic[0] + magnetic[1] * magnetic[1] + magnetic[2] * magnetic[2])
    pressure = jnp.maximum((GAMMA - 1.0) * (state[4] - kinetic - field), PRESSURE_FLOOR)
    return [density] + velocity + [pressure] + list(magnetic)


def fast_speed(prims, normal, inverse, square):
    magnetic = prims[5:8]
    along = magnetic[normal] * magnetic[normal] * inverse
    sound = (GAMMA * prims[4]) * inverse
    total = sound + square * inverse
    inner = jnp.maximum(total * total - (4.0 * sound) * along, TINY)
    return root(0.5 * (total + root(inner)))


def side(prims, normal):
    density, pressure = prims[0], prims[4]
    velocity, magnetic = prims[1:4], prims[5:8]
    square = magnetic[0] * magnetic[0] + magnetic[1] * magnetic[1] + magnetic[2] * magnetic[2]
    fast = fast_speed(prims, normal, 1.0 / density, square)
    total = pressure + 0.5 * square
    motion = velocity[0] * velocity[0] + velocity[1] * velocity[1] + velocity[2] * velocity[2]
    energy = total + 0.5 * (pressure + density * motion)
    cross = velocity[0] * magnetic[0] + velocity[1] * magnetic[1] + velocity[2] * magnetic[2]
    return fast, total, energy, cross


def weighed(prims, normal, weight, other, total, energy, cross):
    density = prims[0]
    velocity, magnetic = prims[1:4], prims[5:8]
    carried = weight * (velocity[normal] - other)
    bent = weight * magnetic[normal]
    mass = carried * density
    push = weight * total
    momentum = [mass * velocity[k] - bent * magnetic[k] for k in range(3)]
    momentum[normal] = momentum[normal] + push
    power = carried * energy + push * velocity[normal] - bent * cross
    induced = [carried * magnetic[k] - bent * velocity[k] for k in range(3)]
    induced[normal] = -(other * bent)
    return [mass] + momentum + [power] + induced


def hlle(left, right, normal):
    fast_l, total_l, energy_l, cross_l = side(left, normal)
    fast_r, total_r, energy_r, cross_r = side(right, normal)
    speed_l, speed_r = left[1 + normal], right[1 + normal]
    upper = jnp.maximum(jnp.maximum(speed_r + fast_r, speed_l + fast_l), 0.0)
    lower = jnp.minimum(jnp.minimum(speed_l - fast_l, speed_r - fast_r), 0.0)
    weight = upper * (1.0 / (upper - lower))
    part_l = weighed(left, normal, weight, lower, total_l, energy_l, cross_l)
    part_r = weighed(right, normal, 1.0 - weight, upper, total_r, energy_r, cross_r)
    return [a + b for a, b in zip(part_l, part_r)]


def minus(first, second):
    return [a - b for a, b in zip(first, second)]


def plus(first, second):
    return [a + b for a, b in zip(first, second)]


def edges(prims, backward, forward):
    upper, lower = [], []
    for w, a, b in zip(prims, backward, forward):
        half = 0.5 * jnp.maximum(jnp.minimum(a, b), jnp.minimum(jnp.maximum(a, b), 0.0))
        upper.append(w + half)
        lower.append(w - half)
    return upper, lower


def cells(ref, x, t):
    return [ref[x, t, k] for k in range(FIELDS)]


def put(ref, x, t, values):
    for k in range(FIELDS):
        ref[x, t, k] = values[k]


def speed_kernel(count_ref, place_ref, blocks_ref, tile_ref, slots, sems):
    count = count_ref[0]
    depth = 4

    def copy(slot):
        at = slot % depth
        return pltpu.make_async_copy(blocks_ref.at[slot], slots.at[at], sems.at[at])

    for slot in range(depth - 1):
        @pl.when(slot < count)
        def _():
            copy(slot).start()

    def block(slot, top):
        @pl.when(slot + depth - 1 < count)
        def _():
            copy(slot + depth - 1).start()
        copy(slot).wait()
        rows = slots.at[slot % depth].reshape(CHUNKS * FIELDS, 128)
        for part in range(4):
            prims = primitive([rows[pl.ds(part * 64 + k, 8, stride=8), :] for k in range(FIELDS)])
            magnetic = prims[5:8]
            square = magnetic[0] * magnetic[0] + magnetic[1] * magnetic[1] + magnetic[2] * magnetic[2]
            inverse = 1.0 / prims[0]
            for normal in range(3):
                top = jnp.maximum(top, jnp.abs(prims[1 + normal]) + fast_speed(prims, normal, inverse, square))
        return top

    top = lax.fori_loop(0, count, block, jnp.zeros((8, 128), jnp.float32))
    fastest = jnp.max(top)
    counted = jnp.where(iota(1) == place_ref[0], count.astype(jnp.float32), 0.0)
    tile_ref[...] = jnp.where(iota(0) == 0, counted, fastest)


def swapped(value, index, flip):
    value = pltpu.roll(value, 0, 1, stride=16, stride_axis=0)
    value = jnp.take_along_axis(value, index, axis=0, mode="promise_in_bounds")
    value = pltpu.roll(value, 16, 1, stride=16, stride_axis=0)
    return jnp.take_along_axis(value, flip, axis=0, mode="promise_in_bounds")


def swap_indices():
    row, group = iota(0), iota(1) // 16
    flip = 7 - row
    return (group - flip) & 7, flip


def pack_sides(w_ref, xl_ref, xh_ref, yl_ref, yh_ref):
    for layer in range(2):
        for t in range(TS):
            put(xl_ref, layer, t, cells(w_ref, layer, t))
            put(xh_ref, layer, t, cells(w_ref, XS - 2 + layer, t))
    rows = w_ref.reshape(XS * 256, 128)
    for layer in range(2):
        for half in range(2):
            for k in range(FIELDS):
                yl_ref[layer, half, k] = y_layer(rows, half, k, layer)
                yh_ref[layer, half, k] = y_layer(rows, half, k, 30 + layer)


def y_layer(rows, half, k, y):
    return rows[pl.ds(half * 2048 + (y // 8) * 64 + k * 8 + y % 8, 8, stride=256), :]


def assemble_kernel(place_ref, tile_ref, came_ref, own_ref, u_ref, w_ref, xl_ref, xh_ref, yl_ref, yh_ref, slots, sems):
    place = place_ref[0]
    earlier = jnp.where((iota(0) == 0) & (iota(1) < place), tile_ref[...], 0.0)
    surplus = jnp.sum(earlier).astype(jnp.int32) - place * BLK_DEV

    for slot in range(BLK_DEV):
        target = slots.at[slot // 8, :, slot % 8]

        @pl.when(slot < surplus)
        def _():
            source = jnp.clip(BLK_DEV - 1 - surplus + slot, 0, BLK_DEV - 2)
            pltpu.make_async_copy(came_ref.at[source], target, sems.at[slot]).start()

        @pl.when(slot >= surplus)
        def _():
            source = jnp.clip(slot - surplus, 0, BLK_DEV - 1)
            pltpu.make_async_copy(own_ref.at[source], target, sems.at[slot]).start()

    index, flip = swap_indices()
    rows = slots.reshape(2 * CHUNKS * 64, 128)
    for ly in range(2):
        for lz in range(8):
            slot = ly * 8 + lz
            pltpu.make_async_copy(own_ref.at[0], slots.at[ly, :, lz], sems.at[slot]).wait()

        def chunk(c, _):
            state = [swapped(rows[pl.ds((ly * CHUNKS + c) * 64 + k, 8, stride=8), :], index, flip) for k in range(FIELDS)]
            x, t = c // 2, ly * 2 + c % 2
            put(u_ref, x, t, state)
            put(w_ref, x, t, primitive(state))
            return 0

        lax.fori_loop(0, CHUNKS, chunk, 0, unroll=4)
    pack_sides(w_ref, xl_ref, xh_ref, yl_ref, yh_ref)


def inner_kernel(w_ref, out_ref):
    row = iota(0)
    last, first = row == 7, row == 0

    def layer(x, _):
        prims = [cells(w_ref, x, t) for t in range(TS)]
        total = []
        for w in prims:
            forward = [pltpu.roll(v, 127, 1) - v for v in w]
            upper, lower = edges(w, [pltpu.roll(v, 1, 1) for v in forward], forward)
            flux = hlle(upper, [pltpu.roll(v, 127, 1) for v in lower], 2)
            total.append([pltpu.roll(v, 1, 1) - v for v in flux])

        def ahead(values):
            rolled = [[pltpu.roll(v, 7, 0) for v in w] for w in values]
            rolled.append(rolled[-1])
            return [[jnp.where(last, b, a) for a, b in zip(rolled[t], rolled[t + 1])] for t in range(TS)]

        def behind(values):
            rolled = [[pltpu.roll(v, 1, 0) for v in w] for w in values]
            rolled.insert(0, rolled[0])
            return [[jnp.where(first, a, b) for a, b in zip(rolled[t], rolled[t + 1])] for t in range(TS)]

        forward = [minus(a, w) for a, w in zip(ahead(prims), prims)]
        backward = behind(forward)
        both = [edges(w, b, f) for w, b, f in zip(prims, backward, forward)]
        right = ahead([lower for _, lower in both])
        flux = [hlle(both[t][0], right[t], 1) for t in range(TS)]
        flux[0] = [jnp.where(first, 0.0, v) for v in flux[0]]
        flux[3] = [jnp.where(row >= 6, 0.0, v) for v in flux[3]]
        rolled = [[pltpu.roll(v, 1, 0) for v in w] for w in flux]
        for t in range(TS):
            if t == 0:
                before = [jnp.where(first, 0.0, v) for v in rolled[0]]
            else:
                before = [jnp.where(first, a, b) for a, b in zip(rolled[t - 1], rolled[t])]
            put(out_ref, x, t, plus(total[t], minus(before, flux[t])))
        return 0

    lax.fori_loop(0, XS, layer, 0)

    def column(t, _):
        w0, w1, w2, w3 = [cells(w_ref, x, t) for x in range(4)]
        d1, d2 = minus(w2, w1), minus(w3, w2)
        upper, _ = edges(w1, minus(w1, w0), d1)
        after, lower = edges(w2, d1, d2)
        flux = hlle(upper, lower, 0)
        put(out_ref, 1, t, minus(cells(out_ref, 1, t), flux))

        def step(x, carry):
            d, upper, flux = carry
            here, ahead = cells(w_ref, x + 1, t), cells(w_ref, x + 2, t)
            forward = minus(ahead, here)
            after, lower = edges(here, d, forward)
            new = hlle(upper, lower, 0)
            put(out_ref, x, t, plus(cells(out_ref, x, t), minus(flux, new)))
            return forward, after, new

        _, _, flux = lax.fori_loop(2, 14, step, (d2, after, flux))
        put(out_ref, 14, t, plus(cells(out_ref, 14, t), flux))
        return 0

    lax.fori_loop(0, TS, column, 0)


def outer_faces(six, normal):
    ds = [minus(six[i + 1], six[i]) for i in range(len(six) - 1)]
    both = [edges(six[i + 1], ds[i], ds[i + 1]) for i in range(len(six) - 2)]
    return [hlle(both[i][0], both[i + 1][1], normal) for i in range(len(six) - 3)]


def outer(w_ref, sides, xc, yc):
    xl_ref, xh_ref, yl_ref, yh_ref = sides

    def column(t, _):
        near = [cells(xl_ref, 0, t), cells(xl_ref, 1, t)] + [cells(w_ref, x, t) for x in range(3)]
        a, b = outer_faces(near, 0)
        put(xc, 0, t, minus(a, b))
        put(xc, 1, t, b)
        far = [cells(w_ref, x, t) for x in range(13, 16)] + [cells(xh_ref, 0, t), cells(xh_ref, 1, t)]
        a, b = outer_faces(far, 0)
        put(xc, 2, t, [-v for v in a])
        put(xc, 3, t, minus(a, b))
        return 0

    lax.fori_loop(0, TS, column, 0)
    rows = w_ref.reshape(XS * 256, 128)
    packed = yc.reshape(XS * 128, 128)
    zero = jnp.zeros((8, 128), jnp.float32)

    def clear(x, _):
        for part in range(2):
            for k in range(FIELDS):
                yc[x, part, k] = zero
        return 0

    lax.fori_loop(0, XS, clear, 0)

    def store(half, part, y, values):
        for k in range(FIELDS):
            packed[pl.ds(half * 1024 + part * 64 + k * 8 + y, 8, stride=128), :] = values[k]

    for half in range(2):
        own = lambda y: [y_layer(rows, half, k, y) for k in range(FIELDS)]
        sent = lambda ref, layer: [ref[layer, half, k] for k in range(FIELDS)]
        a, b = outer_faces([sent(yl_ref, 0), sent(yl_ref, 1), own(0), own(1), own(2)], 1)
        store(half, 0, 0, minus(a, b))
        store(half, 0, 1, b)
        a, b = outer_faces([own(29), own(30), own(31), sent(yh_ref, 0), sent(yh_ref, 1)], 1)
        store(half, 1, 6, [-v for v in a])
        store(half, 1, 7, minus(a, b))


def changes(t_ref, xc, yc, x, t, edge):
    total = cells(t_ref, x, t)
    if t in (0, 3):
        total = plus(total, cells(yc, x, t // 3))
    if edge is not None:
        total = plus(total, cells(xc, edge, t))
    return total


def each_layer(work):
    for edge, x in enumerate((0, 1, XS - 2, XS - 1)):
        work(x, edge)
    lax.fori_loop(2, XS - 2, lambda x, _: (work(x, None), 0)[1], 0)


def step_of(tile_ref):
    return COURANT / jnp.max(jnp.where(iota(0) == 1, tile_ref[...], 0.0))


def first_kernel(tile_ref, w_ref, u_ref, t_ref, xl, xh, yl, yh, s_ref, w2_ref, xl_ref, xh_ref, yl_ref, yh_ref, xc, yc):
    step = step_of(tile_ref)
    outer(w_ref, (xl, xh, yl, yh), xc, yc)

    def work(x, edge):
        for t in range(TS):
            change = changes(t_ref, xc, yc, x, t, edge)
            state = cells(u_ref, x, t)
            first = [u + step * c for u, c in zip(state, change)]
            put(s_ref, x, t, [0.5 * (u + f) for u, f in zip(state, first)])
            put(w2_ref, x, t, primitive(first))

    each_layer(work)
    pack_sides(w2_ref, xl_ref, xh_ref, yl_ref, yh_ref)


def second_kernel(tile_ref, w_ref, s_ref, t_ref, xl, xh, yl, yh, out_ref, xc, yc):
    step = 0.5 * step_of(tile_ref)
    outer(w_ref, (xl, xh, yl, yh), xc, yc)
    index, flip = swap_indices()
    rows = out_ref.reshape(BLK_DEV * CHUNKS * FIELDS, 128)

    def work(x, edge):
        for t in range(TS):
            change = changes(t_ref, xc, yc, x, t, edge)
            chunk = 2 * x + t % 2
            for k, (s, c) in enumerate(zip(cells(s_ref, x, t), change)):
                start = ((t // 2) * 8 * CHUNKS + chunk) * 8 + k
                rows[pl.ds(start, 8, stride=CHUNKS * 8), :] = swapped(s + step * c, index, flip)

    each_layer(work)


VMEM = pl.BlockSpec(memory_space=pltpu.VMEM)
SMEM = pl.BlockSpec(memory_space=pltpu.SMEM)
ANY = pl.BlockSpec(memory_space=pl.ANY)


def shape(dims):
    return jax.ShapeDtypeStruct(dims, jnp.float32)


def kernel(function, in_specs, outs, scratch, name, flops):
    single = not isinstance(outs, list)
    return pl.pallas_call(
        function,
        out_shape=shape(outs) if single else [shape(dims) for dims in outs],
        in_specs=in_specs,
        out_specs=VMEM if single else [VMEM] * len(outs),
        scratch_shapes=scratch,
        name=name,
        compiler_params=pltpu.CompilerParams(vmem_limit_bytes=LIMIT),
        cost_estimate=pl.CostEstimate(flops=flops, bytes_accessed=6 << 20, transcendentals=0),
    )


def shifted(value, axis, by):
    count = lax.axis_size(axis)
    return lax.ppermute(value, axis, [(i, (i + by) % count) for i in range(count)])


def exchanged(xl, xh, yl, yh):
    return shifted(xh, "group", 1), shifted(xl, "group", -1), shifted(yh, "dev", 1), shifted(yl, "dev", -1)


def body(blocks_in, counts):
    devices = lax.axis_size(AXES)
    place = lax.axis_index(AXES).astype(jnp.int32).reshape(1)
    slots = blocks_in.shape[0]
    padded = jnp.concatenate([jnp.zeros((BLK_DEV - 1,) + blocks_in.shape[1:], jnp.float32), blocks_in], axis=0)
    outgoing = lax.dynamic_slice_in_dim(padded, counts[0], BLK_DEV - 1, 0)
    came = lax.ppermute(outgoing, AXES, [(i, i + 1) for i in range(devices - 1)])
    tiles = lambda value: value.reshape(value.shape[0], FIELDS, CHUNKS, 128).swapaxes(1, 2)
    own = tiles(blocks_in)
    tile = kernel(
        speed_kernel,
        [SMEM, SMEM, ANY],
        (8, 128),
        [pltpu.VMEM((4, CHUNKS, FIELDS, 128), jnp.float32), pltpu.SemaphoreType.DMA((4,))],
        "signal_speed",
        1 << 20,
    )(counts, place, own)
    distance = 1
    while distance < devices:
        tile = jnp.maximum(tile, lax.ppermute(tile, AXES, [(i, i ^ distance) for i in range(devices)]))
        distance *= 2
    sides = [XFACE, XFACE, YFACE, YFACE]
    u, w, *faces = kernel(
        assemble_kernel,
        [SMEM, VMEM, ANY, ANY],
        [GRID, GRID] + sides,
        [pltpu.VMEM((2, CHUNKS, 8, FIELDS, 128), jnp.float32), pltpu.SemaphoreType.DMA((BLK_DEV,))],
        "assemble",
        1 << 20,
    )(place, tile, tiles(came), own)
    corrections = [pltpu.VMEM((4, TS, FIELDS, 8, 128), jnp.float32), pltpu.VMEM((XS, 2, FIELDS, 8, 128), jnp.float32)]
    inner = kernel(inner_kernel, [VMEM], GRID, [], "inner_fluxes", 40 << 20)
    ghosts = exchanged(*faces)
    s, w2, *faces = kernel(first_kernel, [VMEM] * 8, [GRID, GRID] + sides, corrections, "first_stage", 1 << 20)(
        tile, w, u, inner(w), *ghosts
    )
    ghosts = exchanged(*faces)
    out = kernel(second_kernel, [VMEM] * 8, (BLK_DEV, CHUNKS, FIELDS, 128), corrections, "second_stage", 1 << 20)(
        tile, w2, s, inner(w2), *ghosts
    )
    return out.swapaxes(1, 2).reshape(BLK_DEV, FIELDS, BS * BS * BS)


def solution(mesh):
    in_specs = (P(AXES, None, None), P(AXES))
    out_specs = P(AXES, None, None)
    return jax.shard_map(body, mesh=mesh, in_specs=in_specs, out_specs=out_specs, check_vma=False)
```

time: 561 us -> 96.9 us (0.17); the launches traced: 554 us -> 96.7 us
  other arithmetic: 226 us -> 0.02 us
  blocking collectives: 146 us -> 0 us
  local copies, waits for them, and re-layouts: 150 us -> 5.16 us
  Pallas kernels: 0 us -> 37.3 us
  starting transfers between devices: 19.1 us -> 36.9 us
  waiting for transfers between devices: 9.03 us -> 16.5 us
    unnamed x1 -> x0, blocking collectives: 83.7 us -> none
    pmax x1 -> x0, blocking collectives: 62.7 us -> none  [global_speed(): return lax.pmax(local_top, ('group', 'dev'))]
    mul x13 -> x0, other arithmetic: 53.7 us -> none  [the longest x6 31.3 us: minmod(): 0.5 * (jnp.sign(first) + jnp.sign(second))]
    sub x18 -> x0, other arithmetic: 50.2 us -> none  [the longest x6 32.8 us: divergence(): right = trimmed(prims, along, 2, 1) - 0.5 * trimmed(slope, along, 1, 0)]
    reshape x4 -> x0, local copies, waits for them, and re-layouts: 45.5 us -> none  [the longest x1 15.2 us: body(): jnp.transpose(result, (1, 3, 5, 0, 2, 4, 6)).reshape(BLK_DEV, fields, cells)]
    div x13 -> x0, other arithmetic: 38.6 us -> none  [the longest x12 38.5 us: hlle_flux(): (upper * flux_left - lower * flux_right + upper * lower * (state_right -...]
    pallas_call x0 -> x6, Pallas kernels: none -> 37.3 us  [the longest x1 10.4 us: body(): inner(w)]
    slice x14 -> x0, local copies, waits for them, and re-layouts: 34 us -> none  [the longest x6 15.6 us: trimmed(): lax.slice_in_dim(values, front, values.shape[along] - back, axis=along)]
  transfers between devices with their start and end apart: 9 -> 16, of which waited for: 2 -> 7; matrix products, arithmetic and copies ran while one was open for 4% -> 0% of each run, Pallas kernels for 0% -> 26%
where the time goes in v1:
time: 96.9 us; the launch traced here: 96.7 us
  Pallas kernels  37.3 us (38%)
  starting transfers between devices  36.9 us (38%)
  waiting for transfers between devices  16.5 us (17%)
  local copies, waits for them, and re-layouts  5.16 us (5%)
    ppermute x8, starting transfers between devices, shifted(): lax.ppermute(value, axis, [(i, (i + by) % count) for i in range(count)])  20.2 us
    ppermute x7, waiting for transfers between devices, body(): lax.ppermute(tile, AXES, [(i, i ^ distance) for i in range(devices)])  16.5 us
    ppermute x7, starting transfers between devices, body(): lax.ppermute(tile, AXES, [(i, i ^ distance) for i in range(devices)])  15.4 us
    pallas_call x1, Pallas kernels, body(): inner(w)  10.4 us
    pallas_call x1, Pallas kernels, body(): inner(w2)  10.3 us
    pallas_call x1, Pallas kernels, body(): kernel(second_kernel, [VMEM] * 8, (BLK_DEV, CHUNKS, FIELDS, 128), correct...  5.78 us
    pallas_call x1, Pallas kernels, body(): kernel(speed_kernel, [SMEM, SMEM, ANY], (8, 128), [pltpu.VMEM((4, CHUNKS,...  4.74 us
    pallas_call x1, Pallas kernels, body(): kernel(assemble_kernel, [SMEM, VMEM, ANY, ANY], [GRID, GRID] + sides, [pl...  3.75 us
  transfers between devices with their start and end apart: 16, of which 7 were waited for; matrix products, arithmetic and copies ran while one was open for 0% of the time, Pallas kernels for 26%

profile of v1, /device:TPU:0, one launch (start us, length us, event | category | flops | bytes accessed | tf_op | source)
XLA Modules:
  0.0 96.7 jit_solution(7694218140124561826)
XLA Ops:
  0.7 3.0 %pad_dynamic-slice_fusion = f32[15,8,4096]{2,1,0:T(8,128)} fusion(s32[]{:T(128)S(6)} %select_n.3, f32[31,8,4096]{2,1,0:T(8,128)} %param.2), kind=kLoop, calls=%fused_computation | loop fusion | bytes 6029316 | tf_op jit(solution)/shard_map/dynamic_slice | solution.py:425
  3.7 1.4 %collective-permute-start.7 = (f32[15,8,4096]{2,1,0:T(8,128)}, f32[15,8,4096]{2,1,0:T(8,128)S(1)}, u32[]{:S(2)}, u32[]{:S(2)}) collective-permute-start(f32[15,8,4096]{2,1,0:T(8,128)} %pad_dynamic-slice_fusion), channel_id=1, source_target_pairs={{0,1},{1,2},{2,3},{3,4},{4,5},{5,6},{6,7},{7,8},{8,9},{9,10},{10,1... | collective-permute-start | bytes 5898248 | tf_op jit(solution)/shard_map/ppermute | solution.py:426
  5.1 0.0 copy-start
  5.1 2.1 %copy-done = f32[31,8,4096]{2,1,0:T(8,128)S(1)} copy-done((f32[31,8,4096]{2,1,0:T(8,128)S(1)}, f32[31,8,4096]{2,1,0:T(8,128)}, u32[]{:S(2)}) %copy-start) | copy-done | bytes 4063256
  7.2 4.7 %signal_speed.1 = f32[8,128]{1,0:T(8,128)S(1)} custom-call(s32[1]{0:T(128)} %copy.3.count_ref, s32[1]{0:T(128)} %bitcast.place_ref, f32[31,32,8,128]{3,2,1,0:T(8,128)S(1)} %bitcast.14), custom_call_target="tpu_custom_call" | custom-call | flops 1048576 | bytes 6291456 | tf_op jit(solution)/shard_map/signal_speed/pallas_call | solution.py:429
  12.0 3.7 %collective-permute-start = (f32[8,128]{1,0:T(8,128)S(1)}, f32[8,128]{1,0:T(8,128)S(1)}, u32[]{:S(2)}, u32[]{:S(2)}) collective-permute-start(f32[8,128]{1,0:T(8,128)S(1)} %signal_speed.1), channel_id=1, source_target_pairs={{0,1},{1,0},{2,3},{3,2},{4,5},{5,4},{6,7},{7,6},{8,9},{9,8},{10,11... | collective-permute-start | bytes 12296 | tf_op jit(solution)/shard_map/ppermute | solution.py:439
  15.7 0.8 collective-permute-done
  16.5 0.0 collective-permute-start.1
  16.5 3.6 %collective-permute-done.1 = f32[8,128]{1,0:T(8,128)S(1)} collective-permute-done((f32[8,128]{1,0:T(8,128)S(1)}, f32[8,128]{1,0:T(8,128)S(1)}, u32[]{:S(2)}, u32[]{:S(2)}) %collective-permute-start.1) | collective-permute-done | bytes 4128 | tf_op jit(solution)/shard_map/ppermute | solution.py:439
  20.1 1.6 %collective-permute-start.2 = (f32[8,128]{1,0:T(8,128)S(1)}, f32[8,128]{1,0:T(8,128)S(1)}, u32[]{:S(2)}, u32[]{:S(2)}) collective-permute-start(f32[8,128]{1,0:T(8,128)S(1)} %max.22), channel_id=1, source_target_pairs={{0,4},{1,5},{2,6},{3,7},{4,0},{5,1},{6,2},{7,3},{8,12},{9,13},{10,... | collective-permute-start | bytes 12296 | tf_op jit(solution)/shard_map/ppermute | solution.py:439
  21.7 3.6 %collective-permute-done.2 = f32[8,128]{1,0:T(8,128)S(1)} collective-permute-done((f32[8,128]{1,0:T(8,128)S(1)}, f32[8,128]{1,0:T(8,128)S(1)}, u32[]{:S(2)}, u32[]{:S(2)}) %collective-permute-start.2) | collective-permute-done | bytes 4128 | tf_op jit(solution)/shard_map/ppermute | solution.py:439
  25.4 1.9 %collective-permute-start.3 = (f32[8,128]{1,0:T(8,128)S(1)}, f32[8,128]{1,0:T(8,128)S(1)}, u32[]{:S(2)}, u32[]{:S(2)}) collective-permute-start(f32[8,128]{1,0:T(8,128)S(1)} %max.23), channel_id=1, source_target_pairs={{0,8},{1,9},{2,10},{3,11},{4,12},{5,13},{6,14},{7,15},{8,0},{9,1},... | collective-permute-start | bytes 12296 | tf_op jit(solution)/shard_map/ppermute | solution.py:439
  27.3 1.7 %collective-permute-done.3 = f32[8,128]{1,0:T(8,128)S(1)} collective-permute-done((f32[8,128]{1,0:T(8,128)S(1)}, f32[8,128]{1,0:T(8,128)S(1)}, u32[]{:S(2)}, u32[]{:S(2)}) %collective-permute-start.3) | collective-permute-done | bytes 4128 | tf_op jit(solution)/shard_map/ppermute | solution.py:439
  29.0 3.0 %collective-permute-start.4 = (f32[8,128]{1,0:T(8,128)S(1)}, f32[8,128]{1,0:T(8,128)S(1)}, u32[]{:S(2)}, u32[]{:S(2)}) collective-permute-start(f32[8,128]{1,0:T(8,128)S(1)} %max.24), channel_id=1, source_target_pairs={{0,16},{1,17},{2,18},{3,19},{4,20},{5,21},{6,22},{7,23},{8,24},{9,... | collective-permute-start | bytes 12296 | tf_op jit(solution)/shard_map/ppermute | solution.py:439
  32.0 2.1 %collective-permute-done.4 = f32[8,128]{1,0:T(8,128)S(1)} collective-permute-done((f32[8,128]{1,0:T(8,128)S(1)}, f32[8,128]{1,0:T(8,128)S(1)}, u32[]{:S(2)}, u32[]{:S(2)}) %collective-permute-start.4) | collective-permute-done | bytes 4128 | tf_op jit(solution)/shard_map/ppermute | solution.py:439
  34.1 3.1 %collective-permute-start.5 = (f32[8,128]{1,0:T(8,128)S(1)}, f32[8,128]{1,0:T(8,128)S(1)}, u32[]{:S(2)}, u32[]{:S(2)}) collective-permute-start(f32[8,128]{1,0:T(8,128)S(1)} %max.25), channel_id=1, source_target_pairs={{0,32},{1,33},{2,34},{3,35},{4,36},{5,37},{6,38},{7,39},{8,40},{9,... | collective-permute-start | bytes 12296 | tf_op jit(solution)/shard_map/ppermute | solution.py:439
  37.1 1.6 %collective-permute-done.5 = f32[8,128]{1,0:T(8,128)S(1)} collective-permute-done((f32[8,128]{1,0:T(8,128)S(1)}, f32[8,128]{1,0:T(8,128)S(1)}, u32[]{:S(2)}, u32[]{:S(2)}) %collective-permute-start.5) | collective-permute-done | bytes 4128 | tf_op jit(solution)/shard_map/ppermute | solution.py:439
  38.7 2.1 %collective-permute-start.6 = (f32[8,128]{1,0:T(8,128)S(1)}, f32[8,128]{1,0:T(8,128)S(1)}, u32[]{:S(2)}, u32[]{:S(2)}) collective-permute-start(f32[8,128]{1,0:T(8,128)S(1)} %max.26), channel_id=1, source_target_pairs={{0,64},{1,65},{2,66},{3,67},{4,68},{5,69},{6,70},{7,71},{8,72},{9,... | collective-permute-start | bytes 12296 | tf_op jit(solution)/shard_map/ppermute | solution.py:439
  40.8 3.0 %collective-permute-done.6 = f32[8,128]{1,0:T(8,128)S(1)} collective-permute-done((f32[8,128]{1,0:T(8,128)S(1)}, f32[8,128]{1,0:T(8,128)S(1)}, u32[]{:S(2)}, u32[]{:S(2)}) %collective-permute-start.6) | collective-permute-done | bytes 4128 | tf_op jit(solution)/shard_map/ppermute | solution.py:439
  43.8 0.0 collective-permute-done.7
  43.9 3.7 %assemble.1 = (f32[16,4,8,8,128]{4,3,2,1,0:T(8,128)S(1)}, f32[16,4,8,8,128]{4,3,2,1,0:T(8,128)S(1)}, f32[2,4,8,8,128]{4,3,2,1,0:T(8,128)S(1)}, f32[2,4,8,8,128]{...) custom-call(s32[1]{0:T(128)} %bitcast.place_ref, f32[8,128]{1,0:T(8,128)S(1)} %max.27.tile_ref, ...), custom_call_target="tpu_custom_call" | custom-call | flops 1048576 | bytes 6291456 | tf_op jit(solution)/shard_map/assemble/pallas_call | solution.py:442
  47.6 2.1 %collective-permute-start.8 = (f32[2,4,8,8,128]{4,3,2,1,0:T(8,128)S(1)}, f32[2,4,8,8,128]{4,3,2,1,0:T(8,128)S(1)}, u32[]{:S(2)}, u32[]{:S(2)}) collective-permute-start(f32[2,4,8,8,128]{4,3,2,1,0:T(8,128)S(1)} %get-tuple-element.19), channel_id=1, source_target_pairs={{0,32},{32,64},{64,96},{96,0},{1,33},{33,65},{65,97},{97,1},{2,34}... | collective-permute-start | bytes 786440 | tf_op jit(solution)/shard_map/ppermute | solution.py:413
  49.7 1.2 %collective-permute-start.9 = (f32[2,4,8,8,128]{4,3,2,1,0:T(8,128)S(1)}, f32[2,4,8,8,128]{4,3,2,1,0:T(8,128)S(1)}, u32[]{:S(2)}, u32[]{:S(2)}) collective-permute-start(f32[2,4,8,8,128]{4,3,2,1,0:T(8,128)S(1)} %get-tuple-element.20), channel_id=1, source_target_pairs={{0,96},{32,0},{64,32},{96,64},{1,97},{33,1},{65,33},{97,65},{2,98}... | collective-permute-start | bytes 786440 | tf_op jit(solution)/shard_map/ppermute | solution.py:413
  50.9 3.2 %collective-permute-start.10 = (f32[2,2,8,8,128]{4,3,2,1,0:T(8,128)S(1)}, f32[2,2,8,8,128]{4,3,2,1,0:T(8,128)S(1)}, u32[]{:S(2)}, u32[]{:S(2)}) collective-permute-start(f32[2,2,8,8,128]{4,3,2,1,0:T(8,128)S(1)} %get-tuple-element.21), channel_id=1, source_target_pairs={{0,1},{1,2},{2,3},{3,4},{4,5},{5,6},{6,7},{7,8},{8,9},{9,10},{10,1... | collective-permute-start | bytes 393224 | tf_op jit(solution)/shard_map/ppermute | solution.py:413
  54.1 5.3 %collective-permute-start.11 = (f32[2,2,8,8,128]{4,3,2,1,0:T(8,128)S(1)}, f32[2,2,8,8,128]{4,3,2,1,0:T(8,128)S(1)}, u32[]{:S(2)}, u32[]{:S(2)}) collective-permute-start(f32[2,2,8,8,128]{4,3,2,1,0:T(8,128)S(1)} %get-tuple-element.22), channel_id=1, source_target_pairs={{0,31},{1,0},{2,1},{3,2},{4,3},{5,4},{6,5},{7,6},{8,7},{9,8},{10,9... | collective-permute-start | bytes 393224 | tf_op jit(solution)/shard_map/ppermute | solution.py:413
  59.4 10.4 %inner_fluxes.2.t_ref = f32[16,4,8,8,128]{4,3,2,1,0:T(8,128)S(1)} custom-call(f32[16,4,8,8,128]{4,3,2,1,0:T(8,128)S(1)} %get-tuple-element.17.w_ref), custom_call_target="tpu_custom_call" | custom-call | flops 41943040 | bytes 6291456 | tf_op jit(solution)/shard_map/inner_fluxes/pallas_call | solution.py:454
  69.8 0.0 collective-permute-done.10.yl
  69.8 0.0 collective-permute-done.11.yh
  69.8 0.0 collective-permute-done.8.xl
  69.8 0.0 collective-permute-done.9.xh
  69.8 2.4 %first_stage.1 = (f32[16,4,8,8,128]{4,3,2,1,0:T(8,128)S(1)}, f32[16,4,8,8,128]{4,3,2,1,0:T(8,128)S(1)}, f32[2,4,8,8,128]{4,3,2,1,0:T(8,128)S(1)}, f32[2,4,8,8,12...) custom-call(f32[8,128]{1,0:T(8,128)S(1)} %max.27.tile_ref, ...), custom_call_target="tpu_custom_call" | custom-call | flops 1048576 | bytes 6291456 | tf_op jit(solution)/shard_map/first_stage/pallas_call | solution.py:453
  72.2 0.1 collective-permute-start.12
  72.3 3.2 %collective-permute-start.13 = (f32[2,4,8,8,128]{4,3,2,1,0:T(8,128)S(1)}, f32[2,4,8,8,128]{4,3,2,1,0:T(8,128)S(1)}, u32[]{:S(2)}, u32[]{:S(2)}) collective-permute-start(f32[2,4,8,8,128]{4,3,2,1,0:T(8,128)S(1)} %get-tuple-element.26), channel_id=1, source_target_pairs={{0,96},{32,0},{64,32},{96,64},{1,97},{33,1},{65,33},{97,65},{2,98}... | collective-permute-start | bytes 786440 | tf_op jit(solution)/shard_map/ppermute | solution.py:413
  75.5 0.0 collective-permute-start.14
  75.5 5.1 %collective-permute-start.15 = (f32[2,2,8,8,128]{4,3,2,1,0:T(8,128)S(1)}, f32[2,2,8,8,128]{4,3,2,1,0:T(8,128)S(1)}, u32[]{:S(2)}, u32[]{:S(2)}) collective-permute-start(f32[2,2,8,8,128]{4,3,2,1,0:T(8,128)S(1)} %get-tuple-element.28), channel_id=1, source_target_pairs={{0,31},{1,0},{2,1},{3,2},{4,3},{5,4},{6,5},{7,6},{8,7},{9,8},{10,9... | collective-permute-start | bytes 393224 | tf_op jit(solution)/shard_map/ppermute | solution.py:413
  80.6 10.3 %inner_fluxes.3.t_ref = f32[16,4,8,8,128]{4,3,2,1,0:T(8,128)S(1)} custom-call(f32[16,4,8,8,128]{4,3,2,1,0:T(8,128)S(1)} %get-tuple-element.23.w_ref), custom_call_target="tpu_custom_call" | custom-call | flops 41943040 | bytes 6291456 | tf_op jit(solution)/shard_map/inner_fluxes/pallas_call | solution.py:458
  90.9 0.0 collective-permute-done.14.yl
  90.9 0.0 collective-permute-done.15.yh
  90.9 0.0 collective-permute-done.12.xl
  90.9 0.0 collective-permute-done.13.xh
  90.9 5.8 %second_stage.1 = f32[16,32,8,128]{3,2,1,0:T(8,128)} custom-call(f32[8,128]{1,0:T(8,128)S(1)} %max.27.tile_ref, f32[16,4,8,8,128]{4,3,2,1,0:T(8,128)S(1)} %get-tuple-element.23.w_ref, f32[16,4,8,8,128]{4,3,2,1,0:T(8,128)S(1)} %get-tuple-element.24.s_ref, f32[16,4,8,8,128]{4,3,2,1,0:T(8,128)S(1)} %inner_fluxes.3.t_ref, ...), custom_call_target="tpu_custom_call" | custom-call | flops 1048576 | bytes 6291456 | tf_op jit(solution)/shard_map/second_stage/pallas_call | solution.py:457
  (7 shorter events, 0.0 us)
Async XLA Ops:
  3.7 40.2 %collective-permute-start.7 = (f32[15,8,4096]{2,1,0:T(8,128)}, f32[15,8,4096]{2,1,0:T(8,128)S(1)}, u32[]{:S(2)}, u32[]{:S(2)}) collective-permute-start(f32[15,8,4096]{2,1,0:T(8,128)} %pad_dynamic-slice_fusion), channel_id=1, source_target_pairs={{0,1},{1,2},{2,3},{3,4},{4,5},{5,6},{6,7},{7,8},{8,9},{9,10},{10,1... | collective-permute-start | bytes 5898248 | tf_op jit(solution)/shard_map/ppermute | solution.py:426
  5.1 2.2 %copy-start = (f32[31,8,4096]{2,1,0:T(8,128)S(1)}, f32[31,8,4096]{2,1,0:T(8,128)}, u32[]{:S(2)}) copy-start(f32[31,8,4096]{2,1,0:T(8,128)} %param.2) | copy-start | bytes 12189700
  12.0 4.5 %collective-permute-start = (f32[8,128]{1,0:T(8,128)S(1)}, f32[8,128]{1,0:T(8,128)S(1)}, u32[]{:S(2)}, u32[]{:S(2)}) collective-permute-start(f32[8,128]{1,0:T(8,128)S(1)} %signal_speed.1), channel_id=1, source_target_pairs={{0,1},{1,0},{2,3},{3,2},{4,5},{5,4},{6,7},{7,6},{8,9},{9,8},{10,11... | collective-permute-start | bytes 12296 | tf_op jit(solution)/shard_map/ppermute | solution.py:439
  16.5 3.6 %collective-permute-start.1 = (f32[8,128]{1,0:T(8,128)S(1)}, f32[8,128]{1,0:T(8,128)S(1)}, u32[]{:S(2)}, u32[]{:S(2)}) collective-permute-start(f32[8,128]{1,0:T(8,128)S(1)} %max.21), channel_id=1, source_target_pairs={{0,2},{1,3},{2,0},{3,1},{4,6},{5,7},{6,4},{7,5},{8,10},{9,11},{10,... | collective-permute-start | bytes 12296 | tf_op jit(solution)/shard_map/ppermute | solution.py:439
  20.1 5.3 %collective-permute-start.2 = (f32[8,128]{1,0:T(8,128)S(1)}, f32[8,128]{1,0:T(8,128)S(1)}, u32[]{:S(2)}, u32[]{:S(2)}) collective-permute-start(f32[8,128]{1,0:T(8,128)S(1)} %max.22), channel_id=1, source_target_pairs={{0,4},{1,5},{2,6},{3,7},{4,0},{5,1},{6,2},{7,3},{8,12},{9,13},{10,... | collective-permute-start | bytes 12296 | tf_op jit(solution)/shard_map/ppermute | solution.py:439
  25.4 3.6 %collective-permute-start.3 = (f32[8,128]{1,0:T(8,128)S(1)}, f32[8,128]{1,0:T(8,128)S(1)}, u32[]{:S(2)}, u32[]{:S(2)}) collective-permute-start(f32[8,128]{1,0:T(8,128)S(1)} %max.23), channel_id=1, source_target_pairs={{0,8},{1,9},{2,10},{3,11},{4,12},{5,13},{6,14},{7,15},{8,0},{9,1},... | collective-permute-start | bytes 12296 | tf_op jit(solution)/shard_map/ppermute | solution.py:439
  29.0 5.1 %collective-permute-start.4 = (f32[8,128]{1,0:T(8,128)S(1)}, f32[8,128]{1,0:T(8,128)S(1)}, u32[]{:S(2)}, u32[]{:S(2)}) collective-permute-start(f32[8,128]{1,0:T(8,128)S(1)} %max.24), channel_id=1, source_target_pairs={{0,16},{1,17},{2,18},{3,19},{4,20},{5,21},{6,22},{7,23},{8,24},{9,... | collective-permute-start | bytes 12296 | tf_op jit(solution)/shard_map/ppermute | solution.py:439
  34.1 4.6 %collective-permute-start.5 = (f32[8,128]{1,0:T(8,128)S(1)}, f32[8,128]{1,0:T(8,128)S(1)}, u32[]{:S(2)}, u32[]{:S(2)}) collective-permute-start(f32[8,128]{1,0:T(8,128)S(1)} %max.25), channel_id=1, source_target_pairs={{0,32},{1,33},{2,34},{3,35},{4,36},{5,37},{6,38},{7,39},{8,40},{9,... | collective-permute-start | bytes 12296 | tf_op jit(solution)/shard_map/ppermute | solution.py:439
  38.7 5.1 %collective-permute-start.6 = (f32[8,128]{1,0:T(8,128)S(1)}, f32[8,128]{1,0:T(8,128)S(1)}, u32[]{:S(2)}, u32[]{:S(2)}) collective-permute-start(f32[8,128]{1,0:T(8,128)S(1)} %max.26), channel_id=1, source_target_pairs={{0,64},{1,65},{2,66},{3,67},{4,68},{5,69},{6,70},{7,71},{8,72},{9,... | collective-permute-start | bytes 12296 | tf_op jit(solution)/shard_map/ppermute | solution.py:439
  47.6 22.2 %collective-permute-start.8 = (f32[2,4,8,8,128]{4,3,2,1,0:T(8,128)S(1)}, f32[2,4,8,8,128]{4,3,2,1,0:T(8,128)S(1)}, u32[]{:S(2)}, u32[]{:S(2)}) collective-permute-start(f32[2,4,8,8,128]{4,3,2,1,0:T(8,128)S(1)} %get-tuple-element.19), channel_id=1, source_target_pairs={{0,32},{32,64},{64,96},{96,0},{1,33},{33,65},{65,97},{97,1},{2,34}... | collective-permute-start | bytes 786440 | tf_op jit(solution)/shard_map/ppermute | solution.py:413
  49.7 20.1 %collective-permute-start.9 = (f32[2,4,8,8,128]{4,3,2,1,0:T(8,128)S(1)}, f32[2,4,8,8,128]{4,3,2,1,0:T(8,128)S(1)}, u32[]{:S(2)}, u32[]{:S(2)}) collective-permute-start(f32[2,4,8,8,128]{4,3,2,1,0:T(8,128)S(1)} %get-tuple-element.20), channel_id=1, source_target_pairs={{0,96},{32,0},{64,32},{96,64},{1,97},{33,1},{65,33},{97,65},{2,98}... | collective-permute-start | bytes 786440 | tf_op jit(solution)/shard_map/ppermute | solution.py:413
  50.9 18.9 %collective-permute-start.10 = (f32[2,2,8,8,128]{4,3,2,1,0:T(8,128)S(1)}, f32[2,2,8,8,128]{4,3,2,1,0:T(8,128)S(1)}, u32[]{:S(2)}, u32[]{:S(2)}) collective-permute-start(f32[2,2,8,8,128]{4,3,2,1,0:T(8,128)S(1)} %get-tuple-element.21), channel_id=1, source_target_pairs={{0,1},{1,2},{2,3},{3,4},{4,5},{5,6},{6,7},{7,8},{8,9},{9,10},{10,1... | collective-permute-start | bytes 393224 | tf_op jit(solution)/shard_map/ppermute | solution.py:413
  54.1 15.7 %collective-permute-start.11 = (f32[2,2,8,8,128]{4,3,2,1,0:T(8,128)S(1)}, f32[2,2,8,8,128]{4,3,2,1,0:T(8,128)S(1)}, u32[]{:S(2)}, u32[]{:S(2)}) collective-permute-start(f32[2,2,8,8,128]{4,3,2,1,0:T(8,128)S(1)} %get-tuple-element.22), channel_id=1, source_target_pairs={{0,31},{1,0},{2,1},{3,2},{4,3},{5,4},{6,5},{7,6},{8,7},{9,8},{10,9... | collective-permute-start | bytes 393224 | tf_op jit(solution)/shard_map/ppermute | solution.py:413
  72.2 18.7 %collective-permute-start.12 = (f32[2,4,8,8,128]{4,3,2,1,0:T(8,128)S(1)}, f32[2,4,8,8,128]{4,3,2,1,0:T(8,128)S(1)}, u32[]{:S(2)}, u32[]{:S(2)}) collective-permute-start(f32[2,4,8,8,128]{4,3,2,1,0:T(8,128)S(1)} %get-tuple-element.25), channel_id=1, source_target_pairs={{0,32},{32,64},{64,96},{96,0},{1,33},{33,65},{65,97},{97,1},{2,34}... | collective-permute-start | bytes 786440 | tf_op jit(solution)/shard_map/ppermute | solution.py:413
  72.3 18.6 %collective-permute-start.13 = (f32[2,4,8,8,128]{4,3,2,1,0:T(8,128)S(1)}, f32[2,4,8,8,128]{4,3,2,1,0:T(8,128)S(1)}, u32[]{:S(2)}, u32[]{:S(2)}) collective-permute-start(f32[2,4,8,8,128]{4,3,2,1,0:T(8,128)S(1)} %get-tuple-element.26), channel_id=1, source_target_pairs={{0,96},{32,0},{64,32},{96,64},{1,97},{33,1},{65,33},{97,65},{2,98}... | collective-permute-start | bytes 786440 | tf_op jit(solution)/shard_map/ppermute | solution.py:413
  75.5 15.4 %collective-permute-start.14 = (f32[2,2,8,8,128]{4,3,2,1,0:T(8,128)S(1)}, f32[2,2,8,8,128]{4,3,2,1,0:T(8,128)S(1)}, u32[]{:S(2)}, u32[]{:S(2)}) collective-permute-start(f32[2,2,8,8,128]{4,3,2,1,0:T(8,128)S(1)} %get-tuple-element.27), channel_id=1, source_target_pairs={{0,1},{1,2},{2,3},{3,4},{4,5},{5,6},{6,7},{7,8},{8,9},{9,10},{10,1... | collective-permute-start | bytes 393224 | tf_op jit(solution)/shard_map/ppermute | solution.py:413
  75.5 15.4 %collective-permute-start.15 = (f32[2,2,8,8,128]{4,3,2,1,0:T(8,128)S(1)}, f32[2,2,8,8,128]{4,3,2,1,0:T(8,128)S(1)}, u32[]{:S(2)}, u32[]{:S(2)}) collective-permute-start(f32[2,2,8,8,128]{4,3,2,1,0:T(8,128)S(1)} %get-tuple-element.28), channel_id=1, source_target_pairs={{0,31},{1,0},{2,1},{3,2},{4,3},{5,4},{6,5},{7,6},{8,7},{9,8},{10,9... | collective-permute-start | bytes 393224 | tf_op jit(solution)/shard_map/ppermute | solution.py:413

commit v2 on v1

--- a/solution.py
+++ b/solution.py
@@ -14,6 +14,7 @@
 TS = 4
 CHUNKS = 32
 AXES = ("group", "dev")
+ROUNDS = ((2, 32), (6, 96), (8, 32), (24, 96), (32, 32), (96, 96))
 
 GAMMA = 5.0 / 3.0
 COURANT = 0.25
@@ -24,7 +25,8 @@
 GRID = (XS, TS, FIELDS, 8, 128)
 XFACE = (2, TS, FIELDS, 8, 128)
 YFACE = (2, 2, FIELDS, 8, 128)
-LIMIT = 40 << 20
+LIMIT = 24 << 20
+ALL = 57 << 20
 
 
 def iota(axis):
@@ -120,38 +122,66 @@
         ref[x, t, k] = values[k]
 
 
-def speed_kernel(count_ref, place_ref, blocks_ref, tile_ref, slots, sems):
-    count = count_ref[0]
-    depth = 4
-
-    def copy(slot):
-        at = slot % depth
-        return pltpu.make_async_copy(blocks_ref.at[slot], slots.at[at], sems.at[at])
-
-    for slot in range(depth - 1):
-        @pl.when(slot < count)
+def depart_kernel(count_ref, place_ref, blocks_ref, out_ref, tile_ref, slots, out_sems, sems):
+    count, places = count_ref[0], BLK_DEV - 1
+    group = 4
+    groups = pl.cdiv(blocks_ref.shape[0], group)
+
+    def outgoing(work):
+        @pl.when(count >= places)
         def _():
-            copy(slot).start()
-
-    def block(slot, top):
-        @pl.when(slot + depth - 1 < count)
+            first = jnp.clip(count - places, 0, blocks_ref.shape[0] - places)
+            work(pltpu.make_async_copy(blocks_ref.at[pl.ds(first, places)], out_ref, out_sems.at[0]))
+
+        for place in range(1, places):
+            slot = count - places + place
+
+            @pl.when((count < places) & (slot >= 0))
+            def _():
+                source = jnp.clip(slot, 0, places)
+                work(pltpu.make_async_copy(blocks_ref.at[source], out_ref.at[place], out_sems.at[place]))
+
+    def incoming(index, work):
+        size = min(group, blocks_ref.shape[0] - index * group)
+        part = pl.ds(index * group, size)
+
+        @pl.when(index * group < count)
         def _():
-            copy(slot + depth - 1).start()
-        copy(slot).wait()
-        rows = slots.at[slot % depth].reshape(CHUNKS * FIELDS, 128)
-        for part in range(4):
-            prims = primitive([rows[pl.ds(part * 64 + k, 8, stride=8), :] for k in range(FIELDS)])
-            magnetic = prims[5:8]
-            square = magnetic[0] * magnetic[0] + magnetic[1] * magnetic[1] + magnetic[2] * magnetic[2]
-            inverse = 1.0 / prims[0]
-            for normal in range(3):
-                top = jnp.maximum(top, jnp.abs(prims[1 + normal]) + fast_speed(prims, normal, inverse, square))
-        return top
-
-    top = lax.fori_loop(0, count, block, jnp.zeros((8, 128), jnp.float32))
-    fastest = jnp.max(top)
+            work(pltpu.make_async_copy(blocks_ref.at[part], slots.at[part], sems.at[index]))
+
+    for index in range(groups):
+        incoming(index, lambda copy: copy.start())
+        if index == 0:
+            outgoing(lambda copy: copy.start())
+
+    rows = slots.reshape(slots.shape[0] * CHUNKS * FIELDS, 128)
+
+    def speeds(start, tops):
+        prims = primitive([rows[pl.ds(start + k, 8, stride=8), :] for k in range(FIELDS)])
+        magnetic = prims[5:8]
+        square = magnetic[0] * magnetic[0] + magnetic[1] * magnetic[1] + magnetic[2] * magnetic[2]
+        inverse = 1.0 / prims[0]
+        for normal in range(3):
+            speed = jnp.abs(prims[1 + normal]) + fast_speed(prims, normal, inverse, square)
+            tops[normal] = jnp.maximum(tops[normal], speed)
+
+    def several(index, tops):
+        for which in range(groups):
+            @pl.when(index == which)
+            def _():
+                incoming(which, lambda copy: copy.wait())
+        tops = list(tops)
+        for which in range(group):
+            slot = jnp.minimum(index * group + which, count - 1)
+            for part in range(4):
+                speeds(slot * (CHUNKS * FIELDS) + part * 64, tops)
+        return tuple(tops)
+
+    tops = lax.fori_loop(0, pl.cdiv(count, group), several, (jnp.zeros((8, 128), jnp.float32),) * 3)
+    fastest = jnp.max(jnp.maximum(jnp.maximum(tops[0], tops[1]), tops[2]))
     counted = jnp.where(iota(1) == place_ref[0], count.astype(jnp.float32), 0.0)
     tile_ref[...] = jnp.where(iota(0) == 0, counted, fastest)
+    outgoing(lambda copy: copy.wait())
 
 
 def swapped(value, index, flip):
@@ -167,24 +197,30 @@
     return (group - flip) & 7, flip
 
 
-def pack_sides(w_ref, xl_ref, xh_ref, yl_ref, yh_ref):
+def pack_sides(core, w_ref, xl_ref, xh_ref, yn_ref, yf_ref):
     for layer in range(2):
         for t in range(TS):
             put(xl_ref, layer, t, cells(w_ref, layer, t))
             put(xh_ref, layer, t, cells(w_ref, XS - 2 + layer, t))
     rows = w_ref.reshape(XS * 256, 128)
+    high = y_offset(30)
     for layer in range(2):
         for half in range(2):
             for k in range(FIELDS):
-                yl_ref[layer, half, k] = y_layer(rows, half, k, layer)
-                yh_ref[layer, half, k] = y_layer(rows, half, k, 30 + layer)
+                start = half * 2048 + k * 8 + layer
+                yn_ref[layer, half, k] = rows[pl.ds(start + (1 - core) * high, 8, stride=256), :]
+                yf_ref[layer, half, k] = rows[pl.ds(start + core * high, 8, stride=256), :]
+
+
+def y_offset(y):
+    return (y // 8) * 64 + y % 8
 
 
 def y_layer(rows, half, k, y):
-    return rows[pl.ds(half * 2048 + (y // 8) * 64 + k * 8 + y % 8, 8, stride=256), :]
-
-
-def assemble_kernel(place_ref, tile_ref, came_ref, own_ref, u_ref, w_ref, xl_ref, xh_ref, yl_ref, yh_ref, slots, sems):
+    return rows[pl.ds(half * 2048 + k * 8 + y_offset(y), 8, stride=256), :]
+
+
+def assemble_kernel(place_ref, tile_ref, came_ref, own_ref, u_ref, w_ref, xl_ref, xh_ref, yn_ref, yf_ref, slots, sems):
     place = place_ref[0]
     earlier = jnp.where((iota(0) == 0) & (iota(1) < place), tile_ref[...], 0.0)
     surplus = jnp.sum(earlier).astype(jnp.int32) - place * BLK_DEV
@@ -217,32 +253,36 @@
             return 0
 
         lax.fori_loop(0, CHUNKS, chunk, 0, unroll=4)
-    pack_sides(w_ref, xl_ref, xh_ref, yl_ref, yh_ref)
-
-
-def inner_kernel(w_ref, out_ref):
+    pack_sides(place % 2, w_ref, xl_ref, xh_ref, yn_ref, yf_ref)
+
+
+def inner_kernel(w_ref, x_ref, y_ref, z_ref):
     row = iota(0)
     last, first = row == 7, row == 0
 
-    def layer(x, _):
+    def along_z(i, _):
+        x, t = i // TS, i % TS
+        w = cells(w_ref, x, t)
+        forward = [pltpu.roll(v, 127, 1) - v for v in w]
+        upper, lower = edges(w, [pltpu.roll(v, 1, 1) for v in forward], forward)
+        flux = hlle(upper, [pltpu.roll(v, 127, 1) for v in lower], 2)
+        put(z_ref, x, t, [pltpu.roll(v, 1, 1) - v for v in flux])
+        return 0
+
+    lax.fori_loop(0, XS * TS, along_z, 0, unroll=8)
+
+    def ahead(values):
+        rolled = [[pltpu.roll(v, 7, 0) for v in w] for w in values]
+        rolled.append(rolled[-1])
+        return [[jnp.where(last, b, a) for a, b in zip(rolled[t], rolled[t + 1])] for t in range(TS)]
+
+    def behind(values):
+        rolled = [[pltpu.roll(v, 1, 0) for v in w] for w in values]
+        rolled.insert(0, rolled[0])
+        return [[jnp.where(first, a, b) for a, b in zip(rolled[t], rolled[t + 1])] for t in range(TS)]
+
+    def along_y(x, _):
         prims = [cells(w_ref, x, t) for t in range(TS)]
-        total = []
-        for w in prims:
-            forward = [pltpu.roll(v, 127, 1) - v for v in w]
-            upper, lower = edges(w, [pltpu.roll(v, 1, 1) for v in forward], forward)
-            flux = hlle(upper, [pltpu.roll(v, 127, 1) for v in lower], 2)
-            total.append([pltpu.roll(v, 1, 1) - v for v in flux])
-
-        def ahead(values):
-            rolled = [[pltpu.roll(v, 7, 0) for v in w] for w in values]
-            rolled.append(rolled[-1])
-            return [[jnp.where(last, b, a) for a, b in zip(rolled[t], rolled[t + 1])] for t in range(TS)]
-
-        def behind(values):
-            rolled = [[pltpu.roll(v, 1, 0) for v in w] for w in values]
-            rolled.insert(0, rolled[0])
-            return [[jnp.where(first, a, b) for a, b in zip(rolled[t], rolled[t + 1])] for t in range(TS)]
-
         forward = [minus(a, w) for a, w in zip(ahead(prims), prims)]
         backward = behind(forward)
         both = [edges(w, b, f) for w, b, f in zip(prims, backward, forward)]
@@ -256,33 +296,39 @@
                 before = [jnp.where(first, 0.0, v) for v in rolled[0]]
             else:
                 before = [jnp.where(first, a, b) for a, b in zip(rolled[t - 1], rolled[t])]
-            put(out_ref, x, t, plus(total[t], minus(before, flux[t])))
+            put(y_ref, x, t, minus(before, flux[t]))
         return 0
 
-    lax.fori_loop(0, XS, layer, 0)
-
-    def column(t, _):
-        w0, w1, w2, w3 = [cells(w_ref, x, t) for x in range(4)]
-        d1, d2 = minus(w2, w1), minus(w3, w2)
-        upper, _ = edges(w1, minus(w1, w0), d1)
-        after, lower = edges(w2, d1, d2)
-        flux = hlle(upper, lower, 0)
-        put(out_ref, 1, t, minus(cells(out_ref, 1, t), flux))
+    lax.fori_loop(0, XS, along_y, 0)
+
+    def along_x(pair, _):
+        both = (2 * pair, 2 * pair + 1)
+        start = []
+        for t in both:
+            w0, w1, w2, w3 = [cells(w_ref, x, t) for x in range(4)]
+            d1, d2 = minus(w2, w1), minus(w3, w2)
+            upper, _ = edges(w1, minus(w1, w0), d1)
+            after, lower = edges(w2, d1, d2)
+            flux = hlle(upper, lower, 0)
+            put(x_ref, 1, t, [-v for v in flux])
+            start.append((d2, after, flux))
 
         def step(x, carry):
-            d, upper, flux = carry
-            here, ahead = cells(w_ref, x + 1, t), cells(w_ref, x + 2, t)
-            forward = minus(ahead, here)
-            after, lower = edges(here, d, forward)
-            new = hlle(upper, lower, 0)
-            put(out_ref, x, t, plus(cells(out_ref, x, t), minus(flux, new)))
-            return forward, after, new
-
-        _, _, flux = lax.fori_loop(2, 14, step, (d2, after, flux))
-        put(out_ref, 14, t, plus(cells(out_ref, 14, t), flux))
+            result = []
+            for t, (d, upper, flux) in zip(both, carry):
+                here, beyond = cells(w_ref, x + 1, t), cells(w_ref, x + 2, t)
+                forward = minus(beyond, here)
+                after, lower = edges(here, d, forward)
+                new = hlle(upper, lower, 0)
+                put(x_ref, x, t, minus(flux, new))
+                result.append((forward, after, new))
+            return result
+
+        for t, (_, _, flux) in zip(both, lax.fori_loop(2, 14, step, start)):
+            put(x_ref, 14, t, flux)
         return 0
 
-    lax.fori_loop(0, TS, column, 0)
+    lax.fori_loop(0, TS // 2, along_x, 0)
 
 
 def outer_faces(six, normal):
@@ -291,8 +337,8 @@
     return [hlle(both[i][0], both[i + 1][1], normal) for i in range(len(six) - 3)]
 
 
-def outer(w_ref, sides, xc, yc):
-    xl_ref, xh_ref, yl_ref, yh_ref = sides
+def outer(core, w_ref, sides, xc, yc):
+    xl_ref, xh_ref, yn_ref, yf_ref = sides
 
     def column(t, _):
         near = [cells(xl_ref, 0, t), cells(xl_ref, 1, t)] + [cells(w_ref, x, t) for x in range(3)]
@@ -324,17 +370,20 @@
 
     for half in range(2):
         own = lambda y: [y_layer(rows, half, k, y) for k in range(FIELDS)]
-        sent = lambda ref, layer: [ref[layer, half, k] for k in range(FIELDS)]
-        a, b = outer_faces([sent(yl_ref, 0), sent(yl_ref, 1), own(0), own(1), own(2)], 1)
+        sent = lambda layer, near: [jnp.where(near, yn_ref[layer, half, k], yf_ref[layer, half, k]) for k in range(FIELDS)]
+        a, b = outer_faces([sent(0, core == 1), sent(1, core == 1), own(0), own(1), own(2)], 1)
         store(half, 0, 0, minus(a, b))
         store(half, 0, 1, b)
-        a, b = outer_faces([own(29), own(30), own(31), sent(yh_ref, 0), sent(yh_ref, 1)], 1)
+        a, b = outer_faces([own(29), own(30), own(31), sent(0, core == 0), sent(1, core == 0)], 1)
         store(half, 1, 6, [-v for v in a])
         store(half, 1, 7, minus(a, b))
 
 
-def changes(t_ref, xc, yc, x, t, edge):
-    total = cells(t_ref, x, t)
+def changes(inner, xc, yc, x, t, edge):
+    x_ref, y_ref, z_ref = inner
+    total = plus(cells(y_ref, x, t), cells(z_ref, x, t))
+    if edge not in (0, 3):
+        total = plus(total, cells(x_ref, x, t))
     if t in (0, 3):
         total = plus(total, cells(yc, x, t // 3))
     if edge is not None:
@@ -352,31 +401,32 @@
     return COURANT / jnp.max(jnp.where(iota(0) == 1, tile_ref[...], 0.0))
 
 
-def first_kernel(tile_ref, w_ref, u_ref, t_ref, xl, xh, yl, yh, s_ref, w2_ref, xl_ref, xh_ref, yl_ref, yh_ref, xc, yc):
+def first_kernel(place_ref, tile_ref, w_ref, u_ref, tx, ty, tz, xl, xh, yn, yf, s_ref, w2_ref, xl_ref, xh_ref, yn_ref, yf_ref, xc, yc):
     step = step_of(tile_ref)
-    outer(w_ref, (xl, xh, yl, yh), xc, yc)
+    core = place_ref[0] % 2
+    outer(core, w_ref, (xl, xh, yn, yf), xc, yc)
 
     def work(x, edge):
         for t in range(TS):
-            change = changes(t_ref, xc, yc, x, t, edge)
+            change = changes((tx, ty, tz), xc, yc, x, t, edge)
             state = cells(u_ref, x, t)
             first = [u + step * c for u, c in zip(state, change)]
             put(s_ref, x, t, [0.5 * (u + f) for u, f in zip(state, first)])
             put(w2_ref, x, t, primitive(first))
 
     each_layer(work)
-    pack_sides(w2_ref, xl_ref, xh_ref, yl_ref, yh_ref)
-
-
-def second_kernel(tile_ref, w_ref, s_ref, t_ref, xl, xh, yl, yh, out_ref, xc, yc):
+    pack_sides(core, w2_ref, xl_ref, xh_ref, yn_ref, yf_ref)
+
+
+def second_kernel(place_ref, tile_ref, w_ref, s_ref, tx, ty, tz, xl, xh, yn, yf, out_ref, xc, yc):
     step = 0.5 * step_of(tile_ref)
-    outer(w_ref, (xl, xh, yl, yh), xc, yc)
+    outer(place_ref[0] % 2, w_ref, (xl, xh, yn, yf), xc, yc)
     index, flip = swap_indices()
     rows = out_ref.reshape(BLK_DEV * CHUNKS * FIELDS, 128)
 
     def work(x, edge):
         for t in range(TS):
-            change = changes(t_ref, xc, yc, x, t, edge)
+            change = changes((tx, ty, tz), xc, yc, x, t, edge)
             chunk = 2 * x + t % 2
             for k, (s, c) in enumerate(zip(cells(s_ref, x, t), change)):
                 start = ((t // 2) * 8 * CHUNKS + chunk) * 8 + k
@@ -388,13 +438,14 @@
 VMEM = pl.BlockSpec(memory_space=pltpu.VMEM)
 SMEM = pl.BlockSpec(memory_space=pltpu.SMEM)
 ANY = pl.BlockSpec(memory_space=pl.ANY)
+HBM = pl.BlockSpec(memory_space=pltpu.HBM)
 
 
 def shape(dims):
     return jax.ShapeDtypeStruct(dims, jnp.float32)
 
 
-def kernel(function, in_specs, outs, scratch, name, flops):
+def kernel(function, in_specs, outs, scratch, name, flops, limit=LIMIT):
     single = not isinstance(outs, list)
     return pl.pallas_call(
         function,
@@ -403,7 +454,7 @@
         out_specs=VMEM if single else [VMEM] * len(outs),
         scratch_shapes=scratch,
         name=name,
-        compiler_params=pltpu.CompilerParams(vmem_limit_bytes=LIMIT),
+        compiler_params=pltpu.CompilerParams(vmem_limit_bytes=limit),
         cost_estimate=pl.CostEstimate(flops=flops, bytes_accessed=6 << 20, transcendentals=0),
     )
 
@@ -413,31 +464,37 @@
     return lax.ppermute(value, axis, [(i, (i + by) % count) for i in range(count)])
 
 
-def exchanged(xl, xh, yl, yh):
-    return shifted(xh, "group", 1), shifted(xl, "group", -1), shifted(yh, "dev", 1), shifted(yl, "dev", -1)
+def exchanged(xl, xh, yn, yf):
+    count = lax.axis_size("dev")
+    near = [(i, i ^ 1) for i in range(count)]
+    far = [(i, (i + 1) % count if i % 2 else (i - 1) % count) for i in range(count)]
+    return shifted(xh, "group", 1), shifted(xl, "group", -1), lax.ppermute(yn, "dev", near), lax.ppermute(yf, "dev", far)
 
 
 def body(blocks_in, counts):
     devices = lax.axis_size(AXES)
     place = lax.axis_index(AXES).astype(jnp.int32).reshape(1)
-    slots = blocks_in.shape[0]
-    padded = jnp.concatenate([jnp.zeros((BLK_DEV - 1,) + blocks_in.shape[1:], jnp.float32), blocks_in], axis=0)
-    outgoing = lax.dynamic_slice_in_dim(padded, counts[0], BLK_DEV - 1, 0)
-    came = lax.ppermute(outgoing, AXES, [(i, i + 1) for i in range(devices - 1)])
     tiles = lambda value: value.reshape(value.shape[0], FIELDS, CHUNKS, 128).swapaxes(1, 2)
     own = tiles(blocks_in)
-    tile = kernel(
-        speed_kernel,
-        [SMEM, SMEM, ANY],
-        (8, 128),
-        [pltpu.VMEM((4, CHUNKS, FIELDS, 128), jnp.float32), pltpu.SemaphoreType.DMA((4,))],
-        "signal_speed",
+    passed = (BLK_DEV - 1, CHUNKS, FIELDS, 128)
+    outgoing, tile = kernel(
+        depart_kernel,
+        [SMEM, SMEM, HBM],
+        [passed, (8, 128)],
+        [
+            pltpu.VMEM((blocks_in.shape[0], CHUNKS, FIELDS, 128), jnp.float32),
+            pltpu.SemaphoreType.DMA((BLK_DEV - 1,)),
+            pltpu.SemaphoreType.DMA((pl.cdiv(blocks_in.shape[0], 4),)),
+        ],
+        "depart",
         1 << 20,
+        ALL,
     )(counts, place, own)
-    distance = 1
-    while distance < devices:
-        tile = jnp.maximum(tile, lax.ppermute(tile, AXES, [(i, i ^ distance) for i in range(devices)]))
-        distance *= 2
+    came = lax.ppermute(outgoing, AXES, [(i, i + 1) for i in range(devices - 1)])
+    tile = jnp.maximum(tile, lax.ppermute(tile, AXES, [(i, i ^ 1) for i in range(devices)]))
+    for masks in ROUNDS:
+        tile = jnp.maximum(tile, lax.ppermute(tile, AXES, [(i, i ^ masks[i % 2]) for i in range(devices)]))
+    tile = jnp.maximum(tile, lax.ppermute(tile, AXES, [(i, i ^ 1) for i in range(devices)]))
     sides = [XFACE, XFACE, YFACE, YFACE]
     u, w, *faces = kernel(
         assemble_kernel,
@@ -446,16 +503,17 @@
         [pltpu.VMEM((2, CHUNKS, 8, FIELDS, 128), jnp.float32), pltpu.SemaphoreType.DMA((BLK_DEV,))],
         "assemble",
         1 << 20,
-    )(place, tile, tiles(came), own)
+    )(place, tile, came, own)
     corrections = [pltpu.VMEM((4, TS, FIELDS, 8, 128), jnp.float32), pltpu.VMEM((XS, 2, FIELDS, 8, 128), jnp.float32)]
-    inner = kernel(inner_kernel, [VMEM], GRID, [], "inner_fluxes", 40 << 20)
+    inner = kernel(inner_kernel, [VMEM], [GRID] * 3, [], "inner_fluxes", 40 << 20)
+    specs = [SMEM] + [VMEM] * 10
     ghosts = exchanged(*faces)
-    s, w2, *faces = kernel(first_kernel, [VMEM] * 8, [GRID, GRID] + sides, corrections, "first_stage", 1 << 20)(
-        tile, w, u, inner(w), *ghosts
+    s, w2, *faces = kernel(first_kernel, specs, [GRID, GRID] + sides, corrections, "first_stage", 1 << 20)(
+        place, tile, w, u, *inner(w), *ghosts
     )
     ghosts = exchanged(*faces)
-    out = kernel(second_kernel, [VMEM] * 8, (BLK_DEV, CHUNKS, FIELDS, 128), corrections, "second_stage", 1 << 20)(
-        tile, w2, s, inner(w2), *ghosts
+    out = kernel(second_kernel, specs, (BLK_DEV, CHUNKS, FIELDS, 128), corrections, "second_stage", 1 << 20)(
+        place, tile, w2, s, *inner(w2), *ghosts
     )
     return out.swapaxes(1, 2).reshape(BLK_DEV, FIELDS, BS * BS * BS)
 

time: 96.9 us -> 84.8 us (0.88)
  local copies, waits for them, and re-layouts: 5.16 us -> 0.01 us
  waiting for transfers between devices: 16.5 us -> 13.7 us
  starting transfers between devices: 36.9 us -> 34.1 us
  Pallas kernels: 37.3 us -> 36 us
    ppermute x8 -> x4, starting transfers between devices: 20.2 us -> 6.68 us  [shifted(): lax.ppermute(value, axis, [(i, (i + by) % count) for i in range(count)])]
    ppermute x7 -> x12, starting transfers between devices: 15.4 us -> 26 us  [the longest x6 19.3 us: body(): lax.ppermute(tile, AXES, [(i, i ^ masks[i % 2]) for i in range(devices)])]
    dynamic_slice x1 -> x0, local copies, waits for them, and re-layouts: 3.01 us -> none  [body(): outgoing = lax.dynamic_slice_in_dim(padded, counts[0], BLK_DEV - 1, 0)]
    ppermute x7 -> x12, waiting for transfers between devices: 16.5 us -> 13.7 us  [the longest x6 11 us: body(): lax.ppermute(tile, AXES, [(i, i ^ masks[i % 2]) for i in range(devices)])]
    unnamed x2, local copies, waits for them, and re-layouts: 2.15 us -> 0.01 us
  transfers between devices with their start and end apart: 16 -> 17, of which waited for: 7 -> 8; matrix products, arithmetic and copies ran while one was open for 0% -> 1% of each run, Pallas kernels for 26% -> 22%
where the time goes in v2:
time: 84.8 us; the launch traced here: 85.3 us
  Pallas kernels  36 us (42%)
  starting transfers between devices  34.1 us (40%)
  waiting for transfers between devices  13.7 us (16%)
    ppermute x6, starting transfers between devices, body(): lax.ppermute(tile, AXES, [(i, i ^ masks[i % 2]) for i in range(devices)])  19.3 us
    ppermute x6, waiting for transfers between devices, body(): lax.ppermute(tile, AXES, [(i, i ^ masks[i % 2]) for i in range(devices)])  11 us
    pallas_call x1, Pallas kernels, body(): inner(w)  9.52 us
    pallas_call x1, Pallas kernels, body(): inner(w2)  9.52 us
    ppermute x4, starting transfers between devices, shifted(): lax.ppermute(value, axis, [(i, (i + by) % count) for i in range(count)])  6.68 us
    pallas_call x1, Pallas kernels, body(): kernel(second_kernel, specs, (BLK_DEV, CHUNKS, FIELDS, 128), corrections,...  5.92 us
    pallas_call x1, Pallas kernels, body(): kernel(depart_kernel, [SMEM, SMEM, HBM], [passed, (8, 128)], [pltpu.VMEM(...  4.74 us
    ppermute x2, starting transfers between devices, exchanged(): lax.ppermute(yf, 'dev', far)  4.51 us
  transfers between devices with their start and end apart: 17, of which 8 were waited for; matrix products, arithmetic and copies ran while one was open for 1% of the time, Pallas kernels for 22%

profile of v2, /device:TPU:0, one launch (start us, length us, event | category | flops | bytes accessed | tf_op | source)
XLA Modules:
  0.0 85.3 jit_solution(6955224240147939776)
XLA Ops:
  0.7 0.0 copy-start
  0.7 4.7 %depart.1 = (f32[15,32,8,128]{3,2,1,0:T(8,128)}, f32[8,128]{1,0:T(8,128)}) custom-call(s32[1]{0:T(128)S(6)} %copy.3.count_ref, s32[1]{0:T(128)} %bitcast.place_ref, f32[31,32,8,128]{3,2,1,0:T(8,128)} %bitcast.7), custom_call_target="tpu_custom_call" | custom-call | flops 1048576 | bytes 6291456 | tf_op jit(solution)/shard_map/depart/pallas_call | solution.py:480
  5.4 1.4 %collective-permute-start.8 = (f32[15,32,8,128]{3,2,1,0:T(8,128)}, f32[15,32,8,128]{3,2,1,0:T(8,128)S(1)}, u32[]{:S(2)}, u32[]{:S(2)}) collective-permute-start(f32[15,32,8,128]{3,2,1,0:T(8,128)} %get-tuple-element.26), channel_id=1, source_target_pairs={{0,1},{1,2},{2,3},{3,4},{4,5},{5,6},{6,7},{7,8},{8,9},{9,10},{10,1... | collective-permute-start | bytes 5898248 | tf_op jit(solution)/shard_map/ppermute | solution.py:493
  6.8 2.2 %collective-permute-start = (f32[8,128]{1,0:T(8,128)}, f32[8,128]{1,0:T(8,128)S(1)}, u32[]{:S(2)}, u32[]{:S(2)}) collective-permute-start(f32[8,128]{1,0:T(8,128)} %get-tuple-element.25), channel_id=1, source_target_pairs={{0,1},{1,0},{2,3},{3,2},{4,5},{5,4},{6,7},{7,6},{8,9},{9,8},{10,11... | collective-permute-start | bytes 12296 | tf_op jit(solution)/shard_map/ppermute | solution.py:494
  9.0 1.5 %collective-permute-done = f32[8,128]{1,0:T(8,128)S(1)} collective-permute-done((f32[8,128]{1,0:T(8,128)}, f32[8,128]{1,0:T(8,128)S(1)}, u32[]{:S(2)}, u32[]{:S(2)}) %collective-permute-start) | collective-permute-done | bytes 4128 | tf_op jit(solution)/shard_map/ppermute | solution.py:494
  10.5 0.7 max.24
  11.2 2.1 %collective-permute-start.1 = (f32[8,128]{1,0:T(8,128)S(1)}, f32[8,128]{1,0:T(8,128)S(1)}, u32[]{:S(2)}, u32[]{:S(2)}) collective-permute-start(f32[8,128]{1,0:T(8,128)S(1)} %max.24), channel_id=1, source_target_pairs={{0,2},{1,33},{2,0},{3,35},{4,6},{5,37},{6,4},{7,39},{8,10},{9,41},... | collective-permute-start | bytes 12296 | tf_op jit(solution)/shard_map/ppermute | solution.py:496
  13.3 1.6 %collective-permute-done.1 = f32[8,128]{1,0:T(8,128)S(1)} collective-permute-done((f32[8,128]{1,0:T(8,128)S(1)}, f32[8,128]{1,0:T(8,128)S(1)}, u32[]{:S(2)}, u32[]{:S(2)}) %collective-permute-start.1) | collective-permute-done | bytes 4128 | tf_op jit(solution)/shard_map/ppermute | solution.py:496
  14.9 3.4 %collective-permute-start.2 = (f32[8,128]{1,0:T(8,128)S(1)}, f32[8,128]{1,0:T(8,128)S(1)}, u32[]{:S(2)}, u32[]{:S(2)}) collective-permute-start(f32[8,128]{1,0:T(8,128)S(1)} %max.25), channel_id=1, source_target_pairs={{0,6},{1,97},{2,4},{3,99},{4,2},{5,101},{6,0},{7,103},{8,14},{9,10... | collective-permute-start | bytes 12296 | tf_op jit(solution)/shard_map/ppermute | solution.py:496
  18.3 2.0 %collective-permute-done.2 = f32[8,128]{1,0:T(8,128)S(1)} collective-permute-done((f32[8,128]{1,0:T(8,128)S(1)}, f32[8,128]{1,0:T(8,128)S(1)}, u32[]{:S(2)}, u32[]{:S(2)}) %collective-permute-start.2) | collective-permute-done | bytes 4128 | tf_op jit(solution)/shard_map/ppermute | solution.py:496
  20.2 1.4 %collective-permute-start.3 = (f32[8,128]{1,0:T(8,128)S(1)}, f32[8,128]{1,0:T(8,128)S(1)}, u32[]{:S(2)}, u32[]{:S(2)}) collective-permute-start(f32[8,128]{1,0:T(8,128)S(1)} %max.26), channel_id=1, source_target_pairs={{0,8},{1,33},{2,10},{3,35},{4,12},{5,37},{6,14},{7,39},{8,0},{9,41... | collective-permute-start | bytes 12296 | tf_op jit(solution)/shard_map/ppermute | solution.py:496
  21.7 2.2 %collective-permute-done.3 = f32[8,128]{1,0:T(8,128)S(1)} collective-permute-done((f32[8,128]{1,0:T(8,128)S(1)}, f32[8,128]{1,0:T(8,128)S(1)}, u32[]{:S(2)}, u32[]{:S(2)}) %collective-permute-start.3) | collective-permute-done | bytes 4128 | tf_op jit(solution)/shard_map/ppermute | solution.py:496
  23.9 2.8 %collective-permute-start.4 = (f32[8,128]{1,0:T(8,128)S(1)}, f32[8,128]{1,0:T(8,128)S(1)}, u32[]{:S(2)}, u32[]{:S(2)}) collective-permute-start(f32[8,128]{1,0:T(8,128)S(1)} %max.27), channel_id=1, source_target_pairs={{0,24},{1,97},{2,26},{3,99},{4,28},{5,101},{6,30},{7,103},{8,16},{... | collective-permute-start | bytes 12296 | tf_op jit(solution)/shard_map/ppermute | solution.py:496
  26.6 2.0 %collective-permute-done.4 = f32[8,128]{1,0:T(8,128)S(1)} collective-permute-done((f32[8,128]{1,0:T(8,128)S(1)}, f32[8,128]{1,0:T(8,128)S(1)}, u32[]{:S(2)}, u32[]{:S(2)}) %collective-permute-start.4) | collective-permute-done | bytes 4128 | tf_op jit(solution)/shard_map/ppermute | solution.py:496
  28.7 2.4 %collective-permute-start.5 = (f32[8,128]{1,0:T(8,128)S(1)}, f32[8,128]{1,0:T(8,128)S(1)}, u32[]{:S(2)}, u32[]{:S(2)}) collective-permute-start(f32[8,128]{1,0:T(8,128)S(1)} %max.28), channel_id=1, source_target_pairs={{0,32},{1,33},{2,34},{3,35},{4,36},{5,37},{6,38},{7,39},{8,40},{9,... | collective-permute-start | bytes 12296 | tf_op jit(solution)/shard_map/ppermute | solution.py:496
  31.1 1.6 %collective-permute-done.5 = f32[8,128]{1,0:T(8,128)S(1)} collective-permute-done((f32[8,128]{1,0:T(8,128)S(1)}, f32[8,128]{1,0:T(8,128)S(1)}, u32[]{:S(2)}, u32[]{:S(2)}) %collective-permute-start.5) | collective-permute-done | bytes 4128 | tf_op jit(solution)/shard_map/ppermute | solution.py:496
  32.7 7.2 %collective-permute-start.6 = (f32[8,128]{1,0:T(8,128)S(1)}, f32[8,128]{1,0:T(8,128)S(1)}, u32[]{:S(2)}, u32[]{:S(2)}) collective-permute-start(f32[8,128]{1,0:T(8,128)S(1)} %max.29), channel_id=1, source_target_pairs={{0,96},{1,97},{2,98},{3,99},{4,100},{5,101},{6,102},{7,103},{8,104... | collective-permute-start | bytes 12296 | tf_op jit(solution)/shard_map/ppermute | solution.py:496
  39.9 1.6 %collective-permute-done.6 = f32[8,128]{1,0:T(8,128)S(1)} collective-permute-done((f32[8,128]{1,0:T(8,128)S(1)}, f32[8,128]{1,0:T(8,128)S(1)}, u32[]{:S(2)}, u32[]{:S(2)}) %collective-permute-start.6) | collective-permute-done | bytes 4128 | tf_op jit(solution)/shard_map/ppermute | solution.py:496
  41.5 0.0 collective-permute-start.7
  41.5 1.2 %collective-permute-done.7 = f32[8,128]{1,0:T(8,128)S(1)} collective-permute-done((f32[8,128]{1,0:T(8,128)S(1)}, f32[8,128]{1,0:T(8,128)S(1)}, u32[]{:S(2)}, u32[]{:S(2)}) %collective-permute-start.7) | collective-permute-done | bytes 4128 | tf_op jit(solution)/shard_map/ppermute | solution.py:497
  42.7 0.0 collective-permute-done.8.came_ref
  42.7 0.0 copy-done
  42.7 3.8 %assemble.1 = (f32[16,4,8,8,128]{4,3,2,1,0:T(8,128)S(1)}, f32[16,4,8,8,128]{4,3,2,1,0:T(8,128)S(1)}, f32[2,4,8,8,128]{4,3,2,1,0:T(8,128)S(1)}, f32[2,4,8,8,128]{...) custom-call(s32[1]{0:T(128)} %bitcast.place_ref, f32[8,128]{1,0:T(8,128)S(1)} %max.31.tile_ref, ...), custom_call_target="tpu_custom_call" | custom-call | flops 1048576 | bytes 6291456 | tf_op jit(solution)/shard_map/assemble/pallas_call | solution.py:499
  46.4 0.2 collective-permute-start.9
  46.6 3.2 %collective-permute-start.10 = (f32[2,4,8,8,128]{4,3,2,1,0:T(8,128)S(1)}, f32[2,4,8,8,128]{4,3,2,1,0:T(8,128)S(1)}, u32[]{:S(2)}, u32[]{:S(2)}) collective-permute-start(f32[2,4,8,8,128]{4,3,2,1,0:T(8,128)S(1)} %get-tuple-element.33), channel_id=1, source_target_pairs={{0,96},{32,0},{64,32},{96,64},{1,97},{33,1},{65,33},{97,65},{2,98}... | collective-permute-start | bytes 786440 | tf_op jit(solution)/shard_map/ppermute | solution.py:464
  49.8 0.0 collective-permute-start.11
  49.8 1.8 %collective-permute-start.12 = (f32[2,2,8,8,128]{4,3,2,1,0:T(8,128)S(1)}, f32[2,2,8,8,128]{4,3,2,1,0:T(8,128)S(1)}, u32[]{:S(2)}, u32[]{:S(2)}) collective-permute-start(f32[2,2,8,8,128]{4,3,2,1,0:T(8,128)S(1)} %get-tuple-element.35), channel_id=1, source_target_pairs={{0,31},{1,2},{2,1},{3,4},{4,3},{5,6},{6,5},{7,8},{8,7},{9,10},{10,... | collective-permute-start | bytes 393224 | tf_op jit(solution)/shard_map/ppermute | solution.py:471
  51.6 9.5 %inner_fluxes.2 = (f32[16,4,8,8,128]{4,3,2,1,0:T(8,128)S(1)}, f32[16,4,8,8,128]{4,3,2,1,0:T(8,128)S(1)}, f32[16,4,8,8,128]{4,3,2,1,0:T(8,128)S(1)}) custom-call(f32[16,4,8,8,128]{4,3,2,1,0:T(8,128)S(1)} %get-tuple-element.27.w_ref), custom_call_target="tpu_custom_call" | custom-call | flops 41943040 | bytes 6291456 | tf_op jit(solution)/shard_map/inner_fluxes/pallas_call | solution.py:512
  61.2 0.0 collective-permute-done.11.yn
  61.2 0.0 collective-permute-done.12.yf
  61.2 0.0 collective-permute-done.9.xl
  61.2 0.0 collective-permute-done.10.xh
  61.2 2.6 %first_stage.1 = (f32[16,4,8,8,128]{4,3,2,1,0:T(8,128)S(1)}, f32[16,4,8,8,128]{4,3,2,1,0:T(8,128)S(1)}, f32[2,4,8,8,128]{4,3,2,1,0:T(8,128)S(1)}, f32[2,4,8,8,12...) custom-call(s32[1]{0:T(128)} %bitcast.place_ref, ...), custom_call_target="tpu_custom_call" | custom-call | flops 1048576 | bytes 6291456 | tf_op jit(solution)/shard_map/first_stage/pallas_call | solution.py:511
  63.8 0.1 collective-permute-start.13
  63.9 3.2 %collective-permute-start.14 = (f32[2,4,8,8,128]{4,3,2,1,0:T(8,128)S(1)}, f32[2,4,8,8,128]{4,3,2,1,0:T(8,128)S(1)}, u32[]{:S(2)}, u32[]{:S(2)}) collective-permute-start(f32[2,4,8,8,128]{4,3,2,1,0:T(8,128)S(1)} %get-tuple-element.42), channel_id=1, source_target_pairs={{0,96},{32,0},{64,32},{96,64},{1,97},{33,1},{65,33},{97,65},{2,98}... | collective-permute-start | bytes 786440 | tf_op jit(solution)/shard_map/ppermute | solution.py:464
  67.1 0.0 collective-permute-start.15
  67.1 2.7 %collective-permute-start.16 = (f32[2,2,8,8,128]{4,3,2,1,0:T(8,128)S(1)}, f32[2,2,8,8,128]{4,3,2,1,0:T(8,128)S(1)}, u32[]{:S(2)}, u32[]{:S(2)}) collective-permute-start(f32[2,2,8,8,128]{4,3,2,1,0:T(8,128)S(1)} %get-tuple-element.44), channel_id=1, source_target_pairs={{0,31},{1,2},{2,1},{3,4},{4,3},{5,6},{6,5},{7,8},{8,7},{9,10},{10,... | collective-permute-start | bytes 393224 | tf_op jit(solution)/shard_map/ppermute | solution.py:471
  69.8 9.5 %inner_fluxes.3 = (f32[16,4,8,8,128]{4,3,2,1,0:T(8,128)S(1)}, f32[16,4,8,8,128]{4,3,2,1,0:T(8,128)S(1)}, f32[16,4,8,8,128]{4,3,2,1,0:T(8,128)S(1)}) custom-call(f32[16,4,8,8,128]{4,3,2,1,0:T(8,128)S(1)} %get-tuple-element.36.w_ref), custom_call_target="tpu_custom_call" | custom-call | flops 41943040 | bytes 6291456 | tf_op jit(solution)/shard_map/inner_fluxes/pallas_call | solution.py:516
  79.3 0.0 collective-permute-done.15.yn
  79.3 0.0 collective-permute-done.16.yf
  79.3 0.0 collective-permute-done.13.xl
  79.3 0.0 collective-permute-done.14.xh
  79.3 5.9 %second_stage.1 = f32[16,32,8,128]{3,2,1,0:T(8,128)} custom-call(s32[1]{0:T(128)} %bitcast.place_ref, f32[8,128]{1,0:T(8,128)S(1)} %max.31.tile_ref, f32[16,4,8,8,128]{4,3,2,1,0:T(8,128)S(1)} %get-tuple-element.36.w_ref, f32[16,4,8,8,128]{4,3,2,1,0:T(8,128)S(1)} %get-tuple-element.37.s_ref, f32[16,4,8,8,128]{4,3,2,1,0:T(8,128)S(1)} %get-tuple-element.38.tx, ...), custom_call_target="tpu_custom_call" | custom-call | flops 1048576 | bytes 6291456 | tf_op jit(solution)/shard_map/second_stage/pallas_call | solution.py:515
  (7 shorter events, 0.0 us)
Async XLA Ops:
  0.7 42.0 %copy-start = (f32[31,8,4096]{2,1,0:T(8,128)S(1)}, f32[31,8,4096]{2,1,0:T(8,128)}, u32[]{:S(2)}) copy-start(f32[31,8,4096]{2,1,0:T(8,128)} %param.2) | copy-start | bytes 12189700
  5.4 37.2 %collective-permute-start.8 = (f32[15,32,8,128]{3,2,1,0:T(8,128)}, f32[15,32,8,128]{3,2,1,0:T(8,128)S(1)}, u32[]{:S(2)}, u32[]{:S(2)}) collective-permute-start(f32[15,32,8,128]{3,2,1,0:T(8,128)} %get-tuple-element.26), channel_id=1, source_target_pairs={{0,1},{1,2},{2,3},{3,4},{4,5},{5,6},{6,7},{7,8},{8,9},{9,10},{10,1... | collective-permute-start | bytes 5898248 | tf_op jit(solution)/shard_map/ppermute | solution.py:493
  6.8 3.7 %collective-permute-start = (f32[8,128]{1,0:T(8,128)}, f32[8,128]{1,0:T(8,128)S(1)}, u32[]{:S(2)}, u32[]{:S(2)}) collective-permute-start(f32[8,128]{1,0:T(8,128)} %get-tuple-element.25), channel_id=1, source_target_pairs={{0,1},{1,0},{2,3},{3,2},{4,5},{5,4},{6,7},{7,6},{8,9},{9,8},{10,11... | collective-permute-start | bytes 12296 | tf_op jit(solution)/shard_map/ppermute | solution.py:494
  11.2 3.7 %collective-permute-start.1 = (f32[8,128]{1,0:T(8,128)S(1)}, f32[8,128]{1,0:T(8,128)S(1)}, u32[]{:S(2)}, u32[]{:S(2)}) collective-permute-start(f32[8,128]{1,0:T(8,128)S(1)} %max.24), channel_id=1, source_target_pairs={{0,2},{1,33},{2,0},{3,35},{4,6},{5,37},{6,4},{7,39},{8,10},{9,41},... | collective-permute-start | bytes 12296 | tf_op jit(solution)/shard_map/ppermute | solution.py:496
  14.9 5.4 %collective-permute-start.2 = (f32[8,128]{1,0:T(8,128)S(1)}, f32[8,128]{1,0:T(8,128)S(1)}, u32[]{:S(2)}, u32[]{:S(2)}) collective-permute-start(f32[8,128]{1,0:T(8,128)S(1)} %max.25), channel_id=1, source_target_pairs={{0,6},{1,97},{2,4},{3,99},{4,2},{5,101},{6,0},{7,103},{8,14},{9,10... | collective-permute-start | bytes 12296 | tf_op jit(solution)/shard_map/ppermute | solution.py:496
  20.2 3.6 %collective-permute-start.3 = (f32[8,128]{1,0:T(8,128)S(1)}, f32[8,128]{1,0:T(8,128)S(1)}, u32[]{:S(2)}, u32[]{:S(2)}) collective-permute-start(f32[8,128]{1,0:T(8,128)S(1)} %max.26), channel_id=1, source_target_pairs={{0,8},{1,33},{2,10},{3,35},{4,12},{5,37},{6,14},{7,39},{8,0},{9,41... | collective-permute-start | bytes 12296 | tf_op jit(solution)/shard_map/ppermute | solution.py:496
  23.9 4.8 %collective-permute-start.4 = (f32[8,128]{1,0:T(8,128)S(1)}, f32[8,128]{1,0:T(8,128)S(1)}, u32[]{:S(2)}, u32[]{:S(2)}) collective-permute-start(f32[8,128]{1,0:T(8,128)S(1)} %max.27), channel_id=1, source_target_pairs={{0,24},{1,97},{2,26},{3,99},{4,28},{5,101},{6,30},{7,103},{8,16},{... | collective-permute-start | bytes 12296 | tf_op jit(solution)/shard_map/ppermute | solution.py:496
  28.7 4.0 %collective-permute-start.5 = (f32[8,128]{1,0:T(8,128)S(1)}, f32[8,128]{1,0:T(8,128)S(1)}, u32[]{:S(2)}, u32[]{:S(2)}) collective-permute-start(f32[8,128]{1,0:T(8,128)S(1)} %max.28), channel_id=1, source_target_pairs={{0,32},{1,33},{2,34},{3,35},{4,36},{5,37},{6,38},{7,39},{8,40},{9,... | collective-permute-start | bytes 12296 | tf_op jit(solution)/shard_map/ppermute | solution.py:496
  32.7 8.8 %collective-permute-start.6 = (f32[8,128]{1,0:T(8,128)S(1)}, f32[8,128]{1,0:T(8,128)S(1)}, u32[]{:S(2)}, u32[]{:S(2)}) collective-permute-start(f32[8,128]{1,0:T(8,128)S(1)} %max.29), channel_id=1, source_target_pairs={{0,96},{1,97},{2,98},{3,99},{4,100},{5,101},{6,102},{7,103},{8,104... | collective-permute-start | bytes 12296 | tf_op jit(solution)/shard_map/ppermute | solution.py:496
  41.5 1.2 %collective-permute-start.7 = (f32[8,128]{1,0:T(8,128)S(1)}, f32[8,128]{1,0:T(8,128)S(1)}, u32[]{:S(2)}, u32[]{:S(2)}) collective-permute-start(f32[8,128]{1,0:T(8,128)S(1)} %max.30), channel_id=1, source_target_pairs={{0,1},{1,0},{2,3},{3,2},{4,5},{5,4},{6,7},{7,6},{8,9},{9,8},{10,11... | collective-permute-start | bytes 12296 | tf_op jit(solution)/shard_map/ppermute | solution.py:497
  46.4 14.8 %collective-permute-start.9 = (f32[2,4,8,8,128]{4,3,2,1,0:T(8,128)S(1)}, f32[2,4,8,8,128]{4,3,2,1,0:T(8,128)S(1)}, u32[]{:S(2)}, u32[]{:S(2)}) collective-permute-start(f32[2,4,8,8,128]{4,3,2,1,0:T(8,128)S(1)} %get-tuple-element.32), channel_id=1, source_target_pairs={{0,32},{32,64},{64,96},{96,0},{1,33},{33,65},{65,97},{97,1},{2,34}... | collective-permute-start | bytes 786440 | tf_op jit(solution)/shard_map/ppermute | solution.py:464
  46.6 14.6 %collective-permute-start.10 = (f32[2,4,8,8,128]{4,3,2,1,0:T(8,128)S(1)}, f32[2,4,8,8,128]{4,3,2,1,0:T(8,128)S(1)}, u32[]{:S(2)}, u32[]{:S(2)}) collective-permute-start(f32[2,4,8,8,128]{4,3,2,1,0:T(8,128)S(1)} %get-tuple-element.33), channel_id=1, source_target_pairs={{0,96},{32,0},{64,32},{96,64},{1,97},{33,1},{65,33},{97,65},{2,98}... | collective-permute-start | bytes 786440 | tf_op jit(solution)/shard_map/ppermute | solution.py:464
  49.8 11.4 %collective-permute-start.11 = (f32[2,2,8,8,128]{4,3,2,1,0:T(8,128)S(1)}, f32[2,2,8,8,128]{4,3,2,1,0:T(8,128)S(1)}, u32[]{:S(2)}, u32[]{:S(2)}) collective-permute-start(f32[2,2,8,8,128]{4,3,2,1,0:T(8,128)S(1)} %get-tuple-element.34), channel_id=1, source_target_pairs={{0,1},{1,0},{2,3},{3,2},{4,5},{5,4},{6,7},{7,6},{8,9},{9,8},{10,11... | collective-permute-start | bytes 393224 | tf_op jit(solution)/shard_map/ppermute | solution.py:471
  49.8 11.4 %collective-permute-start.12 = (f32[2,2,8,8,128]{4,3,2,1,0:T(8,128)S(1)}, f32[2,2,8,8,128]{4,3,2,1,0:T(8,128)S(1)}, u32[]{:S(2)}, u32[]{:S(2)}) collective-permute-start(f32[2,2,8,8,128]{4,3,2,1,0:T(8,128)S(1)} %get-tuple-element.35), channel_id=1, source_target_pairs={{0,31},{1,2},{2,1},{3,4},{4,3},{5,6},{6,5},{7,8},{8,7},{9,10},{10,... | collective-permute-start | bytes 393224 | tf_op jit(solution)/shard_map/ppermute | solution.py:471
  63.8 15.5 %collective-permute-start.13 = (f32[2,4,8,8,128]{4,3,2,1,0:T(8,128)S(1)}, f32[2,4,8,8,128]{4,3,2,1,0:T(8,128)S(1)}, u32[]{:S(2)}, u32[]{:S(2)}) collective-permute-start(f32[2,4,8,8,128]{4,3,2,1,0:T(8,128)S(1)} %get-tuple-element.41), channel_id=1, source_target_pairs={{0,32},{32,64},{64,96},{96,0},{1,33},{33,65},{65,97},{97,1},{2,34}... | collective-permute-start | bytes 786440 | tf_op jit(solution)/shard_map/ppermute | solution.py:464
  63.9 15.5 %collective-permute-start.14 = (f32[2,4,8,8,128]{4,3,2,1,0:T(8,128)S(1)}, f32[2,4,8,8,128]{4,3,2,1,0:T(8,128)S(1)}, u32[]{:S(2)}, u32[]{:S(2)}) collective-permute-start(f32[2,4,8,8,128]{4,3,2,1,0:T(8,128)S(1)} %get-tuple-element.42), channel_id=1, source_target_pairs={{0,96},{32,0},{64,32},{96,64},{1,97},{33,1},{65,33},{97,65},{2,98}... | collective-permute-start | bytes 786440 | tf_op jit(solution)/shard_map/ppermute | solution.py:464
  67.1 12.2 %collective-permute-start.15 = (f32[2,2,8,8,128]{4,3,2,1,0:T(8,128)S(1)}, f32[2,2,8,8,128]{4,3,2,1,0:T(8,128)S(1)}, u32[]{:S(2)}, u32[]{:S(2)}) collective-permute-start(f32[2,2,8,8,128]{4,3,2,1,0:T(8,128)S(1)} %get-tuple-element.43), channel_id=1, source_target_pairs={{0,1},{1,0},{2,3},{3,2},{4,5},{5,4},{6,7},{7,6},{8,9},{9,8},{10,11... | collective-permute-start | bytes 393224 | tf_op jit(solution)/shard_map/ppermute | solution.py:471
  67.1 12.2 %collective-permute-start.16 = (f32[2,2,8,8,128]{4,3,2,1,0:T(8,128)S(1)}, f32[2,2,8,8,128]{4,3,2,1,0:T(8,128)S(1)}, u32[]{:S(2)}, u32[]{:S(2)}) collective-permute-start(f32[2,2,8,8,128]{4,3,2,1,0:T(8,128)S(1)} %get-tuple-element.44), channel_id=1, source_target_pairs={{0,31},{1,2},{2,1},{3,4},{4,3},{5,6},{6,5},{7,8},{8,7},{9,10},{10,... | collective-permute-start | bytes 393224 | tf_op jit(solution)/shard_map/ppermute | solution.py:471

commit v3 on v2

--- a/solution.py
+++ b/solution.py
@@ -26,7 +26,6 @@
 XFACE = (2, TS, FIELDS, 8, 128)
 YFACE = (2, 2, FIELDS, 8, 128)
 LIMIT = 24 << 20
-ALL = 57 << 20
 
 
 def iota(axis):
@@ -122,24 +121,26 @@
         ref[x, t, k] = values[k]
 
 
-def depart_kernel(count_ref, place_ref, blocks_ref, out_ref, tile_ref, slots, out_sems, sems):
+def outgoing_kernel(count_ref, blocks_ref, out_ref, sems):
     count, places = count_ref[0], BLK_DEV - 1
+
+    def each(work):
+        for place in range(places):
+            slot = count - places + place
+
+            @pl.when(slot >= 0)
+            def _():
+                source = jnp.clip(slot, 0, blocks_ref.shape[0] - 1)
+                work(pltpu.make_async_copy(blocks_ref.at[source], out_ref.at[place], sems.at[place]))
+
+    each(lambda copy: copy.start())
+    each(lambda copy: copy.wait())
+
+
+def speed_kernel(count_ref, place_ref, blocks_ref, tile_ref, slots, sems):
+    count = count_ref[0]
     group = 4
     groups = pl.cdiv(blocks_ref.shape[0], group)
-
-    def outgoing(work):
-        @pl.when(count >= places)
-        def _():
-            first = jnp.clip(count - places, 0, blocks_ref.shape[0] - places)
-            work(pltpu.make_async_copy(blocks_ref.at[pl.ds(first, places)], out_ref, out_sems.at[0]))
-
-        for place in range(1, places):
-            slot = count - places + place
-
-            @pl.when((count < places) & (slot >= 0))
-            def _():
-                source = jnp.clip(slot, 0, places)
-                work(pltpu.make_async_copy(blocks_ref.at[source], out_ref.at[place], out_sems.at[place]))
 
     def incoming(index, work):
         size = min(group, blocks_ref.shape[0] - index * group)
@@ -151,8 +152,6 @@
 
     for index in range(groups):
         incoming(index, lambda copy: copy.start())
-        if index == 0:
-            outgoing(lambda copy: copy.start())
 
     rows = slots.reshape(slots.shape[0] * CHUNKS * FIELDS, 128)
 
@@ -181,7 +180,6 @@
     fastest = jnp.max(jnp.maximum(jnp.maximum(tops[0], tops[1]), tops[2]))
     counted = jnp.where(iota(1) == place_ref[0], count.astype(jnp.float32), 0.0)
     tile_ref[...] = jnp.where(iota(0) == 0, counted, fastest)
-    outgoing(lambda copy: copy.wait())
 
 
 def swapped(value, index, flip):
@@ -256,20 +254,9 @@
     pack_sides(place % 2, w_ref, xl_ref, xh_ref, yn_ref, yf_ref)
 
 
-def inner_kernel(w_ref, x_ref, y_ref, z_ref):
+def inner_kernel(w_ref, xz_ref, y_ref, next_ref, prior_ref, flux_ref):
     row = iota(0)
     last, first = row == 7, row == 0
-
-    def along_z(i, _):
-        x, t = i // TS, i % TS
-        w = cells(w_ref, x, t)
-        forward = [pltpu.roll(v, 127, 1) - v for v in w]
-        upper, lower = edges(w, [pltpu.roll(v, 1, 1) for v in forward], forward)
-        flux = hlle(upper, [pltpu.roll(v, 127, 1) for v in lower], 2)
-        put(z_ref, x, t, [pltpu.roll(v, 1, 1) - v for v in flux])
-        return 0
-
-    lax.fori_loop(0, XS * TS, along_z, 0, unroll=8)
 
     def ahead(values):
         rolled = [[pltpu.roll(v, 7, 0) for v in w] for w in values]
@@ -283,6 +270,9 @@
 
     def along_y(x, _):
         prims = [cells(w_ref, x, t) for t in range(TS)]
+        for t in range(TS):
+            put(next_ref, x, t, [pltpu.roll(v, 127, 1) for v in prims[t]])
+            put(prior_ref, x, t, [pltpu.roll(v, 1, 1) for v in prims[t]])
         forward = [minus(a, w) for a, w in zip(ahead(prims), prims)]
         backward = behind(forward)
         both = [edges(w, b, f) for w, b, f in zip(prims, backward, forward)]
@@ -299,10 +289,24 @@
             put(y_ref, x, t, minus(before, flux[t]))
         return 0
 
-    lax.fori_loop(0, XS, along_y, 0)
+    lax.fori_loop(0, XS, along_y, 0, unroll=2)
+
+    def along_z(i, _):
+        x, t = i // TS, i % TS
+        w = cells(w_ref, x, t)
+        upper, lower = edges(w, minus(w, cells(prior_ref, x, t)), minus(cells(next_ref, x, t), w))
+        put(flux_ref, x, t, hlle(upper, [pltpu.roll(v, 127, 1) for v in lower], 2))
+        return 0
+
+    lax.fori_loop(0, XS * TS, along_z, 0, unroll=8)
 
     def along_x(pair, _):
         both = (2 * pair, 2 * pair + 1)
+
+        def store(x, t, change=None):
+            total = [pltpu.roll(v, 1, 1) - v for v in cells(flux_ref, x, t)]
+            put(xz_ref, x, t, total if change is None else plus(total, change))
+
         start = []
         for t in both:
             w0, w1, w2, w3 = [cells(w_ref, x, t) for x in range(4)]
@@ -310,7 +314,8 @@
             upper, _ = edges(w1, minus(w1, w0), d1)
             after, lower = edges(w2, d1, d2)
             flux = hlle(upper, lower, 0)
-            put(x_ref, 1, t, [-v for v in flux])
+            store(0, t)
+            store(1, t, [-v for v in flux])
             start.append((d2, after, flux))
 
         def step(x, carry):
@@ -320,12 +325,13 @@
                 forward = minus(beyond, here)
                 after, lower = edges(here, d, forward)
                 new = hlle(upper, lower, 0)
-                put(x_ref, x, t, minus(flux, new))
+                store(x, t, minus(flux, new))
                 result.append((forward, after, new))
             return result
 
         for t, (_, _, flux) in zip(both, lax.fori_loop(2, 14, step, start)):
-            put(x_ref, 14, t, flux)
+            store(14, t, flux)
+            store(15, t)
         return 0
 
     lax.fori_loop(0, TS // 2, along_x, 0)
@@ -380,10 +386,8 @@
 
 
 def changes(inner, xc, yc, x, t, edge):
-    x_ref, y_ref, z_ref = inner
-    total = plus(cells(y_ref, x, t), cells(z_ref, x, t))
-    if edge not in (0, 3):
-        total = plus(total, cells(x_ref, x, t))
+    xz_ref, y_ref = inner
+    total = plus(cells(xz_ref, x, t), cells(y_ref, x, t))
     if t in (0, 3):
         total = plus(total, cells(yc, x, t // 3))
     if edge is not None:
@@ -401,14 +405,14 @@
     return COURANT / jnp.max(jnp.where(iota(0) == 1, tile_ref[...], 0.0))
 
 
-def first_kernel(place_ref, tile_ref, w_ref, u_ref, tx, ty, tz, xl, xh, yn, yf, s_ref, w2_ref, xl_ref, xh_ref, yn_ref, yf_ref, xc, yc):
+def first_kernel(place_ref, tile_ref, w_ref, u_ref, txz, ty, xl, xh, yn, yf, s_ref, w2_ref, xl_ref, xh_ref, yn_ref, yf_ref, xc, yc):
     step = step_of(tile_ref)
     core = place_ref[0] % 2
     outer(core, w_ref, (xl, xh, yn, yf), xc, yc)
 
     def work(x, edge):
         for t in range(TS):
-            change = changes((tx, ty, tz), xc, yc, x, t, edge)
+            change = changes((txz, ty), xc, yc, x, t, edge)
             state = cells(u_ref, x, t)
             first = [u + step * c for u, c in zip(state, change)]
             put(s_ref, x, t, [0.5 * (u + f) for u, f in zip(state, first)])
@@ -418,21 +422,41 @@
     pack_sides(core, w2_ref, xl_ref, xh_ref, yn_ref, yf_ref)
 
 
-def second_kernel(place_ref, tile_ref, w_ref, s_ref, tx, ty, tz, xl, xh, yn, yf, out_ref, xc, yc):
+def second_kernel(place_ref, tile_ref, w_ref, s_ref, txz, ty, xl, xh, yn, yf, out_ref, xc, yc, blocks, sems):
     step = 0.5 * step_of(tile_ref)
     outer(place_ref[0] % 2, w_ref, (xl, xh, yn, yf), xc, yc)
     index, flip = swap_indices()
-    rows = out_ref.reshape(BLK_DEV * CHUNKS * FIELDS, 128)
+    rows = blocks.reshape(BLK_DEV * CHUNKS * FIELDS, 128)
 
     def work(x, edge):
         for t in range(TS):
-            change = changes((tx, ty, tz), xc, yc, x, t, edge)
+            change = changes((txz, ty), xc, yc, x, t, edge)
             chunk = 2 * x + t % 2
             for k, (s, c) in enumerate(zip(cells(s_ref, x, t), change)):
                 start = ((t // 2) * 8 * CHUNKS + chunk) * 8 + k
                 rows[pl.ds(start, 8, stride=CHUNKS * 8), :] = swapped(s + step * c, index, flip)
 
-    each_layer(work)
+    def part(quarter):
+        chunks = pl.ds(quarter * 8, 8)
+        return pltpu.make_async_copy(blocks.at[:, chunks], out_ref.at[:, chunks], sems.at[quarter])
+
+    def inside(first, last):
+        lax.fori_loop(first, last, lambda x, _: (work(x, None), 0)[1], 0)
+
+    work(0, 0)
+    work(1, 1)
+    inside(2, 4)
+    part(0).start()
+    inside(4, 8)
+    part(1).start()
+    inside(8, 12)
+    part(2).start()
+    inside(12, 14)
+    work(14, 2)
+    work(15, 3)
+    part(3).start()
+    for quarter in range(4):
+        part(quarter).wait()
 
 
 VMEM = pl.BlockSpec(memory_space=pltpu.VMEM)
@@ -442,16 +466,16 @@
 
 
 def shape(dims):
-    return jax.ShapeDtypeStruct(dims, jnp.float32)
-
-
-def kernel(function, in_specs, outs, scratch, name, flops, limit=LIMIT):
+    return pltpu.VMEM(dims, jnp.float32)
+
+
+def kernel(function, in_specs, outs, scratch, name, flops, limit=LIMIT, out_spec=VMEM):
     single = not isinstance(outs, list)
     return pl.pallas_call(
         function,
-        out_shape=shape(outs) if single else [shape(dims) for dims in outs],
+        out_shape=jax.ShapeDtypeStruct(outs, jnp.float32) if out_spec is ANY else shape(outs) if single else [shape(dims) for dims in outs],
         in_specs=in_specs,
-        out_specs=VMEM if single else [VMEM] * len(outs),
+        out_specs=out_spec if single else [out_spec] * len(outs),
         scratch_shapes=scratch,
         name=name,
         compiler_params=pltpu.CompilerParams(vmem_limit_bytes=limit),
@@ -477,21 +501,24 @@
     tiles = lambda value: value.reshape(value.shape[0], FIELDS, CHUNKS, 128).swapaxes(1, 2)
     own = tiles(blocks_in)
     passed = (BLK_DEV - 1, CHUNKS, FIELDS, 128)
-    outgoing, tile = kernel(
-        depart_kernel,
+    there = pltpu.with_memory_space_constraint(own, pltpu.HBM)
+    outgoing = kernel(outgoing_kernel, [SMEM, HBM], passed, [pltpu.SemaphoreType.DMA((BLK_DEV - 1,))], "outgoing", 1 << 10)(
+        counts, there
+    )
+    came = lax.ppermute(outgoing, AXES, [(i, i + 1) for i in range(devices - 1)])
+    tile = kernel(
+        speed_kernel,
         [SMEM, SMEM, HBM],
-        [passed, (8, 128)],
+        (8, 128),
         [
             pltpu.VMEM((blocks_in.shape[0], CHUNKS, FIELDS, 128), jnp.float32),
-            pltpu.SemaphoreType.DMA((BLK_DEV - 1,)),
             pltpu.SemaphoreType.DMA((pl.cdiv(blocks_in.shape[0], 4),)),
         ],
-        "depart",
+        "signal_speed",
         1 << 20,
-        ALL,
-    )(counts, place, own)
-    came = lax.ppermute(outgoing, AXES, [(i, i + 1) for i in range(devices - 1)])
+    )(counts, place, there)
     tile = jnp.maximum(tile, lax.ppermute(tile, AXES, [(i, i ^ 1) for i in range(devices)]))
+    tile, own = lax.optimization_barrier((tile, own))
     for masks in ROUNDS:
         tile = jnp.maximum(tile, lax.ppermute(tile, AXES, [(i, i ^ masks[i % 2]) for i in range(devices)]))
     tile = jnp.maximum(tile, lax.ppermute(tile, AXES, [(i, i ^ 1) for i in range(devices)]))
@@ -505,14 +532,16 @@
         1 << 20,
     )(place, tile, came, own)
     corrections = [pltpu.VMEM((4, TS, FIELDS, 8, 128), jnp.float32), pltpu.VMEM((XS, 2, FIELDS, 8, 128), jnp.float32)]
-    inner = kernel(inner_kernel, [VMEM], [GRID] * 3, [], "inner_fluxes", 40 << 20)
-    specs = [SMEM] + [VMEM] * 10
+    inner = kernel(inner_kernel, [VMEM], [GRID] * 2, [pltpu.VMEM(GRID, jnp.float32)] * 3, "inner_fluxes", 40 << 20)
+    specs = [SMEM] + [VMEM] * 9
     ghosts = exchanged(*faces)
     s, w2, *faces = kernel(first_kernel, specs, [GRID, GRID] + sides, corrections, "first_stage", 1 << 20)(
         place, tile, w, u, *inner(w), *ghosts
     )
     ghosts = exchanged(*faces)
-    out = kernel(second_kernel, specs, (BLK_DEV, CHUNKS, FIELDS, 128), corrections, "second_stage", 1 << 20)(
+    result = (BLK_DEV, CHUNKS, FIELDS, 128)
+    buffers = corrections + [pltpu.VMEM(result, jnp.float32), pltpu.SemaphoreType.DMA((4,))]
+    out = kernel(second_kernel, specs, result, buffers, "second_stage", 1 << 20, out_spec=ANY)(
         place, tile, w2, s, *inner(w2), *ghosts
     )
     return out.swapaxes(1, 2).reshape(BLK_DEV, FIELDS, BS * BS * BS)

time: 84.8 us -> 79 us (0.932)
  Pallas kernels: 36 us -> 31 us
  starting transfers between devices: 34.1 us -> 31.9 us
  waiting for transfers between devices: 13.7 us -> 15 us
    ppermute x6, starting transfers between devices: 19.3 us -> 16 us  [body(): lax.ppermute(tile, AXES, [(i, i ^ masks[i % 2]) for i in range(devices)])]
    ppermute x6, waiting for transfers between devices: 11 us -> 13 us  [body(): lax.ppermute(tile, AXES, [(i, i ^ masks[i % 2]) for i in range(devices)])]
    pallas_call x1, Pallas kernels: 9.52 us -> 7.63 us  [body(): inner(w)]
    pallas_call x1, Pallas kernels: 9.52 us -> 7.63 us  [body(): inner(w2)]
    ppermute x1, starting transfers between devices: 1.41 us -> 2.59 us  [body(): lax.ppermute(outgoing, AXES, [(i, i + 1) for i in range(devices - 1)])]
    pallas_call x2 -> x3, Pallas kernels: 10.7 us -> 9.57 us  [the longest x1 5.55 us: body(): kernel(second_kernel, specs, result, buffers, 'second_stage', 1 << 20, ou...]
    ppermute x2, starting transfers between devices: 2.16 us -> 1.16 us  [body(): lax.ppermute(tile, AXES, [(i, i ^ 1) for i in range(devices)])]
    ppermute x4, starting transfers between devices: 6.68 us -> 7.63 us  [shifted(): lax.ppermute(value, axis, [(i, (i + by) % count) for i in range(count)])]
  transfers between devices with their start and end apart: 17 -> 17, of which waited for: 8 -> 8; matrix products, arithmetic and copies ran while one was open for 1% -> 0% of each run, Pallas kernels for 22% -> 22%
where the time goes in v3:
time: 79 us; the launch traced here: 78.7 us
  starting transfers between devices  31.9 us (40%)
  Pallas kernels  31 us (39%)
  waiting for transfers between devices  15 us (19%)
  between operations  0.79 us (1%)
    ppermute x6, starting transfers between devices, body(): lax.ppermute(tile, AXES, [(i, i ^ masks[i % 2]) for i in range(devices)])  16 us
    ppermute x6, waiting for transfers between devices, body(): lax.ppermute(tile, AXES, [(i, i ^ masks[i % 2]) for i in range(devices)])  13 us
    pallas_call x1, Pallas kernels, body(): inner(w)  7.63 us
    pallas_call x1, Pallas kernels, body(): inner(w2)  7.63 us
    ppermute x4, starting transfers between devices, shifted(): lax.ppermute(value, axis, [(i, (i + by) % count) for i in range(count)])  7.63 us
    pallas_call x1, Pallas kernels, body(): kernel(second_kernel, specs, result, buffers, 'second_stage', 1 << 20, ou...  5.55 us
    ppermute x2, starting transfers between devices, exchanged(): lax.ppermute(yf, 'dev', far)  4.51 us
    pallas_call x1, Pallas kernels, body(): kernel(assemble_kernel, [SMEM, VMEM, ANY, ANY], [GRID, GRID] + sides, [pl...  3.69 us
  transfers between devices with their start and end apart: 17, of which 8 were waited for; matrix products, arithmetic and copies ran while one was open for 0% of the time, Pallas kernels for 22%

profile of v3, /device:TPU:0, one launch (start us, length us, event | category | flops | bytes accessed | tf_op | source)
XLA Modules:
  0.0 78.7 jit_solution(11496359621274491987)
XLA Ops:
  0.7 1.7 %outgoing.1 = f32[15,32,8,128]{3,2,1,0:T(8,128)S(1)} custom-call(s32[1]{0:T(128)S(6)} %copy.3.count_ref, f32[31,32,8,128]{3,2,1,0:T(8,128)} %bitcast.7), custom_call_target="tpu_custom_call" | custom-call | flops 1024 | bytes 6291456 | tf_op jit(solution)/shard_map/outgoing/pallas_call | solution.py:505
  2.4 2.6 %collective-permute-start.8 = (f32[15,32,8,128]{3,2,1,0:T(8,128)S(1)}, f32[15,32,8,128]{3,2,1,0:T(8,128)}, u32[]{:S(2)}, u32[]{:S(2)}) collective-permute-start(f32[15,32,8,128]{3,2,1,0:T(8,128)S(1)} %outgoing.1), channel_id=1, source_target_pairs={{0,1},{1,2},{2,3},{3,4},{4,5},{5,6},{6,7},{7,8},{8,9},{9,10},{10,1... | collective-permute-start | bytes 5898248 | tf_op jit(solution)/shard_map/ppermute | solution.py:508
  4.9 0.0 copy-start
  4.9 2.3 %signal_speed.1 = f32[8,128]{1,0:T(8,128)S(1)} custom-call(s32[1]{0:T(128)S(6)} %copy.3.count_ref, s32[1]{0:T(128)} %bitcast.place_ref, f32[31,32,8,128]{3,2,1,0:T(8,128)} %bitcast.8), custom_call_target="tpu_custom_call" | custom-call | flops 1048576 | bytes 6291456 | tf_op jit(solution)/shard_map/signal_speed/pallas_call | solution.py:509
  7.3 1.2 %collective-permute-start = (f32[8,128]{1,0:T(8,128)S(1)}, f32[8,128]{1,0:T(8,128)S(1)}, u32[]{:S(2)}, u32[]{:S(2)}) collective-permute-start(f32[8,128]{1,0:T(8,128)S(1)} %signal_speed.1), channel_id=1, source_target_pairs={{0,1},{1,0},{2,3},{3,2},{4,5},{5,4},{6,7},{7,6},{8,9},{9,8},{10,11... | collective-permute-start | bytes 12296 | tf_op jit(solution)/shard_map/ppermute | solution.py:520
  8.4 0.8 %collective-permute-done = f32[8,128]{1,0:T(8,128)S(1)} collective-permute-done((f32[8,128]{1,0:T(8,128)S(1)}, f32[8,128]{1,0:T(8,128)S(1)}, u32[]{:S(2)}, u32[]{:S(2)}) %collective-permute-start) | collective-permute-done | bytes 4128 | tf_op jit(solution)/shard_map/ppermute | solution.py:520
  9.3 1.4 %collective-permute-start.1 = (f32[8,128]{1,0:T(8,128)S(1)}, f32[8,128]{1,0:T(8,128)S(1)}, u32[]{:S(2)}, u32[]{:S(2)}) collective-permute-start(f32[8,128]{1,0:T(8,128)S(1)} %max.24), channel_id=1, source_target_pairs={{0,2},{1,33},{2,0},{3,35},{4,6},{5,37},{6,4},{7,39},{8,10},{9,41},... | collective-permute-start | bytes 12296 | tf_op jit(solution)/shard_map/ppermute | solution.py:523
  10.7 2.2 %collective-permute-done.1 = f32[8,128]{1,0:T(8,128)S(1)} collective-permute-done((f32[8,128]{1,0:T(8,128)S(1)}, f32[8,128]{1,0:T(8,128)S(1)}, u32[]{:S(2)}, u32[]{:S(2)}) %collective-permute-start.1) | collective-permute-done | bytes 4128 | tf_op jit(solution)/shard_map/ppermute | solution.py:523
  12.9 2.5 %collective-permute-start.2 = (f32[8,128]{1,0:T(8,128)S(1)}, f32[8,128]{1,0:T(8,128)S(1)}, u32[]{:S(2)}, u32[]{:S(2)}) collective-permute-start(f32[8,128]{1,0:T(8,128)S(1)} %max.25), channel_id=1, source_target_pairs={{0,6},{1,97},{2,4},{3,99},{4,2},{5,101},{6,0},{7,103},{8,14},{9,10... | collective-permute-start | bytes 12296 | tf_op jit(solution)/shard_map/ppermute | solution.py:523
  15.4 2.7 %collective-permute-done.2 = f32[8,128]{1,0:T(8,128)S(1)} collective-permute-done((f32[8,128]{1,0:T(8,128)S(1)}, f32[8,128]{1,0:T(8,128)S(1)}, u32[]{:S(2)}, u32[]{:S(2)}) %collective-permute-start.2) | collective-permute-done | bytes 4128 | tf_op jit(solution)/shard_map/ppermute | solution.py:523
  18.1 1.5 %collective-permute-start.3 = (f32[8,128]{1,0:T(8,128)S(1)}, f32[8,128]{1,0:T(8,128)S(1)}, u32[]{:S(2)}, u32[]{:S(2)}) collective-permute-start(f32[8,128]{1,0:T(8,128)S(1)} %max.26), channel_id=1, source_target_pairs={{0,8},{1,33},{2,10},{3,35},{4,12},{5,37},{6,14},{7,39},{8,0},{9,41... | collective-permute-start | bytes 12296 | tf_op jit(solution)/shard_map/ppermute | solution.py:523
  19.6 2.1 %collective-permute-done.3 = f32[8,128]{1,0:T(8,128)S(1)} collective-permute-done((f32[8,128]{1,0:T(8,128)S(1)}, f32[8,128]{1,0:T(8,128)S(1)}, u32[]{:S(2)}, u32[]{:S(2)}) %collective-permute-start.3) | collective-permute-done | bytes 4128 | tf_op jit(solution)/shard_map/ppermute | solution.py:523
  21.7 2.4 %collective-permute-start.4 = (f32[8,128]{1,0:T(8,128)S(1)}, f32[8,128]{1,0:T(8,128)S(1)}, u32[]{:S(2)}, u32[]{:S(2)}) collective-permute-start(f32[8,128]{1,0:T(8,128)S(1)} %max.27), channel_id=1, source_target_pairs={{0,24},{1,97},{2,26},{3,99},{4,28},{5,101},{6,30},{7,103},{8,16},{... | collective-permute-start | bytes 12296 | tf_op jit(solution)/shard_map/ppermute | solution.py:523
  24.1 2.4 %collective-permute-done.4 = f32[8,128]{1,0:T(8,128)S(1)} collective-permute-done((f32[8,128]{1,0:T(8,128)S(1)}, f32[8,128]{1,0:T(8,128)S(1)}, u32[]{:S(2)}, u32[]{:S(2)}) %collective-permute-start.4) | collective-permute-done | bytes 4128 | tf_op jit(solution)/shard_map/ppermute | solution.py:523
  26.5 1.5 %collective-permute-start.5 = (f32[8,128]{1,0:T(8,128)S(1)}, f32[8,128]{1,0:T(8,128)S(1)}, u32[]{:S(2)}, u32[]{:S(2)}) collective-permute-start(f32[8,128]{1,0:T(8,128)S(1)} %max.28), channel_id=1, source_target_pairs={{0,32},{1,33},{2,34},{3,35},{4,36},{5,37},{6,38},{7,39},{8,40},{9,... | collective-permute-start | bytes 12296 | tf_op jit(solution)/shard_map/ppermute | solution.py:523
  28.1 2.1 %collective-permute-done.5 = f32[8,128]{1,0:T(8,128)S(1)} collective-permute-done((f32[8,128]{1,0:T(8,128)S(1)}, f32[8,128]{1,0:T(8,128)S(1)}, u32[]{:S(2)}, u32[]{:S(2)}) %collective-permute-start.5) | collective-permute-done | bytes 4128 | tf_op jit(solution)/shard_map/ppermute | solution.py:523
  30.1 6.6 %collective-permute-start.6 = (f32[8,128]{1,0:T(8,128)S(1)}, f32[8,128]{1,0:T(8,128)S(1)}, u32[]{:S(2)}, u32[]{:S(2)}) collective-permute-start(f32[8,128]{1,0:T(8,128)S(1)} %max.29), channel_id=1, source_target_pairs={{0,96},{1,97},{2,98},{3,99},{4,100},{5,101},{6,102},{7,103},{8,104... | collective-permute-start | bytes 12296 | tf_op jit(solution)/shard_map/ppermute | solution.py:523
  36.7 1.6 %collective-permute-done.6 = f32[8,128]{1,0:T(8,128)S(1)} collective-permute-done((f32[8,128]{1,0:T(8,128)S(1)}, f32[8,128]{1,0:T(8,128)S(1)}, u32[]{:S(2)}, u32[]{:S(2)}) %collective-permute-start.6) | collective-permute-done | bytes 4128 | tf_op jit(solution)/shard_map/ppermute | solution.py:523
  38.3 0.0 collective-permute-start.7
  38.3 1.2 %collective-permute-done.7 = f32[8,128]{1,0:T(8,128)S(1)} collective-permute-done((f32[8,128]{1,0:T(8,128)S(1)}, f32[8,128]{1,0:T(8,128)S(1)}, u32[]{:S(2)}, u32[]{:S(2)}) %collective-permute-start.7) | collective-permute-done | bytes 4128 | tf_op jit(solution)/shard_map/ppermute | solution.py:524
  39.5 0.0 collective-permute-done.8.came_ref
  39.5 0.0 copy-done
  39.5 3.7 %assemble.1 = (f32[16,4,8,8,128]{4,3,2,1,0:T(8,128)S(1)}, f32[16,4,8,8,128]{4,3,2,1,0:T(8,128)S(1)}, f32[2,4,8,8,128]{4,3,2,1,0:T(8,128)S(1)}, f32[2,4,8,8,128]{...) custom-call(s32[1]{0:T(128)} %bitcast.place_ref, f32[8,128]{1,0:T(8,128)S(1)} %max.31.tile_ref, ...), custom_call_target="tpu_custom_call" | custom-call | flops 1048576 | bytes 6291456 | tf_op jit(solution)/shard_map/assemble/pallas_call | solution.py:526
  43.2 1.1 %collective-permute-start.9 = (f32[2,4,8,8,128]{4,3,2,1,0:T(8,128)S(1)}, f32[2,4,8,8,128]{4,3,2,1,0:T(8,128)S(1)}, u32[]{:S(2)}, u32[]{:S(2)}) collective-permute-start(f32[2,4,8,8,128]{4,3,2,1,0:T(8,128)S(1)} %get-tuple-element.29), channel_id=1, source_target_pairs={{0,32},{32,64},{64,96},{96,0},{1,33},{33,65},{65,97},{97,1},{2,34}... | collective-permute-start | bytes 786440 | tf_op jit(solution)/shard_map/ppermute | solution.py:488
  44.3 3.3 %collective-permute-start.10 = (f32[2,4,8,8,128]{4,3,2,1,0:T(8,128)S(1)}, f32[2,4,8,8,128]{4,3,2,1,0:T(8,128)S(1)}, u32[]{:S(2)}, u32[]{:S(2)}) collective-permute-start(f32[2,4,8,8,128]{4,3,2,1,0:T(8,128)S(1)} %get-tuple-element.30), channel_id=1, source_target_pairs={{0,96},{32,0},{64,32},{96,64},{1,97},{33,1},{65,33},{97,65},{2,98}... | collective-permute-start | bytes 786440 | tf_op jit(solution)/shard_map/ppermute | solution.py:488
  47.5 0.0 collective-permute-start.11
  47.5 1.5 %collective-permute-start.12 = (f32[2,2,8,8,128]{4,3,2,1,0:T(8,128)S(1)}, f32[2,2,8,8,128]{4,3,2,1,0:T(8,128)S(1)}, u32[]{:S(2)}, u32[]{:S(2)}) collective-permute-start(f32[2,2,8,8,128]{4,3,2,1,0:T(8,128)S(1)} %get-tuple-element.32), channel_id=1, source_target_pairs={{0,31},{1,2},{2,1},{3,4},{4,3},{5,6},{6,5},{7,8},{8,7},{9,10},{10,... | collective-permute-start | bytes 393224 | tf_op jit(solution)/shard_map/ppermute | solution.py:495
  49.0 7.6 %inner_fluxes.2 = (f32[16,4,8,8,128]{4,3,2,1,0:T(8,128)S(1)}, f32[16,4,8,8,128]{4,3,2,1,0:T(8,128)S(1)}) custom-call(f32[16,4,8,8,128]{4,3,2,1,0:T(8,128)S(1)} %get-tuple-element.25.w_ref), custom_call_target="tpu_custom_call" | custom-call | flops 41943040 | bytes 6291456 | tf_op jit(solution)/shard_map/inner_fluxes/pallas_call | solution.py:539
  56.7 0.0 collective-permute-done.11.yn
  56.7 0.0 collective-permute-done.12.yf
  56.7 0.0 collective-permute-done.9.xl
  56.7 0.0 collective-permute-done.10.xh
  56.7 2.5 %first_stage.1 = (f32[16,4,8,8,128]{4,3,2,1,0:T(8,128)S(1)}, f32[16,4,8,8,128]{4,3,2,1,0:T(8,128)S(1)}, f32[2,4,8,8,128]{4,3,2,1,0:T(8,128)S(1)}, f32[2,4,8,8,12...) custom-call(s32[1]{0:T(128)} %bitcast.place_ref, ...), custom_call_target="tpu_custom_call" | custom-call | flops 1048576 | bytes 6291456 | tf_op jit(solution)/shard_map/first_stage/pallas_call | solution.py:538
  59.2 0.1 collective-permute-start.13
  59.3 3.2 %collective-permute-start.14 = (f32[2,4,8,8,128]{4,3,2,1,0:T(8,128)S(1)}, f32[2,4,8,8,128]{4,3,2,1,0:T(8,128)S(1)}, u32[]{:S(2)}, u32[]{:S(2)}) collective-permute-start(f32[2,4,8,8,128]{4,3,2,1,0:T(8,128)S(1)} %get-tuple-element.38), channel_id=1, source_target_pairs={{0,96},{32,0},{64,32},{96,64},{1,97},{33,1},{65,33},{97,65},{2,98}... | collective-permute-start | bytes 786440 | tf_op jit(solution)/shard_map/ppermute | solution.py:488
  62.5 0.0 collective-permute-start.15
  62.5 3.0 %collective-permute-start.16 = (f32[2,2,8,8,128]{4,3,2,1,0:T(8,128)S(1)}, f32[2,2,8,8,128]{4,3,2,1,0:T(8,128)S(1)}, u32[]{:S(2)}, u32[]{:S(2)}) collective-permute-start(f32[2,2,8,8,128]{4,3,2,1,0:T(8,128)S(1)} %get-tuple-element.40), channel_id=1, source_target_pairs={{0,31},{1,2},{2,1},{3,4},{4,3},{5,6},{6,5},{7,8},{8,7},{9,10},{10,... | collective-permute-start | bytes 393224 | tf_op jit(solution)/shard_map/ppermute | solution.py:495
  65.5 7.6 %inner_fluxes.3 = (f32[16,4,8,8,128]{4,3,2,1,0:T(8,128)S(1)}, f32[16,4,8,8,128]{4,3,2,1,0:T(8,128)S(1)}) custom-call(f32[16,4,8,8,128]{4,3,2,1,0:T(8,128)S(1)} %get-tuple-element.33.w_ref), custom_call_target="tpu_custom_call" | custom-call | flops 41943040 | bytes 6291456 | tf_op jit(solution)/shard_map/inner_fluxes/pallas_call | solution.py:545
  73.1 0.0 collective-permute-done.15.yn
  73.2 0.0 collective-permute-done.16.yf
  73.2 0.0 collective-permute-done.13.xl
  73.2 0.0 collective-permute-done.14.xh
  73.2 5.5 %second_stage.1 = f32[16,32,8,128]{3,2,1,0:T(8,128)} custom-call(s32[1]{0:T(128)} %bitcast.place_ref, f32[8,128]{1,0:T(8,128)S(1)} %max.31.tile_ref, f32[16,4,8,8,128]{4,3,2,1,0:T(8,128)S(1)} %get-tuple-element.33.w_ref, f32[16,4,8,8,128]{4,3,2,1,0:T(8,128)S(1)} %get-tuple-element.34.s_ref, f32[16,4,8,8,128]{4,3,2,1,0:T(8,128)S(1)} %get-tuple-element.35.txz, ...), custom_call_target="tpu_custom_call" | custom-call | flops 1048576 | bytes 6291456 | tf_op jit(solution)/shard_map/second_stage/pallas_call | solution.py:544
  (8 shorter events, 0.0 us)
Async XLA Ops:
  2.4 37.1 %collective-permute-start.8 = (f32[15,32,8,128]{3,2,1,0:T(8,128)S(1)}, f32[15,32,8,128]{3,2,1,0:T(8,128)}, u32[]{:S(2)}, u32[]{:S(2)}) collective-permute-start(f32[15,32,8,128]{3,2,1,0:T(8,128)S(1)} %outgoing.1), channel_id=1, source_target_pairs={{0,1},{1,2},{2,3},{3,4},{4,5},{5,6},{6,7},{7,8},{8,9},{9,10},{10,1... | collective-permute-start | bytes 5898248 | tf_op jit(solution)/shard_map/ppermute | solution.py:508
  4.9 34.5 %copy-start = (f32[31,8,4096]{2,1,0:T(8,128)S(1)}, f32[31,8,4096]{2,1,0:T(8,128)}, u32[]{:S(2)}) copy-start(f32[31,8,4096]{2,1,0:T(8,128)} %param.2) | copy-start | bytes 12189700
  7.3 2.0 %collective-permute-start = (f32[8,128]{1,0:T(8,128)S(1)}, f32[8,128]{1,0:T(8,128)S(1)}, u32[]{:S(2)}, u32[]{:S(2)}) collective-permute-start(f32[8,128]{1,0:T(8,128)S(1)} %signal_speed.1), channel_id=1, source_target_pairs={{0,1},{1,0},{2,3},{3,2},{4,5},{5,4},{6,7},{7,6},{8,9},{9,8},{10,11... | collective-permute-start | bytes 12296 | tf_op jit(solution)/shard_map/ppermute | solution.py:520
  9.3 3.6 %collective-permute-start.1 = (f32[8,128]{1,0:T(8,128)S(1)}, f32[8,128]{1,0:T(8,128)S(1)}, u32[]{:S(2)}, u32[]{:S(2)}) collective-permute-start(f32[8,128]{1,0:T(8,128)S(1)} %max.24), channel_id=1, source_target_pairs={{0,2},{1,33},{2,0},{3,35},{4,6},{5,37},{6,4},{7,39},{8,10},{9,41},... | collective-permute-start | bytes 12296 | tf_op jit(solution)/shard_map/ppermute | solution.py:523
  12.9 5.2 %collective-permute-start.2 = (f32[8,128]{1,0:T(8,128)S(1)}, f32[8,128]{1,0:T(8,128)S(1)}, u32[]{:S(2)}, u32[]{:S(2)}) collective-permute-start(f32[8,128]{1,0:T(8,128)S(1)} %max.25), channel_id=1, source_target_pairs={{0,6},{1,97},{2,4},{3,99},{4,2},{5,101},{6,0},{7,103},{8,14},{9,10... | collective-permute-start | bytes 12296 | tf_op jit(solution)/shard_map/ppermute | solution.py:523
  18.1 3.6 %collective-permute-start.3 = (f32[8,128]{1,0:T(8,128)S(1)}, f32[8,128]{1,0:T(8,128)S(1)}, u32[]{:S(2)}, u32[]{:S(2)}) collective-permute-start(f32[8,128]{1,0:T(8,128)S(1)} %max.26), channel_id=1, source_target_pairs={{0,8},{1,33},{2,10},{3,35},{4,12},{5,37},{6,14},{7,39},{8,0},{9,41... | collective-permute-start | bytes 12296 | tf_op jit(solution)/shard_map/ppermute | solution.py:523
  21.7 4.8 %collective-permute-start.4 = (f32[8,128]{1,0:T(8,128)S(1)}, f32[8,128]{1,0:T(8,128)S(1)}, u32[]{:S(2)}, u32[]{:S(2)}) collective-permute-start(f32[8,128]{1,0:T(8,128)S(1)} %max.27), channel_id=1, source_target_pairs={{0,24},{1,97},{2,26},{3,99},{4,28},{5,101},{6,30},{7,103},{8,16},{... | collective-permute-start | bytes 12296 | tf_op jit(solution)/shard_map/ppermute | solution.py:523
  26.5 3.6 %collective-permute-start.5 = (f32[8,128]{1,0:T(8,128)S(1)}, f32[8,128]{1,0:T(8,128)S(1)}, u32[]{:S(2)}, u32[]{:S(2)}) collective-permute-start(f32[8,128]{1,0:T(8,128)S(1)} %max.28), channel_id=1, source_target_pairs={{0,32},{1,33},{2,34},{3,35},{4,36},{5,37},{6,38},{7,39},{8,40},{9,... | collective-permute-start | bytes 12296 | tf_op jit(solution)/shard_map/ppermute | solution.py:523
  30.1 8.2 %collective-permute-start.6 = (f32[8,128]{1,0:T(8,128)S(1)}, f32[8,128]{1,0:T(8,128)S(1)}, u32[]{:S(2)}, u32[]{:S(2)}) collective-permute-start(f32[8,128]{1,0:T(8,128)S(1)} %max.29), channel_id=1, source_target_pairs={{0,96},{1,97},{2,98},{3,99},{4,100},{5,101},{6,102},{7,103},{8,104... | collective-permute-start | bytes 12296 | tf_op jit(solution)/shard_map/ppermute | solution.py:523
  38.3 1.2 %collective-permute-start.7 = (f32[8,128]{1,0:T(8,128)S(1)}, f32[8,128]{1,0:T(8,128)S(1)}, u32[]{:S(2)}, u32[]{:S(2)}) collective-permute-start(f32[8,128]{1,0:T(8,128)S(1)} %max.30), channel_id=1, source_target_pairs={{0,1},{1,0},{2,3},{3,2},{4,5},{5,4},{6,7},{7,6},{8,9},{9,8},{10,11... | collective-permute-start | bytes 12296 | tf_op jit(solution)/shard_map/ppermute | solution.py:524
  43.2 13.5 %collective-permute-start.9 = (f32[2,4,8,8,128]{4,3,2,1,0:T(8,128)S(1)}, f32[2,4,8,8,128]{4,3,2,1,0:T(8,128)S(1)}, u32[]{:S(2)}, u32[]{:S(2)}) collective-permute-start(f32[2,4,8,8,128]{4,3,2,1,0:T(8,128)S(1)} %get-tuple-element.29), channel_id=1, source_target_pairs={{0,32},{32,64},{64,96},{96,0},{1,33},{33,65},{65,97},{97,1},{2,34}... | collective-permute-start | bytes 786440 | tf_op jit(solution)/shard_map/ppermute | solution.py:488
  44.3 12.5 %collective-permute-start.10 = (f32[2,4,8,8,128]{4,3,2,1,0:T(8,128)S(1)}, f32[2,4,8,8,128]{4,3,2,1,0:T(8,128)S(1)}, u32[]{:S(2)}, u32[]{:S(2)}) collective-permute-start(f32[2,4,8,8,128]{4,3,2,1,0:T(8,128)S(1)} %get-tuple-element.30), channel_id=1, source_target_pairs={{0,96},{32,0},{64,32},{96,64},{1,97},{33,1},{65,33},{97,65},{2,98}... | collective-permute-start | bytes 786440 | tf_op jit(solution)/shard_map/ppermute | solution.py:488
  47.5 9.2 %collective-permute-start.11 = (f32[2,2,8,8,128]{4,3,2,1,0:T(8,128)S(1)}, f32[2,2,8,8,128]{4,3,2,1,0:T(8,128)S(1)}, u32[]{:S(2)}, u32[]{:S(2)}) collective-permute-start(f32[2,2,8,8,128]{4,3,2,1,0:T(8,128)S(1)} %get-tuple-element.31), channel_id=1, source_target_pairs={{0,1},{1,0},{2,3},{3,2},{4,5},{5,4},{6,7},{7,6},{8,9},{9,8},{10,11... | collective-permute-start | bytes 393224 | tf_op jit(solution)/shard_map/ppermute | solution.py:495
  47.5 9.2 %collective-permute-start.12 = (f32[2,2,8,8,128]{4,3,2,1,0:T(8,128)S(1)}, f32[2,2,8,8,128]{4,3,2,1,0:T(8,128)S(1)}, u32[]{:S(2)}, u32[]{:S(2)}) collective-permute-start(f32[2,2,8,8,128]{4,3,2,1,0:T(8,128)S(1)} %get-tuple-element.32), channel_id=1, source_target_pairs={{0,31},{1,2},{2,1},{3,4},{4,3},{5,6},{6,5},{7,8},{8,7},{9,10},{10,... | collective-permute-start | bytes 393224 | tf_op jit(solution)/shard_map/ppermute | solution.py:495
  59.2 14.0 %collective-permute-start.13 = (f32[2,4,8,8,128]{4,3,2,1,0:T(8,128)S(1)}, f32[2,4,8,8,128]{4,3,2,1,0:T(8,128)S(1)}, u32[]{:S(2)}, u32[]{:S(2)}) collective-permute-start(f32[2,4,8,8,128]{4,3,2,1,0:T(8,128)S(1)} %get-tuple-element.37), channel_id=1, source_target_pairs={{0,32},{32,64},{64,96},{96,0},{1,33},{33,65},{65,97},{97,1},{2,34}... | collective-permute-start | bytes 786440 | tf_op jit(solution)/shard_map/ppermute | solution.py:488
  59.3 13.9 %collective-permute-start.14 = (f32[2,4,8,8,128]{4,3,2,1,0:T(8,128)S(1)}, f32[2,4,8,8,128]{4,3,2,1,0:T(8,128)S(1)}, u32[]{:S(2)}, u32[]{:S(2)}) collective-permute-start(f32[2,4,8,8,128]{4,3,2,1,0:T(8,128)S(1)} %get-tuple-element.38), channel_id=1, source_target_pairs={{0,96},{32,0},{64,32},{96,64},{1,97},{33,1},{65,33},{97,65},{2,98}... | collective-permute-start | bytes 786440 | tf_op jit(solution)/shard_map/ppermute | solution.py:488
  62.5 10.6 %collective-permute-start.15 = (f32[2,2,8,8,128]{4,3,2,1,0:T(8,128)S(1)}, f32[2,2,8,8,128]{4,3,2,1,0:T(8,128)S(1)}, u32[]{:S(2)}, u32[]{:S(2)}) collective-permute-start(f32[2,2,8,8,128]{4,3,2,1,0:T(8,128)S(1)} %get-tuple-element.39), channel_id=1, source_target_pairs={{0,1},{1,0},{2,3},{3,2},{4,5},{5,4},{6,7},{7,6},{8,9},{9,8},{10,11... | collective-permute-start | bytes 393224 | tf_op jit(solution)/shard_map/ppermute | solution.py:495
  62.5 10.6 %collective-permute-start.16 = (f32[2,2,8,8,128]{4,3,2,1,0:T(8,128)S(1)}, f32[2,2,8,8,128]{4,3,2,1,0:T(8,128)S(1)}, u32[]{:S(2)}, u32[]{:S(2)}) collective-permute-start(f32[2,2,8,8,128]{4,3,2,1,0:T(8,128)S(1)} %get-tuple-element.40), channel_id=1, source_target_pairs={{0,31},{1,2},{2,1},{3,4},{4,3},{5,6},{6,5},{7,8},{8,7},{9,10},{10,... | collective-permute-start | bytes 393224 | tf_op jit(solution)/shard_map/ppermute | solution.py:495

commit v4 on v3

--- a/solution.py
+++ b/solution.py
@@ -47,21 +47,25 @@
     return [density] + velocity + [pressure] + list(magnetic)
 
 
-def fast_speed(prims, normal, inverse, square):
+def fast_speed(prims, normal, inverse, half):
     magnetic = prims[5:8]
     along = magnetic[normal] * magnetic[normal] * inverse
-    sound = (GAMMA * prims[4]) * inverse
-    total = sound + square * inverse
-    inner = jnp.maximum(total * total - (4.0 * sound) * along, TINY)
-    return root(0.5 * (total + root(inner)))
+    sound = (0.5 * GAMMA * prims[4]) * inverse
+    total = sound + half * inverse
+    inner = jnp.maximum(total * total - (2.0 * sound) * along, TINY)
+    return root(total + root(inner))
+
+
+def half_square(field):
+    return 0.5 * (field[0] * field[0] + field[1] * field[1] + field[2] * field[2])
 
 
 def side(prims, normal):
     density, pressure = prims[0], prims[4]
     velocity, magnetic = prims[1:4], prims[5:8]
-    square = magnetic[0] * magnetic[0] + magnetic[1] * magnetic[1] + magnetic[2] * magnetic[2]
-    fast = fast_speed(prims, normal, 1.0 / density, square)
-    total = pressure + 0.5 * square
+    half = half_square(magnetic)
+    fast = fast_speed(prims, normal, 1.0 / density, half)
+    total = pressure + half
     motion = velocity[0] * velocity[0] + velocity[1] * velocity[1] + velocity[2] * velocity[2]
     energy = total + 0.5 * (pressure + density * motion)
     cross = velocity[0] * magnetic[0] + velocity[1] * magnetic[1] + velocity[2] * magnetic[2]
@@ -79,7 +83,7 @@
     momentum[normal] = momentum[normal] + push
     power = carried * energy + push * velocity[normal] - bent * cross
     induced = [carried * magnetic[k] - bent * velocity[k] for k in range(3)]
-    induced[normal] = -(other * bent)
+    induced[normal] = other * bent
     return [mass] + momentum + [power] + induced
 
 
@@ -92,7 +96,9 @@
     weight = upper * (1.0 / (upper - lower))
     part_l = weighed(left, normal, weight, lower, total_l, energy_l, cross_l)
     part_r = weighed(right, normal, 1.0 - weight, upper, total_r, energy_r, cross_r)
-    return [a + b for a, b in zip(part_l, part_r)]
+    flux = [a + b for a, b in zip(part_l, part_r)]
+    flux[5 + normal] = -flux[5 + normal]
+    return flux
 
 
 def minus(first, second):
@@ -157,11 +163,10 @@
 
     def speeds(start, tops):
         prims = primitive([rows[pl.ds(start + k, 8, stride=8), :] for k in range(FIELDS)])
-        magnetic = prims[5:8]
-        square = magnetic[0] * magnetic[0] + magnetic[1] * magnetic[1] + magnetic[2] * magnetic[2]
+        half = half_square(prims[5:8])
         inverse = 1.0 / prims[0]
         for normal in range(3):
-            speed = jnp.abs(prims[1 + normal]) + fast_speed(prims, normal, inverse, square)
+            speed = jnp.abs(prims[1 + normal]) + fast_speed(prims, normal, inverse, half)
             tops[normal] = jnp.maximum(tops[normal], speed)
 
     def several(index, tops):
@@ -250,7 +255,7 @@
             put(w_ref, x, t, primitive(state))
             return 0
 
-        lax.fori_loop(0, CHUNKS, chunk, 0, unroll=4)
+        lax.fori_loop(0, CHUNKS, chunk, 0, unroll=16)
     pack_sides(place % 2, w_ref, xl_ref, xh_ref, yn_ref, yf_ref)
 
 
@@ -329,7 +334,7 @@
                 result.append((forward, after, new))
             return result
 
-        for t, (_, _, flux) in zip(both, lax.fori_loop(2, 14, step, start)):
+        for t, (_, _, flux) in zip(both, lax.fori_loop(2, 14, step, start, unroll=3)):
             store(14, t, flux)
             store(15, t)
         return 0
@@ -357,7 +362,7 @@
         put(xc, 3, t, minus(a, b))
         return 0
 
-    lax.fori_loop(0, TS, column, 0)
+    lax.fori_loop(0, TS, column, 0, unroll=4)
     rows = w_ref.reshape(XS * 256, 128)
     packed = yc.reshape(XS * 128, 128)
     zero = jnp.zeros((8, 128), jnp.float32)
@@ -398,7 +403,7 @@
 def each_layer(work):
     for edge, x in enumerate((0, 1, XS - 2, XS - 1)):
         work(x, edge)
-    lax.fori_loop(2, XS - 2, lambda x, _: (work(x, None), 0)[1], 0)
+    lax.fori_loop(2, XS - 2, lambda x, _: (work(x, None), 0)[1], 0, unroll=4)
 
 
 def step_of(tile_ref):
@@ -440,18 +445,18 @@
         chunks = pl.ds(quarter * 8, 8)
         return pltpu.make_async_copy(blocks.at[:, chunks], out_ref.at[:, chunks], sems.at[quarter])
 
-    def inside(first, last):
-        lax.fori_loop(first, last, lambda x, _: (work(x, None), 0)[1], 0)
+    def pairs(first, last):
+        lax.fori_loop(first, last, lambda x, _: (work(x, None), 0)[1], 0, unroll=min(4, last - first))
 
     work(0, 0)
     work(1, 1)
-    inside(2, 4)
+    pairs(2, 4)
     part(0).start()
-    inside(4, 8)
+    pairs(4, 8)
     part(1).start()
-    inside(8, 12)
+    pairs(8, 12)
     part(2).start()
-    inside(12, 14)
+    pairs(12, 14)
     work(14, 2)
     work(15, 3)
     part(3).start()
@@ -518,7 +523,6 @@
         1 << 20,
     )(counts, place, there)
     tile = jnp.maximum(tile, lax.ppermute(tile, AXES, [(i, i ^ 1) for i in range(devices)]))
-    tile, own = lax.optimization_barrier((tile, own))
     for masks in ROUNDS:
         tile = jnp.maximum(tile, lax.ppermute(tile, AXES, [(i, i ^ masks[i % 2]) for i in range(devices)]))
     tile = jnp.maximum(tile, lax.ppermute(tile, AXES, [(i, i ^ 1) for i in range(devices)]))
@@ -530,7 +534,7 @@
         [pltpu.VMEM((2, CHUNKS, 8, FIELDS, 128), jnp.float32), pltpu.SemaphoreType.DMA((BLK_DEV,))],
         "assemble",
         1 << 20,
-    )(place, tile, came, own)
+    )(place, tile, pltpu.with_memory_space_constraint(came, pltpu.HBM), there)
     corrections = [pltpu.VMEM((4, TS, FIELDS, 8, 128), jnp.float32), pltpu.VMEM((XS, 2, FIELDS, 8, 128), jnp.float32)]
     inner = kernel(inner_kernel, [VMEM], [GRID] * 2, [pltpu.VMEM(GRID, jnp.float32)] * 3, "inner_fluxes", 40 << 20)
     specs = [SMEM] + [VMEM] * 9

time: 79 us -> 75.2 us (0.952)
  Pallas kernels: 31 us -> 28.3 us
  waiting for transfers between devices: 15 us -> 13.7 us
    pallas_call x1, Pallas kernels: 5.55 us -> 3.69 us  [body(): kernel(second_kernel, specs, result, buffers, 'second_stage', 1 << 20, ou...]
    ppermute x6, starting transfers between devices: 16 us -> 17.8 us  [body(): lax.ppermute(tile, AXES, [(i, i ^ masks[i % 2]) for i in range(devices)])]
    ppermute x6, waiting for transfers between devices: 13 us -> 11.7 us  [body(): lax.ppermute(tile, AXES, [(i, i ^ masks[i % 2]) for i in range(devices)])]
    ppermute x4, starting transfers between devices: 7.63 us -> 6.67 us  [shifted(): lax.ppermute(value, axis, [(i, (i + by) % count) for i in range(count)])]
  transfers between devices with their start and end apart: 17 -> 17, of which waited for: 8 -> 8; matrix products, arithmetic and copies ran while one was open for 0% -> 0% of each run, Pallas kernels for 22% -> 23%
where the time goes in v4:
time: 75.2 us; the launch traced here: 75 us
  starting transfers between devices  32 us (43%)
  Pallas kernels  28.3 us (38%)
  waiting for transfers between devices  13.7 us (18%)
  between operations  0.95 us (1%)
    ppermute x6, starting transfers between devices, body(): lax.ppermute(tile, AXES, [(i, i ^ masks[i % 2]) for i in range(devices)])  17.8 us
    ppermute x6, waiting for transfers between devices, body(): lax.ppermute(tile, AXES, [(i, i ^ masks[i % 2]) for i in range(devices)])  11.7 us
    pallas_call x1, Pallas kernels, body(): inner(w)  7.24 us
    pallas_call x1, Pallas kernels, body(): inner(w2)  7.24 us
    ppermute x4, starting transfers between devices, shifted(): lax.ppermute(value, axis, [(i, (i + by) % count) for i in range(count)])  6.67 us
    ppermute x2, starting transfers between devices, exchanged(): lax.ppermute(yf, 'dev', far)  4.51 us
    pallas_call x1, Pallas kernels, body(): kernel(second_kernel, specs, result, buffers, 'second_stage', 1 << 20, ou...  3.69 us
    pallas_call x1, Pallas kernels, body(): kernel(assemble_kernel, [SMEM, VMEM, ANY, ANY], [GRID, GRID] + sides, [pl...  3.54 us
  transfers between devices with their start and end apart: 17, of which 8 were waited for; matrix products, arithmetic and copies ran while one was open for 0% of the time, Pallas kernels for 23%

profile of v4, /device:TPU:0, one launch (start us, length us, event | category | flops | bytes accessed | tf_op | source)
XLA Modules:
  0.0 75.0 jit_solution(11651203180041786032)
XLA Ops:
  0.7 1.7 %outgoing.1 = f32[15,32,8,128]{3,2,1,0:T(8,128)S(1)} custom-call(s32[1]{0:T(128)S(6)} %copy.3.count_ref, f32[31,32,8,128]{3,2,1,0:T(8,128)} %bitcast.7), custom_call_target="tpu_custom_call" | custom-call | flops 1024 | bytes 6291456 | tf_op jit(solution)/shard_map/outgoing/pallas_call | solution.py:510
  2.4 2.6 %collective-permute-start.8 = (f32[15,32,8,128]{3,2,1,0:T(8,128)S(1)}, f32[15,32,8,128]{3,2,1,0:T(8,128)}, u32[]{:S(2)}, u32[]{:S(2)}) collective-permute-start(f32[15,32,8,128]{3,2,1,0:T(8,128)S(1)} %outgoing.1), channel_id=1, source_target_pairs={{0,1},{1,2},{2,3},{3,4},{4,5},{5,6},{6,7},{7,8},{8,9},{9,10},{10,1... | collective-permute-start | bytes 5898248 | tf_op jit(solution)/shard_map/ppermute | solution.py:513
  5.0 2.7 %signal_speed.1 = f32[8,128]{1,0:T(8,128)S(1)} custom-call(s32[1]{0:T(128)S(6)} %copy.3.count_ref, s32[1]{0:T(128)} %bitcast.place_ref, f32[31,32,8,128]{3,2,1,0:T(8,128)} %bitcast.8), custom_call_target="tpu_custom_call" | custom-call | flops 1048576 | bytes 6291456 | tf_op jit(solution)/shard_map/signal_speed/pallas_call | solution.py:514
  7.6 0.5 collective-permute-start
  8.1 0.8 %collective-permute-done = f32[8,128]{1,0:T(8,128)S(1)} collective-permute-done((f32[8,128]{1,0:T(8,128)S(1)}, f32[8,128]{1,0:T(8,128)S(1)}, u32[]{:S(2)}, u32[]{:S(2)}) %collective-permute-start) | collective-permute-done | bytes 4128 | tf_op jit(solution)/shard_map/ppermute | solution.py:525
  8.9 1.4 %collective-permute-start.1 = (f32[8,128]{1,0:T(8,128)S(1)}, f32[8,128]{1,0:T(8,128)S(1)}, u32[]{:S(2)}, u32[]{:S(2)}) collective-permute-start(f32[8,128]{1,0:T(8,128)S(1)} %max.24), channel_id=1, source_target_pairs={{0,2},{1,33},{2,0},{3,35},{4,6},{5,37},{6,4},{7,39},{8,10},{9,41},... | collective-permute-start | bytes 12296 | tf_op jit(solution)/shard_map/ppermute | solution.py:527
  10.3 2.2 %collective-permute-done.1 = f32[8,128]{1,0:T(8,128)S(1)} collective-permute-done((f32[8,128]{1,0:T(8,128)S(1)}, f32[8,128]{1,0:T(8,128)S(1)}, u32[]{:S(2)}, u32[]{:S(2)}) %collective-permute-start.1) | collective-permute-done | bytes 4128 | tf_op jit(solution)/shard_map/ppermute | solution.py:527
  12.5 3.1 %collective-permute-start.2 = (f32[8,128]{1,0:T(8,128)S(1)}, f32[8,128]{1,0:T(8,128)S(1)}, u32[]{:S(2)}, u32[]{:S(2)}) collective-permute-start(f32[8,128]{1,0:T(8,128)S(1)} %max.25), channel_id=1, source_target_pairs={{0,6},{1,97},{2,4},{3,99},{4,2},{5,101},{6,0},{7,103},{8,14},{9,10... | collective-permute-start | bytes 12296 | tf_op jit(solution)/shard_map/ppermute | solution.py:527
  15.7 2.1 %collective-permute-done.2 = f32[8,128]{1,0:T(8,128)S(1)} collective-permute-done((f32[8,128]{1,0:T(8,128)S(1)}, f32[8,128]{1,0:T(8,128)S(1)}, u32[]{:S(2)}, u32[]{:S(2)}) %collective-permute-start.2) | collective-permute-done | bytes 4128 | tf_op jit(solution)/shard_map/ppermute | solution.py:527
  17.8 1.1 %collective-permute-start.3 = (f32[8,128]{1,0:T(8,128)S(1)}, f32[8,128]{1,0:T(8,128)S(1)}, u32[]{:S(2)}, u32[]{:S(2)}) collective-permute-start(f32[8,128]{1,0:T(8,128)S(1)} %max.26), channel_id=1, source_target_pairs={{0,8},{1,33},{2,10},{3,35},{4,12},{5,37},{6,14},{7,39},{8,0},{9,41... | collective-permute-start | bytes 12296 | tf_op jit(solution)/shard_map/ppermute | solution.py:527
  18.9 2.5 %collective-permute-done.3 = f32[8,128]{1,0:T(8,128)S(1)} collective-permute-done((f32[8,128]{1,0:T(8,128)S(1)}, f32[8,128]{1,0:T(8,128)S(1)}, u32[]{:S(2)}, u32[]{:S(2)}) %collective-permute-start.3) | collective-permute-done | bytes 4128 | tf_op jit(solution)/shard_map/ppermute | solution.py:527
  21.4 3.1 %collective-permute-start.4 = (f32[8,128]{1,0:T(8,128)S(1)}, f32[8,128]{1,0:T(8,128)S(1)}, u32[]{:S(2)}, u32[]{:S(2)}) collective-permute-start(f32[8,128]{1,0:T(8,128)S(1)} %max.27), channel_id=1, source_target_pairs={{0,24},{1,97},{2,26},{3,99},{4,28},{5,101},{6,30},{7,103},{8,16},{... | collective-permute-start | bytes 12296 | tf_op jit(solution)/shard_map/ppermute | solution.py:527
  24.5 1.7 %collective-permute-done.4 = f32[8,128]{1,0:T(8,128)S(1)} collective-permute-done((f32[8,128]{1,0:T(8,128)S(1)}, f32[8,128]{1,0:T(8,128)S(1)}, u32[]{:S(2)}, u32[]{:S(2)}) %collective-permute-start.4) | collective-permute-done | bytes 4128 | tf_op jit(solution)/shard_map/ppermute | solution.py:527
  26.2 2.0 %collective-permute-start.5 = (f32[8,128]{1,0:T(8,128)S(1)}, f32[8,128]{1,0:T(8,128)S(1)}, u32[]{:S(2)}, u32[]{:S(2)}) collective-permute-start(f32[8,128]{1,0:T(8,128)S(1)} %max.28), channel_id=1, source_target_pairs={{0,32},{1,33},{2,34},{3,35},{4,36},{5,37},{6,38},{7,39},{8,40},{9,... | collective-permute-start | bytes 12296 | tf_op jit(solution)/shard_map/ppermute | solution.py:527
  28.2 1.6 %collective-permute-done.5 = f32[8,128]{1,0:T(8,128)S(1)} collective-permute-done((f32[8,128]{1,0:T(8,128)S(1)}, f32[8,128]{1,0:T(8,128)S(1)}, u32[]{:S(2)}, u32[]{:S(2)}) %collective-permute-start.5) | collective-permute-done | bytes 4128 | tf_op jit(solution)/shard_map/ppermute | solution.py:527
  29.8 7.0 %collective-permute-start.6 = (f32[8,128]{1,0:T(8,128)S(1)}, f32[8,128]{1,0:T(8,128)S(1)}, u32[]{:S(2)}, u32[]{:S(2)}) collective-permute-start(f32[8,128]{1,0:T(8,128)S(1)} %max.29), channel_id=1, source_target_pairs={{0,96},{1,97},{2,98},{3,99},{4,100},{5,101},{6,102},{7,103},{8,104... | collective-permute-start | bytes 12296 | tf_op jit(solution)/shard_map/ppermute | solution.py:527
  36.8 1.6 %collective-permute-done.6 = f32[8,128]{1,0:T(8,128)S(1)} collective-permute-done((f32[8,128]{1,0:T(8,128)S(1)}, f32[8,128]{1,0:T(8,128)S(1)}, u32[]{:S(2)}, u32[]{:S(2)}) %collective-permute-start.6) | collective-permute-done | bytes 4128 | tf_op jit(solution)/shard_map/ppermute | solution.py:527
  38.4 0.0 collective-permute-start.7
  38.4 1.2 %collective-permute-done.7 = f32[8,128]{1,0:T(8,128)S(1)} collective-permute-done((f32[8,128]{1,0:T(8,128)S(1)}, f32[8,128]{1,0:T(8,128)S(1)}, u32[]{:S(2)}, u32[]{:S(2)}) %collective-permute-start.7) | collective-permute-done | bytes 4128 | tf_op jit(solution)/shard_map/ppermute | solution.py:528
  39.6 0.0 collective-permute-done.8.came_ref
  39.6 3.5 %assemble.1 = (f32[16,4,8,8,128]{4,3,2,1,0:T(8,128)S(1)}, f32[16,4,8,8,128]{4,3,2,1,0:T(8,128)S(1)}, f32[2,4,8,8,128]{4,3,2,1,0:T(8,128)S(1)}, f32[2,4,8,8,128]{...) custom-call(s32[1]{0:T(128)} %bitcast.place_ref, f32[8,128]{1,0:T(8,128)S(1)} %max.31.tile_ref, ...), custom_call_target="tpu_custom_call" | custom-call | flops 1048576 | bytes 6291456 | tf_op jit(solution)/shard_map/assemble/pallas_call | solution.py:530
  43.1 0.1 collective-permute-start.9
  43.2 3.3 %collective-permute-start.10 = (f32[2,4,8,8,128]{4,3,2,1,0:T(8,128)S(1)}, f32[2,4,8,8,128]{4,3,2,1,0:T(8,128)S(1)}, u32[]{:S(2)}, u32[]{:S(2)}) collective-permute-start(f32[2,4,8,8,128]{4,3,2,1,0:T(8,128)S(1)} %get-tuple-element.26), channel_id=1, source_target_pairs={{0,96},{32,0},{64,32},{96,64},{1,97},{33,1},{65,33},{97,65},{2,98}... | collective-permute-start | bytes 786440 | tf_op jit(solution)/shard_map/ppermute | solution.py:493
  46.5 0.0 collective-permute-start.11
  46.5 1.7 %collective-permute-start.12 = (f32[2,2,8,8,128]{4,3,2,1,0:T(8,128)S(1)}, f32[2,2,8,8,128]{4,3,2,1,0:T(8,128)S(1)}, u32[]{:S(2)}, u32[]{:S(2)}) collective-permute-start(f32[2,2,8,8,128]{4,3,2,1,0:T(8,128)S(1)} %get-tuple-element.28), channel_id=1, source_target_pairs={{0,31},{1,2},{2,1},{3,4},{4,3},{5,6},{6,5},{7,8},{8,7},{9,10},{10,... | collective-permute-start | bytes 393224 | tf_op jit(solution)/shard_map/ppermute | solution.py:500
  48.2 7.2 %inner_fluxes.2 = (f32[16,4,8,8,128]{4,3,2,1,0:T(8,128)S(1)}, f32[16,4,8,8,128]{4,3,2,1,0:T(8,128)S(1)}) custom-call(f32[16,4,8,8,128]{4,3,2,1,0:T(8,128)S(1)} %get-tuple-element.21.w_ref), custom_call_target="tpu_custom_call" | custom-call | flops 41943040 | bytes 6291456 | tf_op jit(solution)/shard_map/inner_fluxes/pallas_call | solution.py:543
  55.5 0.0 collective-permute-done.11.yn
  55.5 0.0 collective-permute-done.12.yf
  55.5 0.0 collective-permute-done.9.xl
  55.5 0.0 collective-permute-done.10.xh
  55.5 2.2 %first_stage.1 = (f32[16,4,8,8,128]{4,3,2,1,0:T(8,128)S(1)}, f32[16,4,8,8,128]{4,3,2,1,0:T(8,128)S(1)}, f32[2,4,8,8,128]{4,3,2,1,0:T(8,128)S(1)}, f32[2,4,8,8,12...) custom-call(s32[1]{0:T(128)} %bitcast.place_ref, ...), custom_call_target="tpu_custom_call" | custom-call | flops 1048576 | bytes 6291456 | tf_op jit(solution)/shard_map/first_stage/pallas_call | solution.py:542
  57.7 0.1 collective-permute-start.13
  57.8 3.2 %collective-permute-start.14 = (f32[2,4,8,8,128]{4,3,2,1,0:T(8,128)S(1)}, f32[2,4,8,8,128]{4,3,2,1,0:T(8,128)S(1)}, u32[]{:S(2)}, u32[]{:S(2)}) collective-permute-start(f32[2,4,8,8,128]{4,3,2,1,0:T(8,128)S(1)} %get-tuple-element.34), channel_id=1, source_target_pairs={{0,96},{32,0},{64,32},{96,64},{1,97},{33,1},{65,33},{97,65},{2,98}... | collective-permute-start | bytes 786440 | tf_op jit(solution)/shard_map/ppermute | solution.py:493
  61.0 0.0 collective-permute-start.15
  61.0 2.8 %collective-permute-start.16 = (f32[2,2,8,8,128]{4,3,2,1,0:T(8,128)S(1)}, f32[2,2,8,8,128]{4,3,2,1,0:T(8,128)S(1)}, u32[]{:S(2)}, u32[]{:S(2)}) collective-permute-start(f32[2,2,8,8,128]{4,3,2,1,0:T(8,128)S(1)} %get-tuple-element.36), channel_id=1, source_target_pairs={{0,31},{1,2},{2,1},{3,4},{4,3},{5,6},{6,5},{7,8},{8,7},{9,10},{10,... | collective-permute-start | bytes 393224 | tf_op jit(solution)/shard_map/ppermute | solution.py:500
  63.8 7.2 %inner_fluxes.3 = (f32[16,4,8,8,128]{4,3,2,1,0:T(8,128)S(1)}, f32[16,4,8,8,128]{4,3,2,1,0:T(8,128)S(1)}) custom-call(f32[16,4,8,8,128]{4,3,2,1,0:T(8,128)S(1)} %get-tuple-element.29.w_ref), custom_call_target="tpu_custom_call" | custom-call | flops 41943040 | bytes 6291456 | tf_op jit(solution)/shard_map/inner_fluxes/pallas_call | solution.py:549
  71.1 0.0 collective-permute-done.15.yn
  71.1 0.0 collective-permute-done.16.yf
  71.1 0.0 collective-permute-done.13.xl
  71.1 0.0 collective-permute-done.14.xh
  71.1 3.7 %second_stage.1 = f32[16,32,8,128]{3,2,1,0:T(8,128)} custom-call(s32[1]{0:T(128)} %bitcast.place_ref, f32[8,128]{1,0:T(8,128)S(1)} %max.31.tile_ref, f32[16,4,8,8,128]{4,3,2,1,0:T(8,128)S(1)} %get-tuple-element.29.w_ref, f32[16,4,8,8,128]{4,3,2,1,0:T(8,128)S(1)} %get-tuple-element.30.s_ref, f32[16,4,8,8,128]{4,3,2,1,0:T(8,128)S(1)} %get-tuple-element.31.txz, ...), custom_call_target="tpu_custom_call" | custom-call | flops 1048576 | bytes 6291456 | tf_op jit(solution)/shard_map/second_stage/pallas_call | solution.py:548
  (8 shorter events, 0.0 us)
Async XLA Ops:
  2.4 37.2 %collective-permute-start.8 = (f32[15,32,8,128]{3,2,1,0:T(8,128)S(1)}, f32[15,32,8,128]{3,2,1,0:T(8,128)}, u32[]{:S(2)}, u32[]{:S(2)}) collective-permute-start(f32[15,32,8,128]{3,2,1,0:T(8,128)S(1)} %outgoing.1), channel_id=1, source_target_pairs={{0,1},{1,2},{2,3},{3,4},{4,5},{5,6},{6,7},{7,8},{8,9},{9,10},{10,1... | collective-permute-start | bytes 5898248 | tf_op jit(solution)/shard_map/ppermute | solution.py:513
  7.6 1.3 %collective-permute-start = (f32[8,128]{1,0:T(8,128)S(1)}, f32[8,128]{1,0:T(8,128)S(1)}, u32[]{:S(2)}, u32[]{:S(2)}) collective-permute-start(f32[8,128]{1,0:T(8,128)S(1)} %signal_speed.1), channel_id=1, source_target_pairs={{0,1},{1,0},{2,3},{3,2},{4,5},{5,4},{6,7},{7,6},{8,9},{9,8},{10,11... | collective-permute-start | bytes 12296 | tf_op jit(solution)/shard_map/ppermute | solution.py:525
  8.9 3.6 %collective-permute-start.1 = (f32[8,128]{1,0:T(8,128)S(1)}, f32[8,128]{1,0:T(8,128)S(1)}, u32[]{:S(2)}, u32[]{:S(2)}) collective-permute-start(f32[8,128]{1,0:T(8,128)S(1)} %max.24), channel_id=1, source_target_pairs={{0,2},{1,33},{2,0},{3,35},{4,6},{5,37},{6,4},{7,39},{8,10},{9,41},... | collective-permute-start | bytes 12296 | tf_op jit(solution)/shard_map/ppermute | solution.py:527
  12.5 5.2 %collective-permute-start.2 = (f32[8,128]{1,0:T(8,128)S(1)}, f32[8,128]{1,0:T(8,128)S(1)}, u32[]{:S(2)}, u32[]{:S(2)}) collective-permute-start(f32[8,128]{1,0:T(8,128)S(1)} %max.25), channel_id=1, source_target_pairs={{0,6},{1,97},{2,4},{3,99},{4,2},{5,101},{6,0},{7,103},{8,14},{9,10... | collective-permute-start | bytes 12296 | tf_op jit(solution)/shard_map/ppermute | solution.py:527
  17.8 3.6 %collective-permute-start.3 = (f32[8,128]{1,0:T(8,128)S(1)}, f32[8,128]{1,0:T(8,128)S(1)}, u32[]{:S(2)}, u32[]{:S(2)}) collective-permute-start(f32[8,128]{1,0:T(8,128)S(1)} %max.26), channel_id=1, source_target_pairs={{0,8},{1,33},{2,10},{3,35},{4,12},{5,37},{6,14},{7,39},{8,0},{9,41... | collective-permute-start | bytes 12296 | tf_op jit(solution)/shard_map/ppermute | solution.py:527
  21.4 4.8 %collective-permute-start.4 = (f32[8,128]{1,0:T(8,128)S(1)}, f32[8,128]{1,0:T(8,128)S(1)}, u32[]{:S(2)}, u32[]{:S(2)}) collective-permute-start(f32[8,128]{1,0:T(8,128)S(1)} %max.27), channel_id=1, source_target_pairs={{0,24},{1,97},{2,26},{3,99},{4,28},{5,101},{6,30},{7,103},{8,16},{... | collective-permute-start | bytes 12296 | tf_op jit(solution)/shard_map/ppermute | solution.py:527
  26.2 3.6 %collective-permute-start.5 = (f32[8,128]{1,0:T(8,128)S(1)}, f32[8,128]{1,0:T(8,128)S(1)}, u32[]{:S(2)}, u32[]{:S(2)}) collective-permute-start(f32[8,128]{1,0:T(8,128)S(1)} %max.28), channel_id=1, source_target_pairs={{0,32},{1,33},{2,34},{3,35},{4,36},{5,37},{6,38},{7,39},{8,40},{9,... | collective-permute-start | bytes 12296 | tf_op jit(solution)/shard_map/ppermute | solution.py:527
  29.8 8.6 %collective-permute-start.6 = (f32[8,128]{1,0:T(8,128)S(1)}, f32[8,128]{1,0:T(8,128)S(1)}, u32[]{:S(2)}, u32[]{:S(2)}) collective-permute-start(f32[8,128]{1,0:T(8,128)S(1)} %max.29), channel_id=1, source_target_pairs={{0,96},{1,97},{2,98},{3,99},{4,100},{5,101},{6,102},{7,103},{8,104... | collective-permute-start | bytes 12296 | tf_op jit(solution)/shard_map/ppermute | solution.py:527
  38.4 1.2 %collective-permute-start.7 = (f32[8,128]{1,0:T(8,128)S(1)}, f32[8,128]{1,0:T(8,128)S(1)}, u32[]{:S(2)}, u32[]{:S(2)}) collective-permute-start(f32[8,128]{1,0:T(8,128)S(1)} %max.30), channel_id=1, source_target_pairs={{0,1},{1,0},{2,3},{3,2},{4,5},{5,4},{6,7},{7,6},{8,9},{9,8},{10,11... | collective-permute-start | bytes 12296 | tf_op jit(solution)/shard_map/ppermute | solution.py:528
  43.1 12.4 %collective-permute-start.9 = (f32[2,4,8,8,128]{4,3,2,1,0:T(8,128)S(1)}, f32[2,4,8,8,128]{4,3,2,1,0:T(8,128)S(1)}, u32[]{:S(2)}, u32[]{:S(2)}) collective-permute-start(f32[2,4,8,8,128]{4,3,2,1,0:T(8,128)S(1)} %get-tuple-element.25), channel_id=1, source_target_pairs={{0,32},{32,64},{64,96},{96,0},{1,33},{33,65},{65,97},{97,1},{2,34}... | collective-permute-start | bytes 786440 | tf_op jit(solution)/shard_map/ppermute | solution.py:493
  43.2 12.3 %collective-permute-start.10 = (f32[2,4,8,8,128]{4,3,2,1,0:T(8,128)S(1)}, f32[2,4,8,8,128]{4,3,2,1,0:T(8,128)S(1)}, u32[]{:S(2)}, u32[]{:S(2)}) collective-permute-start(f32[2,4,8,8,128]{4,3,2,1,0:T(8,128)S(1)} %get-tuple-element.26), channel_id=1, source_target_pairs={{0,96},{32,0},{64,32},{96,64},{1,97},{33,1},{65,33},{97,65},{2,98}... | collective-permute-start | bytes 786440 | tf_op jit(solution)/shard_map/ppermute | solution.py:493
  46.5 9.0 %collective-permute-start.11 = (f32[2,2,8,8,128]{4,3,2,1,0:T(8,128)S(1)}, f32[2,2,8,8,128]{4,3,2,1,0:T(8,128)S(1)}, u32[]{:S(2)}, u32[]{:S(2)}) collective-permute-start(f32[2,2,8,8,128]{4,3,2,1,0:T(8,128)S(1)} %get-tuple-element.27), channel_id=1, source_target_pairs={{0,1},{1,0},{2,3},{3,2},{4,5},{5,4},{6,7},{7,6},{8,9},{9,8},{10,11... | collective-permute-start | bytes 393224 | tf_op jit(solution)/shard_map/ppermute | solution.py:500
  46.5 9.0 %collective-permute-start.12 = (f32[2,2,8,8,128]{4,3,2,1,0:T(8,128)S(1)}, f32[2,2,8,8,128]{4,3,2,1,0:T(8,128)S(1)}, u32[]{:S(2)}, u32[]{:S(2)}) collective-permute-start(f32[2,2,8,8,128]{4,3,2,1,0:T(8,128)S(1)} %get-tuple-element.28), channel_id=1, source_target_pairs={{0,31},{1,2},{2,1},{3,4},{4,3},{5,6},{6,5},{7,8},{8,7},{9,10},{10,... | collective-permute-start | bytes 393224 | tf_op jit(solution)/shard_map/ppermute | solution.py:500
  57.7 13.4 %collective-permute-start.13 = (f32[2,4,8,8,128]{4,3,2,1,0:T(8,128)S(1)}, f32[2,4,8,8,128]{4,3,2,1,0:T(8,128)S(1)}, u32[]{:S(2)}, u32[]{:S(2)}) collective-permute-start(f32[2,4,8,8,128]{4,3,2,1,0:T(8,128)S(1)} %get-tuple-element.33), channel_id=1, source_target_pairs={{0,32},{32,64},{64,96},{96,0},{1,33},{33,65},{65,97},{97,1},{2,34}... | collective-permute-start | bytes 786440 | tf_op jit(solution)/shard_map/ppermute | solution.py:493
  57.8 13.3 %collective-permute-start.14 = (f32[2,4,8,8,128]{4,3,2,1,0:T(8,128)S(1)}, f32[2,4,8,8,128]{4,3,2,1,0:T(8,128)S(1)}, u32[]{:S(2)}, u32[]{:S(2)}) collective-permute-start(f32[2,4,8,8,128]{4,3,2,1,0:T(8,128)S(1)} %get-tuple-element.34), channel_id=1, source_target_pairs={{0,96},{32,0},{64,32},{96,64},{1,97},{33,1},{65,33},{97,65},{2,98}... | collective-permute-start | bytes 786440 | tf_op jit(solution)/shard_map/ppermute | solution.py:493
  61.0 10.0 %collective-permute-start.15 = (f32[2,2,8,8,128]{4,3,2,1,0:T(8,128)S(1)}, f32[2,2,8,8,128]{4,3,2,1,0:T(8,128)S(1)}, u32[]{:S(2)}, u32[]{:S(2)}) collective-permute-start(f32[2,2,8,8,128]{4,3,2,1,0:T(8,128)S(1)} %get-tuple-element.35), channel_id=1, source_target_pairs={{0,1},{1,0},{2,3},{3,2},{4,5},{5,4},{6,7},{7,6},{8,9},{9,8},{10,11... | collective-permute-start | bytes 393224 | tf_op jit(solution)/shard_map/ppermute | solution.py:500
  61.0 10.0 %collective-permute-start.16 = (f32[2,2,8,8,128]{4,3,2,1,0:T(8,128)S(1)}, f32[2,2,8,8,128]{4,3,2,1,0:T(8,128)S(1)}, u32[]{:S(2)}, u32[]{:S(2)}) collective-permute-start(f32[2,2,8,8,128]{4,3,2,1,0:T(8,128)S(1)} %get-tuple-element.36), channel_id=1, source_target_pairs={{0,31},{1,2},{2,1},{3,4},{4,3},{5,6},{6,5},{7,8},{8,7},{9,10},{10,... | collective-permute-start | bytes 393224 | tf_op jit(solution)/shard_map/ppermute | solution.py:500

commit v5 on v4

--- a/solution.py
+++ b/solution.py
@@ -112,7 +112,7 @@
 def edges(prims, backward, forward):
     upper, lower = [], []
     for w, a, b in zip(prims, backward, forward):
-        half = 0.5 * jnp.maximum(jnp.minimum(a, b), jnp.minimum(jnp.maximum(a, b), 0.0))
+        half = jnp.maximum(jnp.minimum(a, b), jnp.minimum(jnp.maximum(a, b), 0.0))
         upper.append(w + half)
         lower.append(w - half)
     return upper, lower
@@ -255,11 +255,11 @@
             put(w_ref, x, t, primitive(state))
             return 0
 
-        lax.fori_loop(0, CHUNKS, chunk, 0, unroll=16)
+        lax.fori_loop(0, CHUNKS, chunk, 0, unroll=32)
     pack_sides(place % 2, w_ref, xl_ref, xh_ref, yn_ref, yf_ref)
 
 
-def inner_kernel(w_ref, xz_ref, y_ref, next_ref, prior_ref, flux_ref):
+def inner_kernel(w_ref, xz_ref, y_ref, half_ref, next_ref, prior_ref, flux_ref):
     row = iota(0)
     last, first = row == 7, row == 0
 
@@ -275,10 +275,12 @@
 
     def along_y(x, _):
         prims = [cells(w_ref, x, t) for t in range(TS)]
+        halves = [[0.5 * v for v in w] for w in prims]
         for t in range(TS):
-            put(next_ref, x, t, [pltpu.roll(v, 127, 1) for v in prims[t]])
-            put(prior_ref, x, t, [pltpu.roll(v, 1, 1) for v in prims[t]])
-        forward = [minus(a, w) for a, w in zip(ahead(prims), prims)]
+            put(half_ref, x, t, halves[t])
+            put(next_ref, x, t, [pltpu.roll(v, 127, 1) for v in halves[t]])
+            put(prior_ref, x, t, [pltpu.roll(v, 1, 1) for v in halves[t]])
+        forward = [minus(a, w) for a, w in zip(ahead(halves), halves)]
         backward = behind(forward)
         both = [edges(w, b, f) for w, b, f in zip(prims, backward, forward)]
         right = ahead([lower for _, lower in both])
@@ -294,16 +296,16 @@
             put(y_ref, x, t, minus(before, flux[t]))
         return 0
 
-    lax.fori_loop(0, XS, along_y, 0, unroll=2)
+    lax.fori_loop(0, XS, along_y, 0, unroll=4)
 
     def along_z(i, _):
         x, t = i // TS, i % TS
-        w = cells(w_ref, x, t)
-        upper, lower = edges(w, minus(w, cells(prior_ref, x, t)), minus(cells(next_ref, x, t), w))
+        half = cells(half_ref, x, t)
+        upper, lower = edges(cells(w_ref, x, t), minus(half, cells(prior_ref, x, t)), minus(cells(next_ref, x, t), half))
         put(flux_ref, x, t, hlle(upper, [pltpu.roll(v, 127, 1) for v in lower], 2))
         return 0
 
-    lax.fori_loop(0, XS * TS, along_z, 0, unroll=8)
+    lax.fori_loop(0, XS * TS, along_z, 0, unroll=16)
 
     def along_x(pair, _):
         both = (2 * pair, 2 * pair + 1)
@@ -314,10 +316,10 @@
 
         start = []
         for t in both:
-            w0, w1, w2, w3 = [cells(w_ref, x, t) for x in range(4)]
-            d1, d2 = minus(w2, w1), minus(w3, w2)
-            upper, _ = edges(w1, minus(w1, w0), d1)
-            after, lower = edges(w2, d1, d2)
+            h0, h1, h2, h3 = [cells(half_ref, x, t) for x in range(4)]
+            d1, d2 = minus(h2, h1), minus(h3, h2)
+            upper, _ = edges(cells(w_ref, 1, t), minus(h1, h0), d1)
+            after, lower = edges(cells(w_ref, 2, t), d1, d2)
             flux = hlle(upper, lower, 0)
             store(0, t)
             store(1, t, [-v for v in flux])
@@ -326,15 +328,14 @@
         def step(x, carry):
             result = []
             for t, (d, upper, flux) in zip(both, carry):
-                here, beyond = cells(w_ref, x + 1, t), cells(w_ref, x + 2, t)
-                forward = minus(beyond, here)
-                after, lower = edges(here, d, forward)
+                forward = minus(cells(half_ref, x + 2, t), cells(half_ref, x + 1, t))
+                after, lower = edges(cells(w_ref, x + 1, t), d, forward)
                 new = hlle(upper, lower, 0)
                 store(x, t, minus(flux, new))
                 result.append((forward, after, new))
             return result
 
-        for t, (_, _, flux) in zip(both, lax.fori_loop(2, 14, step, start, unroll=3)):
+        for t, (_, _, flux) in zip(both, lax.fori_loop(2, 14, step, start, unroll=12)):
             store(14, t, flux)
             store(15, t)
         return 0
@@ -343,7 +344,7 @@
 
 
 def outer_faces(six, normal):
-    ds = [minus(six[i + 1], six[i]) for i in range(len(six) - 1)]
+    ds = [[0.5 * v for v in minus(six[i + 1], six[i])] for i in range(len(six) - 1)]
     both = [edges(six[i + 1], ds[i], ds[i + 1]) for i in range(len(six) - 2)]
     return [hlle(both[i][0], both[i + 1][1], normal) for i in range(len(six) - 3)]
 
@@ -403,7 +404,7 @@
 def each_layer(work):
     for edge, x in enumerate((0, 1, XS - 2, XS - 1)):
         work(x, edge)
-    lax.fori_loop(2, XS - 2, lambda x, _: (work(x, None), 0)[1], 0, unroll=4)
+    lax.fori_loop(2, XS - 2, lambda x, _: (work(x, None), 0)[1], 0, unroll=12)
 
 
 def step_of(tile_ref):
@@ -446,13 +447,12 @@
         return pltpu.make_async_copy(blocks.at[:, chunks], out_ref.at[:, chunks], sems.at[quarter])
 
     def pairs(first, last):
-        lax.fori_loop(first, last, lambda x, _: (work(x, None), 0)[1], 0, unroll=min(4, last - first))
+        lax.fori_loop(first, last, lambda x, _: (work(x, None), 0)[1], 0, unroll=last - first)
 
     work(0, 0)
     work(1, 1)
-    pairs(2, 4)
+    pairs(2, 8)
     part(0).start()
-    pairs(4, 8)
     part(1).start()
     pairs(8, 12)
     part(2).start()
@@ -536,7 +536,7 @@
         1 << 20,
     )(place, tile, pltpu.with_memory_space_constraint(came, pltpu.HBM), there)
     corrections = [pltpu.VMEM((4, TS, FIELDS, 8, 128), jnp.float32), pltpu.VMEM((XS, 2, FIELDS, 8, 128), jnp.float32)]
-    inner = kernel(inner_kernel, [VMEM], [GRID] * 2, [pltpu.VMEM(GRID, jnp.float32)] * 3, "inner_fluxes", 40 << 20)
+    inner = kernel(inner_kernel, [VMEM], [GRID] * 2, [pltpu.VMEM(GRID, jnp.float32)] * 4, "inner_fluxes", 40 << 20)
     specs = [SMEM] + [VMEM] * 9
     ghosts = exchanged(*faces)
     s, w2, *faces = kernel(first_kernel, specs, [GRID, GRID] + sides, corrections, "first_stage", 1 << 20)(

time: 75.2 us -> 73.2 us (0.973)
  Pallas kernels: 28.3 us -> 26 us
  waiting for transfers between devices: 13.7 us -> 15.6 us
  starting transfers between devices: 32 us -> 30.4 us
    ppermute x6, starting transfers between devices: 17.8 us -> 15.2 us  [body(): lax.ppermute(tile, AXES, [(i, i ^ masks[i % 2]) for i in range(devices)])]
    ppermute x6, waiting for transfers between devices: 11.7 us -> 13.5 us  [body(): lax.ppermute(tile, AXES, [(i, i ^ masks[i % 2]) for i in range(devices)])]
    ppermute x2, starting transfers between devices: 0.47 us -> 1.38 us  [body(): lax.ppermute(tile, AXES, [(i, i ^ 1) for i in range(devices)])]
  transfers between devices with their start and end apart: 17 -> 17, of which waited for: 8 -> 8; matrix products, arithmetic and copies ran while one was open for 0% -> 0% of each run, Pallas kernels for 23% -> 21%
where the time goes in v5:
time: 73.2 us; the launch traced here: 72.9 us
  starting transfers between devices  30.4 us (42%)
  Pallas kernels  26 us (36%)
  waiting for transfers between devices  15.6 us (21%)
  between operations  0.95 us (1%)
    ppermute x6, starting transfers between devices, body(): lax.ppermute(tile, AXES, [(i, i ^ masks[i % 2]) for i in range(devices)])  15.2 us
    ppermute x6, waiting for transfers between devices, body(): lax.ppermute(tile, AXES, [(i, i ^ masks[i % 2]) for i in range(devices)])  13.5 us
    ppermute x4, starting transfers between devices, shifted(): lax.ppermute(value, axis, [(i, (i + by) % count) for i in range(count)])  6.68 us
    pallas_call x1, Pallas kernels, body(): inner(w2)  6.58 us
    pallas_call x1, Pallas kernels, body(): inner(w)  6.58 us
    ppermute x2, starting transfers between devices, exchanged(): lax.ppermute(yf, 'dev', far)  4.51 us
    pallas_call x1, Pallas kernels, body(): kernel(second_kernel, specs, result, buffers, 'second_stage', 1 << 20, ou...  3.7 us
    pallas_call x1, Pallas kernels, body(): kernel(assemble_kernel, [SMEM, VMEM, ANY, ANY], [GRID, GRID] + sides, [pl...  3.19 us
  transfers between devices with their start and end apart: 17, of which 8 were waited for; matrix products, arithmetic and copies ran while one was open for 0% of the time, Pallas kernels for 21%

profile of v5, /device:TPU:0, one launch (start us, length us, event | category | flops | bytes accessed | tf_op | source)
XLA Modules:
  0.0 72.9 jit_solution(1727638748600309143)
XLA Ops:
  0.7 1.7 %outgoing.1 = f32[15,32,8,128]{3,2,1,0:T(8,128)S(1)} custom-call(s32[1]{0:T(128)S(6)} %copy.3.count_ref, f32[31,32,8,128]{3,2,1,0:T(8,128)} %bitcast.7), custom_call_target="tpu_custom_call" | custom-call | flops 1024 | bytes 6291456 | tf_op jit(solution)/shard_map/outgoing/pallas_call | solution.py:510
  2.4 2.6 %collective-permute-start.8 = (f32[15,32,8,128]{3,2,1,0:T(8,128)S(1)}, f32[15,32,8,128]{3,2,1,0:T(8,128)}, u32[]{:S(2)}, u32[]{:S(2)}) collective-permute-start(f32[15,32,8,128]{3,2,1,0:T(8,128)S(1)} %outgoing.1), channel_id=1, source_target_pairs={{0,1},{1,2},{2,3},{3,4},{4,5},{5,6},{6,7},{7,8},{8,9},{9,10},{10,1... | collective-permute-start | bytes 5898248 | tf_op jit(solution)/shard_map/ppermute | solution.py:513
  5.0 2.1 %signal_speed.1 = f32[8,128]{1,0:T(8,128)S(1)} custom-call(s32[1]{0:T(128)S(6)} %copy.3.count_ref, s32[1]{0:T(128)} %bitcast.place_ref, f32[31,32,8,128]{3,2,1,0:T(8,128)} %bitcast.8), custom_call_target="tpu_custom_call" | custom-call | flops 1048576 | bytes 6291456 | tf_op jit(solution)/shard_map/signal_speed/pallas_call | solution.py:514
  7.1 1.4 %collective-permute-start = (f32[8,128]{1,0:T(8,128)S(1)}, f32[8,128]{1,0:T(8,128)S(1)}, u32[]{:S(2)}, u32[]{:S(2)}) collective-permute-start(f32[8,128]{1,0:T(8,128)S(1)} %signal_speed.1), channel_id=1, source_target_pairs={{0,1},{1,0},{2,3},{3,2},{4,5},{5,4},{6,7},{7,6},{8,9},{9,8},{10,11... | collective-permute-start | bytes 12296 | tf_op jit(solution)/shard_map/ppermute | solution.py:525
  8.5 0.8 %collective-permute-done = f32[8,128]{1,0:T(8,128)S(1)} collective-permute-done((f32[8,128]{1,0:T(8,128)S(1)}, f32[8,128]{1,0:T(8,128)S(1)}, u32[]{:S(2)}, u32[]{:S(2)}) %collective-permute-start) | collective-permute-done | bytes 4128 | tf_op jit(solution)/shard_map/ppermute | solution.py:525
  9.3 1.6 %collective-permute-start.1 = (f32[8,128]{1,0:T(8,128)S(1)}, f32[8,128]{1,0:T(8,128)S(1)}, u32[]{:S(2)}, u32[]{:S(2)}) collective-permute-start(f32[8,128]{1,0:T(8,128)S(1)} %max.24), channel_id=1, source_target_pairs={{0,2},{1,33},{2,0},{3,35},{4,6},{5,37},{6,4},{7,39},{8,10},{9,41},... | collective-permute-start | bytes 12296 | tf_op jit(solution)/shard_map/ppermute | solution.py:527
  10.9 2.0 %collective-permute-done.1 = f32[8,128]{1,0:T(8,128)S(1)} collective-permute-done((f32[8,128]{1,0:T(8,128)S(1)}, f32[8,128]{1,0:T(8,128)S(1)}, u32[]{:S(2)}, u32[]{:S(2)}) %collective-permute-start.1) | collective-permute-done | bytes 4128 | tf_op jit(solution)/shard_map/ppermute | solution.py:527
  12.9 2.2 %collective-permute-start.2 = (f32[8,128]{1,0:T(8,128)S(1)}, f32[8,128]{1,0:T(8,128)S(1)}, u32[]{:S(2)}, u32[]{:S(2)}) collective-permute-start(f32[8,128]{1,0:T(8,128)S(1)} %max.25), channel_id=1, source_target_pairs={{0,6},{1,97},{2,4},{3,99},{4,2},{5,101},{6,0},{7,103},{8,14},{9,10... | collective-permute-start | bytes 12296 | tf_op jit(solution)/shard_map/ppermute | solution.py:527
  15.1 3.0 %collective-permute-done.2 = f32[8,128]{1,0:T(8,128)S(1)} collective-permute-done((f32[8,128]{1,0:T(8,128)S(1)}, f32[8,128]{1,0:T(8,128)S(1)}, u32[]{:S(2)}, u32[]{:S(2)}) %collective-permute-start.2) | collective-permute-done | bytes 4128 | tf_op jit(solution)/shard_map/ppermute | solution.py:527
  18.1 1.5 %collective-permute-start.3 = (f32[8,128]{1,0:T(8,128)S(1)}, f32[8,128]{1,0:T(8,128)S(1)}, u32[]{:S(2)}, u32[]{:S(2)}) collective-permute-start(f32[8,128]{1,0:T(8,128)S(1)} %max.26), channel_id=1, source_target_pairs={{0,8},{1,33},{2,10},{3,35},{4,12},{5,37},{6,14},{7,39},{8,0},{9,41... | collective-permute-start | bytes 12296 | tf_op jit(solution)/shard_map/ppermute | solution.py:527
  19.6 2.1 %collective-permute-done.3 = f32[8,128]{1,0:T(8,128)S(1)} collective-permute-done((f32[8,128]{1,0:T(8,128)S(1)}, f32[8,128]{1,0:T(8,128)S(1)}, u32[]{:S(2)}, u32[]{:S(2)}) %collective-permute-start.3) | collective-permute-done | bytes 4128 | tf_op jit(solution)/shard_map/ppermute | solution.py:527
  21.7 2.2 %collective-permute-start.4 = (f32[8,128]{1,0:T(8,128)S(1)}, f32[8,128]{1,0:T(8,128)S(1)}, u32[]{:S(2)}, u32[]{:S(2)}) collective-permute-start(f32[8,128]{1,0:T(8,128)S(1)} %max.27), channel_id=1, source_target_pairs={{0,24},{1,97},{2,26},{3,99},{4,28},{5,101},{6,30},{7,103},{8,16},{... | collective-permute-start | bytes 12296 | tf_op jit(solution)/shard_map/ppermute | solution.py:527
  23.9 2.6 %collective-permute-done.4 = f32[8,128]{1,0:T(8,128)S(1)} collective-permute-done((f32[8,128]{1,0:T(8,128)S(1)}, f32[8,128]{1,0:T(8,128)S(1)}, u32[]{:S(2)}, u32[]{:S(2)}) %collective-permute-start.4) | collective-permute-done | bytes 4128 | tf_op jit(solution)/shard_map/ppermute | solution.py:527
  26.6 1.4 %collective-permute-start.5 = (f32[8,128]{1,0:T(8,128)S(1)}, f32[8,128]{1,0:T(8,128)S(1)}, u32[]{:S(2)}, u32[]{:S(2)}) collective-permute-start(f32[8,128]{1,0:T(8,128)S(1)} %max.28), channel_id=1, source_target_pairs={{0,32},{1,33},{2,34},{3,35},{4,36},{5,37},{6,38},{7,39},{8,40},{9,... | collective-permute-start | bytes 12296 | tf_op jit(solution)/shard_map/ppermute | solution.py:527
  27.9 2.2 %collective-permute-done.5 = f32[8,128]{1,0:T(8,128)S(1)} collective-permute-done((f32[8,128]{1,0:T(8,128)S(1)}, f32[8,128]{1,0:T(8,128)S(1)}, u32[]{:S(2)}, u32[]{:S(2)}) %collective-permute-start.5) | collective-permute-done | bytes 4128 | tf_op jit(solution)/shard_map/ppermute | solution.py:527
  30.2 6.3 %collective-permute-start.6 = (f32[8,128]{1,0:T(8,128)S(1)}, f32[8,128]{1,0:T(8,128)S(1)}, u32[]{:S(2)}, u32[]{:S(2)}) collective-permute-start(f32[8,128]{1,0:T(8,128)S(1)} %max.29), channel_id=1, source_target_pairs={{0,96},{1,97},{2,98},{3,99},{4,100},{5,101},{6,102},{7,103},{8,104... | collective-permute-start | bytes 12296 | tf_op jit(solution)/shard_map/ppermute | solution.py:527
  36.5 1.6 %collective-permute-done.6 = f32[8,128]{1,0:T(8,128)S(1)} collective-permute-done((f32[8,128]{1,0:T(8,128)S(1)}, f32[8,128]{1,0:T(8,128)S(1)}, u32[]{:S(2)}, u32[]{:S(2)}) %collective-permute-start.6) | collective-permute-done | bytes 4128 | tf_op jit(solution)/shard_map/ppermute | solution.py:527
  38.1 0.0 collective-permute-start.7
  38.1 1.2 %collective-permute-done.7 = f32[8,128]{1,0:T(8,128)S(1)} collective-permute-done((f32[8,128]{1,0:T(8,128)S(1)}, f32[8,128]{1,0:T(8,128)S(1)}, u32[]{:S(2)}, u32[]{:S(2)}) %collective-permute-start.7) | collective-permute-done | bytes 4128 | tf_op jit(solution)/shard_map/ppermute | solution.py:528
  39.2 0.0 collective-permute-done.8.came_ref
  39.2 3.2 %assemble.1 = (f32[16,4,8,8,128]{4,3,2,1,0:T(8,128)S(1)}, f32[16,4,8,8,128]{4,3,2,1,0:T(8,128)S(1)}, f32[2,4,8,8,128]{4,3,2,1,0:T(8,128)S(1)}, f32[2,4,8,8,128]{...) custom-call(s32[1]{0:T(128)} %bitcast.place_ref, f32[8,128]{1,0:T(8,128)S(1)} %max.31.tile_ref, ...), custom_call_target="tpu_custom_call" | custom-call | flops 1048576 | bytes 6291456 | tf_op jit(solution)/shard_map/assemble/pallas_call | solution.py:530
  42.4 0.3 collective-permute-start.9
  42.8 3.0 %collective-permute-start.10 = (f32[2,4,8,8,128]{4,3,2,1,0:T(8,128)S(1)}, f32[2,4,8,8,128]{4,3,2,1,0:T(8,128)S(1)}, u32[]{:S(2)}, u32[]{:S(2)}) collective-permute-start(f32[2,4,8,8,128]{4,3,2,1,0:T(8,128)S(1)} %get-tuple-element.26), channel_id=1, source_target_pairs={{0,96},{32,0},{64,32},{96,64},{1,97},{33,1},{65,33},{97,65},{2,98}... | collective-permute-start | bytes 786440 | tf_op jit(solution)/shard_map/ppermute | solution.py:493
  45.8 0.0 collective-permute-start.11
  45.8 1.7 %collective-permute-start.12 = (f32[2,2,8,8,128]{4,3,2,1,0:T(8,128)S(1)}, f32[2,2,8,8,128]{4,3,2,1,0:T(8,128)S(1)}, u32[]{:S(2)}, u32[]{:S(2)}) collective-permute-start(f32[2,2,8,8,128]{4,3,2,1,0:T(8,128)S(1)} %get-tuple-element.28), channel_id=1, source_target_pairs={{0,31},{1,2},{2,1},{3,4},{4,3},{5,6},{6,5},{7,8},{8,7},{9,10},{10,... | collective-permute-start | bytes 393224 | tf_op jit(solution)/shard_map/ppermute | solution.py:500
  47.5 6.6 %inner_fluxes.2 = (f32[16,4,8,8,128]{4,3,2,1,0:T(8,128)S(1)}, f32[16,4,8,8,128]{4,3,2,1,0:T(8,128)S(1)}) custom-call(f32[16,4,8,8,128]{4,3,2,1,0:T(8,128)S(1)} %get-tuple-element.21.w_ref), custom_call_target="tpu_custom_call" | custom-call | flops 41943040 | bytes 6291456 | tf_op jit(solution)/shard_map/inner_fluxes/pallas_call | solution.py:543
  54.1 0.0 collective-permute-done.11.yn
  54.1 0.0 collective-permute-done.12.yf
  54.1 0.0 collective-permute-done.9.xl
  54.1 0.0 collective-permute-done.10.xh
  54.1 2.1 %first_stage.1 = (f32[16,4,8,8,128]{4,3,2,1,0:T(8,128)S(1)}, f32[16,4,8,8,128]{4,3,2,1,0:T(8,128)S(1)}, f32[2,4,8,8,128]{4,3,2,1,0:T(8,128)S(1)}, f32[2,4,8,8,12...) custom-call(s32[1]{0:T(128)} %bitcast.place_ref, ...), custom_call_target="tpu_custom_call" | custom-call | flops 1048576 | bytes 6291456 | tf_op jit(solution)/shard_map/first_stage/pallas_call | solution.py:542
  56.2 0.1 collective-permute-start.13
  56.3 3.2 %collective-permute-start.14 = (f32[2,4,8,8,128]{4,3,2,1,0:T(8,128)S(1)}, f32[2,4,8,8,128]{4,3,2,1,0:T(8,128)S(1)}, u32[]{:S(2)}, u32[]{:S(2)}) collective-permute-start(f32[2,4,8,8,128]{4,3,2,1,0:T(8,128)S(1)} %get-tuple-element.34), channel_id=1, source_target_pairs={{0,96},{32,0},{64,32},{96,64},{1,97},{33,1},{65,33},{97,65},{2,98}... | collective-permute-start | bytes 786440 | tf_op jit(solution)/shard_map/ppermute | solution.py:493
  59.5 0.0 collective-permute-start.15
  59.5 2.8 %collective-permute-start.16 = (f32[2,2,8,8,128]{4,3,2,1,0:T(8,128)S(1)}, f32[2,2,8,8,128]{4,3,2,1,0:T(8,128)S(1)}, u32[]{:S(2)}, u32[]{:S(2)}) collective-permute-start(f32[2,2,8,8,128]{4,3,2,1,0:T(8,128)S(1)} %get-tuple-element.36), channel_id=1, source_target_pairs={{0,31},{1,2},{2,1},{3,4},{4,3},{5,6},{6,5},{7,8},{8,7},{9,10},{10,... | collective-permute-start | bytes 393224 | tf_op jit(solution)/shard_map/ppermute | solution.py:500
  62.4 6.6 %inner_fluxes.3 = (f32[16,4,8,8,128]{4,3,2,1,0:T(8,128)S(1)}, f32[16,4,8,8,128]{4,3,2,1,0:T(8,128)S(1)}) custom-call(f32[16,4,8,8,128]{4,3,2,1,0:T(8,128)S(1)} %get-tuple-element.29.w_ref), custom_call_target="tpu_custom_call" | custom-call | flops 41943040 | bytes 6291456 | tf_op jit(solution)/shard_map/inner_fluxes/pallas_call | solution.py:549
  69.0 0.0 collective-permute-done.15.yn
  69.0 0.0 collective-permute-done.16.yf
  69.0 0.0 collective-permute-done.13.xl
  69.0 0.0 collective-permute-done.14.xh
  69.0 3.7 %second_stage.1 = f32[16,32,8,128]{3,2,1,0:T(8,128)} custom-call(s32[1]{0:T(128)} %bitcast.place_ref, f32[8,128]{1,0:T(8,128)S(1)} %max.31.tile_ref, f32[16,4,8,8,128]{4,3,2,1,0:T(8,128)S(1)} %get-tuple-element.29.w_ref, f32[16,4,8,8,128]{4,3,2,1,0:T(8,128)S(1)} %get-tuple-element.30.s_ref, f32[16,4,8,8,128]{4,3,2,1,0:T(8,128)S(1)} %get-tuple-element.31.txz, ...), custom_call_target="tpu_custom_call" | custom-call | flops 1048576 | bytes 6291456 | tf_op jit(solution)/shard_map/second_stage/pallas_call | solution.py:548
  (8 shorter events, 0.0 us)
Async XLA Ops:
  2.4 36.9 %collective-permute-start.8 = (f32[15,32,8,128]{3,2,1,0:T(8,128)S(1)}, f32[15,32,8,128]{3,2,1,0:T(8,128)}, u32[]{:S(2)}, u32[]{:S(2)}) collective-permute-start(f32[15,32,8,128]{3,2,1,0:T(8,128)S(1)} %outgoing.1), channel_id=1, source_target_pairs={{0,1},{1,2},{2,3},{3,4},{4,5},{5,6},{6,7},{7,8},{8,9},{9,10},{10,1... | collective-permute-start | bytes 5898248 | tf_op jit(solution)/shard_map/ppermute | solution.py:513
  7.1 2.2 %collective-permute-start = (f32[8,128]{1,0:T(8,128)S(1)}, f32[8,128]{1,0:T(8,128)S(1)}, u32[]{:S(2)}, u32[]{:S(2)}) collective-permute-start(f32[8,128]{1,0:T(8,128)S(1)} %signal_speed.1), channel_id=1, source_target_pairs={{0,1},{1,0},{2,3},{3,2},{4,5},{5,4},{6,7},{7,6},{8,9},{9,8},{10,11... | collective-permute-start | bytes 12296 | tf_op jit(solution)/shard_map/ppermute | solution.py:525
  9.3 3.6 %collective-permute-start.1 = (f32[8,128]{1,0:T(8,128)S(1)}, f32[8,128]{1,0:T(8,128)S(1)}, u32[]{:S(2)}, u32[]{:S(2)}) collective-permute-start(f32[8,128]{1,0:T(8,128)S(1)} %max.24), channel_id=1, source_target_pairs={{0,2},{1,33},{2,0},{3,35},{4,6},{5,37},{6,4},{7,39},{8,10},{9,41},... | collective-permute-start | bytes 12296 | tf_op jit(solution)/shard_map/ppermute | solution.py:527
  12.9 5.2 %collective-permute-start.2 = (f32[8,128]{1,0:T(8,128)S(1)}, f32[8,128]{1,0:T(8,128)S(1)}, u32[]{:S(2)}, u32[]{:S(2)}) collective-permute-start(f32[8,128]{1,0:T(8,128)S(1)} %max.25), channel_id=1, source_target_pairs={{0,6},{1,97},{2,4},{3,99},{4,2},{5,101},{6,0},{7,103},{8,14},{9,10... | collective-permute-start | bytes 12296 | tf_op jit(solution)/shard_map/ppermute | solution.py:527
  18.1 3.6 %collective-permute-start.3 = (f32[8,128]{1,0:T(8,128)S(1)}, f32[8,128]{1,0:T(8,128)S(1)}, u32[]{:S(2)}, u32[]{:S(2)}) collective-permute-start(f32[8,128]{1,0:T(8,128)S(1)} %max.26), channel_id=1, source_target_pairs={{0,8},{1,33},{2,10},{3,35},{4,12},{5,37},{6,14},{7,39},{8,0},{9,41... | collective-permute-start | bytes 12296 | tf_op jit(solution)/shard_map/ppermute | solution.py:527
  21.7 4.8 %collective-permute-start.4 = (f32[8,128]{1,0:T(8,128)S(1)}, f32[8,128]{1,0:T(8,128)S(1)}, u32[]{:S(2)}, u32[]{:S(2)}) collective-permute-start(f32[8,128]{1,0:T(8,128)S(1)} %max.27), channel_id=1, source_target_pairs={{0,24},{1,97},{2,26},{3,99},{4,28},{5,101},{6,30},{7,103},{8,16},{... | collective-permute-start | bytes 12296 | tf_op jit(solution)/shard_map/ppermute | solution.py:527
  26.6 3.6 %collective-permute-start.5 = (f32[8,128]{1,0:T(8,128)S(1)}, f32[8,128]{1,0:T(8,128)S(1)}, u32[]{:S(2)}, u32[]{:S(2)}) collective-permute-start(f32[8,128]{1,0:T(8,128)S(1)} %max.28), channel_id=1, source_target_pairs={{0,32},{1,33},{2,34},{3,35},{4,36},{5,37},{6,38},{7,39},{8,40},{9,... | collective-permute-start | bytes 12296 | tf_op jit(solution)/shard_map/ppermute | solution.py:527
  30.2 7.9 %collective-permute-start.6 = (f32[8,128]{1,0:T(8,128)S(1)}, f32[8,128]{1,0:T(8,128)S(1)}, u32[]{:S(2)}, u32[]{:S(2)}) collective-permute-start(f32[8,128]{1,0:T(8,128)S(1)} %max.29), channel_id=1, source_target_pairs={{0,96},{1,97},{2,98},{3,99},{4,100},{5,101},{6,102},{7,103},{8,104... | collective-permute-start | bytes 12296 | tf_op jit(solution)/shard_map/ppermute | solution.py:527
  38.1 1.2 %collective-permute-start.7 = (f32[8,128]{1,0:T(8,128)S(1)}, f32[8,128]{1,0:T(8,128)S(1)}, u32[]{:S(2)}, u32[]{:S(2)}) collective-permute-start(f32[8,128]{1,0:T(8,128)S(1)} %max.30), channel_id=1, source_target_pairs={{0,1},{1,0},{2,3},{3,2},{4,5},{5,4},{6,7},{7,6},{8,9},{9,8},{10,11... | collective-permute-start | bytes 12296 | tf_op jit(solution)/shard_map/ppermute | solution.py:528
  42.4 11.7 %collective-permute-start.9 = (f32[2,4,8,8,128]{4,3,2,1,0:T(8,128)S(1)}, f32[2,4,8,8,128]{4,3,2,1,0:T(8,128)S(1)}, u32[]{:S(2)}, u32[]{:S(2)}) collective-permute-start(f32[2,4,8,8,128]{4,3,2,1,0:T(8,128)S(1)} %get-tuple-element.25), channel_id=1, source_target_pairs={{0,32},{32,64},{64,96},{96,0},{1,33},{33,65},{65,97},{97,1},{2,34}... | collective-permute-start | bytes 786440 | tf_op jit(solution)/shard_map/ppermute | solution.py:493
  42.8 11.3 %collective-permute-start.10 = (f32[2,4,8,8,128]{4,3,2,1,0:T(8,128)S(1)}, f32[2,4,8,8,128]{4,3,2,1,0:T(8,128)S(1)}, u32[]{:S(2)}, u32[]{:S(2)}) collective-permute-start(f32[2,4,8,8,128]{4,3,2,1,0:T(8,128)S(1)} %get-tuple-element.26), channel_id=1, source_target_pairs={{0,96},{32,0},{64,32},{96,64},{1,97},{33,1},{65,33},{97,65},{2,98}... | collective-permute-start | bytes 786440 | tf_op jit(solution)/shard_map/ppermute | solution.py:493
  45.8 8.3 %collective-permute-start.11 = (f32[2,2,8,8,128]{4,3,2,1,0:T(8,128)S(1)}, f32[2,2,8,8,128]{4,3,2,1,0:T(8,128)S(1)}, u32[]{:S(2)}, u32[]{:S(2)}) collective-permute-start(f32[2,2,8,8,128]{4,3,2,1,0:T(8,128)S(1)} %get-tuple-element.27), channel_id=1, source_target_pairs={{0,1},{1,0},{2,3},{3,2},{4,5},{5,4},{6,7},{7,6},{8,9},{9,8},{10,11... | collective-permute-start | bytes 393224 | tf_op jit(solution)/shard_map/ppermute | solution.py:500
  45.8 8.3 %collective-permute-start.12 = (f32[2,2,8,8,128]{4,3,2,1,0:T(8,128)S(1)}, f32[2,2,8,8,128]{4,3,2,1,0:T(8,128)S(1)}, u32[]{:S(2)}, u32[]{:S(2)}) collective-permute-start(f32[2,2,8,8,128]{4,3,2,1,0:T(8,128)S(1)} %get-tuple-element.28), channel_id=1, source_target_pairs={{0,31},{1,2},{2,1},{3,4},{4,3},{5,6},{6,5},{7,8},{8,7},{9,10},{10,... | collective-permute-start | bytes 393224 | tf_op jit(solution)/shard_map/ppermute | solution.py:500
  56.2 12.8 %collective-permute-start.13 = (f32[2,4,8,8,128]{4,3,2,1,0:T(8,128)S(1)}, f32[2,4,8,8,128]{4,3,2,1,0:T(8,128)S(1)}, u32[]{:S(2)}, u32[]{:S(2)}) collective-permute-start(f32[2,4,8,8,128]{4,3,2,1,0:T(8,128)S(1)} %get-tuple-element.33), channel_id=1, source_target_pairs={{0,32},{32,64},{64,96},{96,0},{1,33},{33,65},{65,97},{97,1},{2,34}... | collective-permute-start | bytes 786440 | tf_op jit(solution)/shard_map/ppermute | solution.py:493
  56.3 12.7 %collective-permute-start.14 = (f32[2,4,8,8,128]{4,3,2,1,0:T(8,128)S(1)}, f32[2,4,8,8,128]{4,3,2,1,0:T(8,128)S(1)}, u32[]{:S(2)}, u32[]{:S(2)}) collective-permute-start(f32[2,4,8,8,128]{4,3,2,1,0:T(8,128)S(1)} %get-tuple-element.34), channel_id=1, source_target_pairs={{0,96},{32,0},{64,32},{96,64},{1,97},{33,1},{65,33},{97,65},{2,98}... | collective-permute-start | bytes 786440 | tf_op jit(solution)/shard_map/ppermute | solution.py:493
  59.5 9.4 %collective-permute-start.15 = (f32[2,2,8,8,128]{4,3,2,1,0:T(8,128)S(1)}, f32[2,2,8,8,128]{4,3,2,1,0:T(8,128)S(1)}, u32[]{:S(2)}, u32[]{:S(2)}) collective-permute-start(f32[2,2,8,8,128]{4,3,2,1,0:T(8,128)S(1)} %get-tuple-element.35), channel_id=1, source_target_pairs={{0,1},{1,0},{2,3},{3,2},{4,5},{5,4},{6,7},{7,6},{8,9},{9,8},{10,11... | collective-permute-start | bytes 393224 | tf_op jit(solution)/shard_map/ppermute | solution.py:500
  59.5 9.4 %collective-permute-start.16 = (f32[2,2,8,8,128]{4,3,2,1,0:T(8,128)S(1)}, f32[2,2,8,8,128]{4,3,2,1,0:T(8,128)S(1)}, u32[]{:S(2)}, u32[]{:S(2)}) collective-permute-start(f32[2,2,8,8,128]{4,3,2,1,0:T(8,128)S(1)} %get-tuple-element.36), channel_id=1, source_target_pairs={{0,31},{1,2},{2,1},{3,4},{4,3},{5,6},{6,5},{7,8},{8,7},{9,10},{10,... | collective-permute-start | bytes 393224 | tf_op jit(solution)/shard_map/ppermute | solution.py:500

commit v6 on v5

--- a/solution.py
+++ b/solution.py
@@ -14,7 +14,7 @@
 TS = 4
 CHUNKS = 32
 AXES = ("group", "dev")
-ROUNDS = ((2, 32), (6, 96), (8, 32), (24, 96), (32, 32), (96, 96))
+ROUNDS = ((8, 32), (24, 96), (2, 32), (6, 96), (32, 32), (96, 96))
 
 GAMMA = 5.0 / 3.0
 COURANT = 0.25

time: 73.2 us -> 73.4 us (level)
  starting transfers between devices: 30.4 us -> 32.7 us
  waiting for transfers between devices: 15.6 us -> 13.4 us
    ppermute x6, starting transfers between devices: 15.2 us -> 18.3 us  [body(): lax.ppermute(tile, AXES, [(i, i ^ masks[i % 2]) for i in range(devices)])]
    ppermute x6, waiting for transfers between devices: 13.5 us -> 11.3 us  [body(): lax.ppermute(tile, AXES, [(i, i ^ masks[i % 2]) for i in range(devices)])]
where the time goes in v6:
time: 73.4 us; the launch traced here: 73.2 us
  starting transfers between devices  32.7 us (45%)
  Pallas kernels  26.2 us (36%)
  waiting for transfers between devices  13.4 us (18%)
  between operations  0.95 us (1%)
    ppermute x6, starting transfers between devices, body(): lax.ppermute(tile, AXES, [(i, i ^ masks[i % 2]) for i in range(devices)])  18.3 us
    ppermute x6, waiting for transfers between devices, body(): lax.ppermute(tile, AXES, [(i, i ^ masks[i % 2]) for i in range(devices)])  11.3 us
    ppermute x4, starting transfers between devices, shifted(): lax.ppermute(value, axis, [(i, (i + by) % count) for i in range(count)])  6.67 us
    pallas_call x1, Pallas kernels, body(): inner(w)  6.58 us
    pallas_call x1, Pallas kernels, body(): inner(w2)  6.58 us
    ppermute x2, starting transfers between devices, exchanged(): lax.ppermute(yf, 'dev', far)  4.51 us
    pallas_call x1, Pallas kernels, body(): kernel(second_kernel, specs, result, buffers, 'second_stage', 1 << 20, ou...  3.7 us
    pallas_call x1, Pallas kernels, body(): kernel(assemble_kernel, [SMEM, VMEM, ANY, ANY], [GRID, GRID] + sides, [pl...  3.19 us
  transfers between devices with their start and end apart: 17, of which 8 were waited for; matrix products, arithmetic and copies ran while one was open for 0% of the time, Pallas kernels for 21%

profile of v6, /device:TPU:0, one launch (start us, length us, event | category | flops | bytes accessed | tf_op | source)
XLA Modules:
  0.0 73.2 jit_solution(4080422473573811937)
XLA Ops:
  0.7 1.7 %outgoing.1 = f32[15,32,8,128]{3,2,1,0:T(8,128)S(1)} custom-call(s32[1]{0:T(128)S(6)} %copy.3.count_ref, f32[31,32,8,128]{3,2,1,0:T(8,128)} %bitcast.7), custom_call_target="tpu_custom_call" | custom-call | flops 1024 | bytes 6291456 | tf_op jit(solution)/shard_map/outgoing/pallas_call | solution.py:510
  2.4 2.6 %collective-permute-start.8 = (f32[15,32,8,128]{3,2,1,0:T(8,128)S(1)}, f32[15,32,8,128]{3,2,1,0:T(8,128)}, u32[]{:S(2)}, u32[]{:S(2)}) collective-permute-start(f32[15,32,8,128]{3,2,1,0:T(8,128)S(1)} %outgoing.1), channel_id=1, source_target_pairs={{0,1},{1,2},{2,3},{3,4},{4,5},{5,6},{6,7},{7,8},{8,9},{9,10},{10,1... | collective-permute-start | bytes 5898248 | tf_op jit(solution)/shard_map/ppermute | solution.py:513
  5.0 2.3 %signal_speed.1 = f32[8,128]{1,0:T(8,128)S(1)} custom-call(s32[1]{0:T(128)S(6)} %copy.3.count_ref, s32[1]{0:T(128)} %bitcast.place_ref, f32[31,32,8,128]{3,2,1,0:T(8,128)} %bitcast.8), custom_call_target="tpu_custom_call" | custom-call | flops 1048576 | bytes 6291456 | tf_op jit(solution)/shard_map/signal_speed/pallas_call | solution.py:514
  7.3 0.6 collective-permute-start
  7.9 0.8 %collective-permute-done = f32[8,128]{1,0:T(8,128)S(1)} collective-permute-done((f32[8,128]{1,0:T(8,128)S(1)}, f32[8,128]{1,0:T(8,128)S(1)}, u32[]{:S(2)}, u32[]{:S(2)}) %collective-permute-start) | collective-permute-done | bytes 4128 | tf_op jit(solution)/shard_map/ppermute | solution.py:525
  8.7 1.3 %collective-permute-start.1 = (f32[8,128]{1,0:T(8,128)S(1)}, f32[8,128]{1,0:T(8,128)S(1)}, u32[]{:S(2)}, u32[]{:S(2)}) collective-permute-start(f32[8,128]{1,0:T(8,128)S(1)} %max.24), channel_id=1, source_target_pairs={{0,8},{1,33},{2,10},{3,35},{4,12},{5,37},{6,14},{7,39},{8,0},{9,41... | collective-permute-start | bytes 12296 | tf_op jit(solution)/shard_map/ppermute | solution.py:527
  10.0 2.3 %collective-permute-done.1 = f32[8,128]{1,0:T(8,128)S(1)} collective-permute-done((f32[8,128]{1,0:T(8,128)S(1)}, f32[8,128]{1,0:T(8,128)S(1)}, u32[]{:S(2)}, u32[]{:S(2)}) %collective-permute-start.1) | collective-permute-done | bytes 4128 | tf_op jit(solution)/shard_map/ppermute | solution.py:527
  12.3 2.9 %collective-permute-start.2 = (f32[8,128]{1,0:T(8,128)S(1)}, f32[8,128]{1,0:T(8,128)S(1)}, u32[]{:S(2)}, u32[]{:S(2)}) collective-permute-start(f32[8,128]{1,0:T(8,128)S(1)} %max.25), channel_id=1, source_target_pairs={{0,24},{1,97},{2,26},{3,99},{4,28},{5,101},{6,30},{7,103},{8,16},{... | collective-permute-start | bytes 12296 | tf_op jit(solution)/shard_map/ppermute | solution.py:527
  15.2 1.9 %collective-permute-done.2 = f32[8,128]{1,0:T(8,128)S(1)} collective-permute-done((f32[8,128]{1,0:T(8,128)S(1)}, f32[8,128]{1,0:T(8,128)S(1)}, u32[]{:S(2)}, u32[]{:S(2)}) %collective-permute-start.2) | collective-permute-done | bytes 4128 | tf_op jit(solution)/shard_map/ppermute | solution.py:527
  17.2 1.9 %collective-permute-start.3 = (f32[8,128]{1,0:T(8,128)S(1)}, f32[8,128]{1,0:T(8,128)S(1)}, u32[]{:S(2)}, u32[]{:S(2)}) collective-permute-start(f32[8,128]{1,0:T(8,128)S(1)} %max.26), channel_id=1, source_target_pairs={{0,2},{1,33},{2,0},{3,35},{4,6},{5,37},{6,4},{7,39},{8,10},{9,41},... | collective-permute-start | bytes 12296 | tf_op jit(solution)/shard_map/ppermute | solution.py:527
  19.1 1.7 %collective-permute-done.3 = f32[8,128]{1,0:T(8,128)S(1)} collective-permute-done((f32[8,128]{1,0:T(8,128)S(1)}, f32[8,128]{1,0:T(8,128)S(1)}, u32[]{:S(2)}, u32[]{:S(2)}) %collective-permute-start.3) | collective-permute-done | bytes 4128 | tf_op jit(solution)/shard_map/ppermute | solution.py:527
  20.8 3.3 %collective-permute-start.4 = (f32[8,128]{1,0:T(8,128)S(1)}, f32[8,128]{1,0:T(8,128)S(1)}, u32[]{:S(2)}, u32[]{:S(2)}) collective-permute-start(f32[8,128]{1,0:T(8,128)S(1)} %max.27), channel_id=1, source_target_pairs={{0,6},{1,97},{2,4},{3,99},{4,2},{5,101},{6,0},{7,103},{8,14},{9,10... | collective-permute-start | bytes 12296 | tf_op jit(solution)/shard_map/ppermute | solution.py:527
  24.1 2.0 %collective-permute-done.4 = f32[8,128]{1,0:T(8,128)S(1)} collective-permute-done((f32[8,128]{1,0:T(8,128)S(1)}, f32[8,128]{1,0:T(8,128)S(1)}, u32[]{:S(2)}, u32[]{:S(2)}) %collective-permute-start.4) | collective-permute-done | bytes 4128 | tf_op jit(solution)/shard_map/ppermute | solution.py:527
  26.1 1.8 %collective-permute-start.5 = (f32[8,128]{1,0:T(8,128)S(1)}, f32[8,128]{1,0:T(8,128)S(1)}, u32[]{:S(2)}, u32[]{:S(2)}) collective-permute-start(f32[8,128]{1,0:T(8,128)S(1)} %max.28), channel_id=1, source_target_pairs={{0,32},{1,33},{2,34},{3,35},{4,36},{5,37},{6,38},{7,39},{8,40},{9,... | collective-permute-start | bytes 12296 | tf_op jit(solution)/shard_map/ppermute | solution.py:527
  27.9 1.9 %collective-permute-done.5 = f32[8,128]{1,0:T(8,128)S(1)} collective-permute-done((f32[8,128]{1,0:T(8,128)S(1)}, f32[8,128]{1,0:T(8,128)S(1)}, u32[]{:S(2)}, u32[]{:S(2)}) %collective-permute-start.5) | collective-permute-done | bytes 4128 | tf_op jit(solution)/shard_map/ppermute | solution.py:527
  29.7 7.1 %collective-permute-start.6 = (f32[8,128]{1,0:T(8,128)S(1)}, f32[8,128]{1,0:T(8,128)S(1)}, u32[]{:S(2)}, u32[]{:S(2)}) collective-permute-start(f32[8,128]{1,0:T(8,128)S(1)} %max.29), channel_id=1, source_target_pairs={{0,96},{1,97},{2,98},{3,99},{4,100},{5,101},{6,102},{7,103},{8,104... | collective-permute-start | bytes 12296 | tf_op jit(solution)/shard_map/ppermute | solution.py:527
  36.8 1.6 %collective-permute-done.6 = f32[8,128]{1,0:T(8,128)S(1)} collective-permute-done((f32[8,128]{1,0:T(8,128)S(1)}, f32[8,128]{1,0:T(8,128)S(1)}, u32[]{:S(2)}, u32[]{:S(2)}) %collective-permute-start.6) | collective-permute-done | bytes 4128 | tf_op jit(solution)/shard_map/ppermute | solution.py:527
  38.4 0.0 collective-permute-start.7
  38.4 1.2 %collective-permute-done.7 = f32[8,128]{1,0:T(8,128)S(1)} collective-permute-done((f32[8,128]{1,0:T(8,128)S(1)}, f32[8,128]{1,0:T(8,128)S(1)}, u32[]{:S(2)}, u32[]{:S(2)}) %collective-permute-start.7) | collective-permute-done | bytes 4128 | tf_op jit(solution)/shard_map/ppermute | solution.py:528
  39.6 0.0 collective-permute-done.8.came_ref
  39.6 3.2 %assemble.1 = (f32[16,4,8,8,128]{4,3,2,1,0:T(8,128)S(1)}, f32[16,4,8,8,128]{4,3,2,1,0:T(8,128)S(1)}, f32[2,4,8,8,128]{4,3,2,1,0:T(8,128)S(1)}, f32[2,4,8,8,128]{...) custom-call(s32[1]{0:T(128)} %bitcast.place_ref, f32[8,128]{1,0:T(8,128)S(1)} %max.31.tile_ref, ...), custom_call_target="tpu_custom_call" | custom-call | flops 1048576 | bytes 6291456 | tf_op jit(solution)/shard_map/assemble/pallas_call | solution.py:530
  42.8 0.1 collective-permute-start.9
  42.8 3.3 %collective-permute-start.10 = (f32[2,4,8,8,128]{4,3,2,1,0:T(8,128)S(1)}, f32[2,4,8,8,128]{4,3,2,1,0:T(8,128)S(1)}, u32[]{:S(2)}, u32[]{:S(2)}) collective-permute-start(f32[2,4,8,8,128]{4,3,2,1,0:T(8,128)S(1)} %get-tuple-element.26), channel_id=1, source_target_pairs={{0,96},{32,0},{64,32},{96,64},{1,97},{33,1},{65,33},{97,65},{2,98}... | collective-permute-start | bytes 786440 | tf_op jit(solution)/shard_map/ppermute | solution.py:493
  46.1 0.0 collective-permute-start.11
  46.1 1.6 %collective-permute-start.12 = (f32[2,2,8,8,128]{4,3,2,1,0:T(8,128)S(1)}, f32[2,2,8,8,128]{4,3,2,1,0:T(8,128)S(1)}, u32[]{:S(2)}, u32[]{:S(2)}) collective-permute-start(f32[2,2,8,8,128]{4,3,2,1,0:T(8,128)S(1)} %get-tuple-element.28), channel_id=1, source_target_pairs={{0,31},{1,2},{2,1},{3,4},{4,3},{5,6},{6,5},{7,8},{8,7},{9,10},{10,... | collective-permute-start | bytes 393224 | tf_op jit(solution)/shard_map/ppermute | solution.py:500
  47.7 6.6 %inner_fluxes.2 = (f32[16,4,8,8,128]{4,3,2,1,0:T(8,128)S(1)}, f32[16,4,8,8,128]{4,3,2,1,0:T(8,128)S(1)}) custom-call(f32[16,4,8,8,128]{4,3,2,1,0:T(8,128)S(1)} %get-tuple-element.21.w_ref), custom_call_target="tpu_custom_call" | custom-call | flops 41943040 | bytes 6291456 | tf_op jit(solution)/shard_map/inner_fluxes/pallas_call | solution.py:543
  54.3 0.0 collective-permute-done.11.yn
  54.3 0.0 collective-permute-done.12.yf
  54.3 0.0 collective-permute-done.9.xl
  54.3 0.0 collective-permute-done.10.xh
  54.3 2.1 %first_stage.1 = (f32[16,4,8,8,128]{4,3,2,1,0:T(8,128)S(1)}, f32[16,4,8,8,128]{4,3,2,1,0:T(8,128)S(1)}, f32[2,4,8,8,128]{4,3,2,1,0:T(8,128)S(1)}, f32[2,4,8,8,12...) custom-call(s32[1]{0:T(128)} %bitcast.place_ref, ...), custom_call_target="tpu_custom_call" | custom-call | flops 1048576 | bytes 6291456 | tf_op jit(solution)/shard_map/first_stage/pallas_call | solution.py:542
  56.4 0.1 collective-permute-start.13
  56.5 3.2 %collective-permute-start.14 = (f32[2,4,8,8,128]{4,3,2,1,0:T(8,128)S(1)}, f32[2,4,8,8,128]{4,3,2,1,0:T(8,128)S(1)}, u32[]{:S(2)}, u32[]{:S(2)}) collective-permute-start(f32[2,4,8,8,128]{4,3,2,1,0:T(8,128)S(1)} %get-tuple-element.34), channel_id=1, source_target_pairs={{0,96},{32,0},{64,32},{96,64},{1,97},{33,1},{65,33},{97,65},{2,98}... | collective-permute-start | bytes 786440 | tf_op jit(solution)/shard_map/ppermute | solution.py:493
  59.8 0.0 collective-permute-start.15
  59.8 2.9 %collective-permute-start.16 = (f32[2,2,8,8,128]{4,3,2,1,0:T(8,128)S(1)}, f32[2,2,8,8,128]{4,3,2,1,0:T(8,128)S(1)}, u32[]{:S(2)}, u32[]{:S(2)}) collective-permute-start(f32[2,2,8,8,128]{4,3,2,1,0:T(8,128)S(1)} %get-tuple-element.36), channel_id=1, source_target_pairs={{0,31},{1,2},{2,1},{3,4},{4,3},{5,6},{6,5},{7,8},{8,7},{9,10},{10,... | collective-permute-start | bytes 393224 | tf_op jit(solution)/shard_map/ppermute | solution.py:500
  62.7 6.6 %inner_fluxes.3 = (f32[16,4,8,8,128]{4,3,2,1,0:T(8,128)S(1)}, f32[16,4,8,8,128]{4,3,2,1,0:T(8,128)S(1)}) custom-call(f32[16,4,8,8,128]{4,3,2,1,0:T(8,128)S(1)} %get-tuple-element.29.w_ref), custom_call_target="tpu_custom_call" | custom-call | flops 41943040 | bytes 6291456 | tf_op jit(solution)/shard_map/inner_fluxes/pallas_call | solution.py:549
  69.3 0.0 collective-permute-done.15.yn
  69.3 0.0 collective-permute-done.16.yf
  69.3 0.0 collective-permute-done.13.xl
  69.3 0.0 collective-permute-done.14.xh
  69.3 3.7 %second_stage.1 = f32[16,32,8,128]{3,2,1,0:T(8,128)} custom-call(s32[1]{0:T(128)} %bitcast.place_ref, f32[8,128]{1,0:T(8,128)S(1)} %max.31.tile_ref, f32[16,4,8,8,128]{4,3,2,1,0:T(8,128)S(1)} %get-tuple-element.29.w_ref, f32[16,4,8,8,128]{4,3,2,1,0:T(8,128)S(1)} %get-tuple-element.30.s_ref, f32[16,4,8,8,128]{4,3,2,1,0:T(8,128)S(1)} %get-tuple-element.31.txz, ...), custom_call_target="tpu_custom_call" | custom-call | flops 1048576 | bytes 6291456 | tf_op jit(solution)/shard_map/second_stage/pallas_call | solution.py:548
  (8 shorter events, 0.0 us)
Async XLA Ops:
  2.4 37.2 %collective-permute-start.8 = (f32[15,32,8,128]{3,2,1,0:T(8,128)S(1)}, f32[15,32,8,128]{3,2,1,0:T(8,128)}, u32[]{:S(2)}, u32[]{:S(2)}) collective-permute-start(f32[15,32,8,128]{3,2,1,0:T(8,128)S(1)} %outgoing.1), channel_id=1, source_target_pairs={{0,1},{1,2},{2,3},{3,4},{4,5},{5,6},{6,7},{7,8},{8,9},{9,10},{10,1... | collective-permute-start | bytes 5898248 | tf_op jit(solution)/shard_map/ppermute | solution.py:513
  7.3 1.5 %collective-permute-start = (f32[8,128]{1,0:T(8,128)S(1)}, f32[8,128]{1,0:T(8,128)S(1)}, u32[]{:S(2)}, u32[]{:S(2)}) collective-permute-start(f32[8,128]{1,0:T(8,128)S(1)} %signal_speed.1), channel_id=1, source_target_pairs={{0,1},{1,0},{2,3},{3,2},{4,5},{5,4},{6,7},{7,6},{8,9},{9,8},{10,11... | collective-permute-start | bytes 12296 | tf_op jit(solution)/shard_map/ppermute | solution.py:525
  8.7 3.6 %collective-permute-start.1 = (f32[8,128]{1,0:T(8,128)S(1)}, f32[8,128]{1,0:T(8,128)S(1)}, u32[]{:S(2)}, u32[]{:S(2)}) collective-permute-start(f32[8,128]{1,0:T(8,128)S(1)} %max.24), channel_id=1, source_target_pairs={{0,8},{1,33},{2,10},{3,35},{4,12},{5,37},{6,14},{7,39},{8,0},{9,41... | collective-permute-start | bytes 12296 | tf_op jit(solution)/shard_map/ppermute | solution.py:527
  12.3 4.8 %collective-permute-start.2 = (f32[8,128]{1,0:T(8,128)S(1)}, f32[8,128]{1,0:T(8,128)S(1)}, u32[]{:S(2)}, u32[]{:S(2)}) collective-permute-start(f32[8,128]{1,0:T(8,128)S(1)} %max.25), channel_id=1, source_target_pairs={{0,24},{1,97},{2,26},{3,99},{4,28},{5,101},{6,30},{7,103},{8,16},{... | collective-permute-start | bytes 12296 | tf_op jit(solution)/shard_map/ppermute | solution.py:527
  17.2 3.6 %collective-permute-start.3 = (f32[8,128]{1,0:T(8,128)S(1)}, f32[8,128]{1,0:T(8,128)S(1)}, u32[]{:S(2)}, u32[]{:S(2)}) collective-permute-start(f32[8,128]{1,0:T(8,128)S(1)} %max.26), channel_id=1, source_target_pairs={{0,2},{1,33},{2,0},{3,35},{4,6},{5,37},{6,4},{7,39},{8,10},{9,41},... | collective-permute-start | bytes 12296 | tf_op jit(solution)/shard_map/ppermute | solution.py:527
  20.8 5.3 %collective-permute-start.4 = (f32[8,128]{1,0:T(8,128)S(1)}, f32[8,128]{1,0:T(8,128)S(1)}, u32[]{:S(2)}, u32[]{:S(2)}) collective-permute-start(f32[8,128]{1,0:T(8,128)S(1)} %max.27), channel_id=1, source_target_pairs={{0,6},{1,97},{2,4},{3,99},{4,2},{5,101},{6,0},{7,103},{8,14},{9,10... | collective-permute-start | bytes 12296 | tf_op jit(solution)/shard_map/ppermute | solution.py:527
  26.1 3.6 %collective-permute-start.5 = (f32[8,128]{1,0:T(8,128)S(1)}, f32[8,128]{1,0:T(8,128)S(1)}, u32[]{:S(2)}, u32[]{:S(2)}) collective-permute-start(f32[8,128]{1,0:T(8,128)S(1)} %max.28), channel_id=1, source_target_pairs={{0,32},{1,33},{2,34},{3,35},{4,36},{5,37},{6,38},{7,39},{8,40},{9,... | collective-permute-start | bytes 12296 | tf_op jit(solution)/shard_map/ppermute | solution.py:527
  29.7 8.7 %collective-permute-start.6 = (f32[8,128]{1,0:T(8,128)S(1)}, f32[8,128]{1,0:T(8,128)S(1)}, u32[]{:S(2)}, u32[]{:S(2)}) collective-permute-start(f32[8,128]{1,0:T(8,128)S(1)} %max.29), channel_id=1, source_target_pairs={{0,96},{1,97},{2,98},{3,99},{4,100},{5,101},{6,102},{7,103},{8,104... | collective-permute-start | bytes 12296 | tf_op jit(solution)/shard_map/ppermute | solution.py:527
  38.4 1.2 %collective-permute-start.7 = (f32[8,128]{1,0:T(8,128)S(1)}, f32[8,128]{1,0:T(8,128)S(1)}, u32[]{:S(2)}, u32[]{:S(2)}) collective-permute-start(f32[8,128]{1,0:T(8,128)S(1)} %max.30), channel_id=1, source_target_pairs={{0,1},{1,0},{2,3},{3,2},{4,5},{5,4},{6,7},{7,6},{8,9},{9,8},{10,11... | collective-permute-start | bytes 12296 | tf_op jit(solution)/shard_map/ppermute | solution.py:528
  42.8 11.6 %collective-permute-start.9 = (f32[2,4,8,8,128]{4,3,2,1,0:T(8,128)S(1)}, f32[2,4,8,8,128]{4,3,2,1,0:T(8,128)S(1)}, u32[]{:S(2)}, u32[]{:S(2)}) collective-permute-start(f32[2,4,8,8,128]{4,3,2,1,0:T(8,128)S(1)} %get-tuple-element.25), channel_id=1, source_target_pairs={{0,32},{32,64},{64,96},{96,0},{1,33},{33,65},{65,97},{97,1},{2,34}... | collective-permute-start | bytes 786440 | tf_op jit(solution)/shard_map/ppermute | solution.py:493
  42.8 11.5 %collective-permute-start.10 = (f32[2,4,8,8,128]{4,3,2,1,0:T(8,128)S(1)}, f32[2,4,8,8,128]{4,3,2,1,0:T(8,128)S(1)}, u32[]{:S(2)}, u32[]{:S(2)}) collective-permute-start(f32[2,4,8,8,128]{4,3,2,1,0:T(8,128)S(1)} %get-tuple-element.26), channel_id=1, source_target_pairs={{0,96},{32,0},{64,32},{96,64},{1,97},{33,1},{65,33},{97,65},{2,98}... | collective-permute-start | bytes 786440 | tf_op jit(solution)/shard_map/ppermute | solution.py:493
  46.1 8.2 %collective-permute-start.11 = (f32[2,2,8,8,128]{4,3,2,1,0:T(8,128)S(1)}, f32[2,2,8,8,128]{4,3,2,1,0:T(8,128)S(1)}, u32[]{:S(2)}, u32[]{:S(2)}) collective-permute-start(f32[2,2,8,8,128]{4,3,2,1,0:T(8,128)S(1)} %get-tuple-element.27), channel_id=1, source_target_pairs={{0,1},{1,0},{2,3},{3,2},{4,5},{5,4},{6,7},{7,6},{8,9},{9,8},{10,11... | collective-permute-start | bytes 393224 | tf_op jit(solution)/shard_map/ppermute | solution.py:500
  46.1 8.2 %collective-permute-start.12 = (f32[2,2,8,8,128]{4,3,2,1,0:T(8,128)S(1)}, f32[2,2,8,8,128]{4,3,2,1,0:T(8,128)S(1)}, u32[]{:S(2)}, u32[]{:S(2)}) collective-permute-start(f32[2,2,8,8,128]{4,3,2,1,0:T(8,128)S(1)} %get-tuple-element.28), channel_id=1, source_target_pairs={{0,31},{1,2},{2,1},{3,4},{4,3},{5,6},{6,5},{7,8},{8,7},{9,10},{10,... | collective-permute-start | bytes 393224 | tf_op jit(solution)/shard_map/ppermute | solution.py:500
  56.4 12.9 %collective-permute-start.13 = (f32[2,4,8,8,128]{4,3,2,1,0:T(8,128)S(1)}, f32[2,4,8,8,128]{4,3,2,1,0:T(8,128)S(1)}, u32[]{:S(2)}, u32[]{:S(2)}) collective-permute-start(f32[2,4,8,8,128]{4,3,2,1,0:T(8,128)S(1)} %get-tuple-element.33), channel_id=1, source_target_pairs={{0,32},{32,64},{64,96},{96,0},{1,33},{33,65},{65,97},{97,1},{2,34}... | collective-permute-start | bytes 786440 | tf_op jit(solution)/shard_map/ppermute | solution.py:493
  56.5 12.8 %collective-permute-start.14 = (f32[2,4,8,8,128]{4,3,2,1,0:T(8,128)S(1)}, f32[2,4,8,8,128]{4,3,2,1,0:T(8,128)S(1)}, u32[]{:S(2)}, u32[]{:S(2)}) collective-permute-start(f32[2,4,8,8,128]{4,3,2,1,0:T(8,128)S(1)} %get-tuple-element.34), channel_id=1, source_target_pairs={{0,96},{32,0},{64,32},{96,64},{1,97},{33,1},{65,33},{97,65},{2,98}... | collective-permute-start | bytes 786440 | tf_op jit(solution)/shard_map/ppermute | solution.py:493
  59.8 9.5 %collective-permute-start.15 = (f32[2,2,8,8,128]{4,3,2,1,0:T(8,128)S(1)}, f32[2,2,8,8,128]{4,3,2,1,0:T(8,128)S(1)}, u32[]{:S(2)}, u32[]{:S(2)}) collective-permute-start(f32[2,2,8,8,128]{4,3,2,1,0:T(8,128)S(1)} %get-tuple-element.35), channel_id=1, source_target_pairs={{0,1},{1,0},{2,3},{3,2},{4,5},{5,4},{6,7},{7,6},{8,9},{9,8},{10,11... | collective-permute-start | bytes 393224 | tf_op jit(solution)/shard_map/ppermute | solution.py:500
  59.8 9.5 %collective-permute-start.16 = (f32[2,2,8,8,128]{4,3,2,1,0:T(8,128)S(1)}, f32[2,2,8,8,128]{4,3,2,1,0:T(8,128)S(1)}, u32[]{:S(2)}, u32[]{:S(2)}) collective-permute-start(f32[2,2,8,8,128]{4,3,2,1,0:T(8,128)S(1)} %get-tuple-element.36), channel_id=1, source_target_pairs={{0,31},{1,2},{2,1},{3,4},{4,3},{5,6},{6,5},{7,8},{8,7},{9,10},{10,... | collective-permute-start | bytes 393224 | tf_op jit(solution)/shard_map/ppermute | solution.py:500

commit v7 on v6

--- a/solution.py
+++ b/solution.py
@@ -374,7 +374,7 @@
                 yc[x, part, k] = zero
         return 0
 
-    lax.fori_loop(0, XS, clear, 0)
+    lax.fori_loop(0, XS, clear, 0, unroll=4)
 
     def store(half, part, y, values):
         for k in range(FIELDS):
@@ -408,7 +408,7 @@
 
 
 def step_of(tile_ref):
-    return COURANT / jnp.max(jnp.where(iota(0) == 1, tile_ref[...], 0.0))
+    return COURANT / jnp.broadcast_to(tile_ref[1:2, :], (8, 128))
 
 
 def first_kernel(place_ref, tile_ref, w_ref, u_ref, txz, ty, xl, xh, yn, yf, s_ref, w2_ref, xl_ref, xh_ref, yn_ref, yf_ref, xc, yc):

time: 73.4 us -> 73.4 us (level)
  starting transfers between devices: 32.7 us -> 30.7 us
  waiting for transfers between devices: 13.4 us -> 15.3 us
    ppermute x6, starting transfers between devices: 18.3 us -> 15.8 us  [body(): lax.ppermute(tile, AXES, [(i, i ^ masks[i % 2]) for i in range(devices)])]
    ppermute x6, waiting for transfers between devices: 11.3 us -> 13.3 us  [body(): lax.ppermute(tile, AXES, [(i, i ^ masks[i % 2]) for i in range(devices)])]
where the time goes in v7:
time: 73.4 us; the launch traced here: 73.2 us
  starting transfers between devices  30.7 us (42%)
  Pallas kernels  26.1 us (36%)
  waiting for transfers between devices  15.3 us (21%)
  between operations  0.95 us (1%)
    ppermute x6, starting transfers between devices, body(): lax.ppermute(tile, AXES, [(i, i ^ masks[i % 2]) for i in range(devices)])  15.8 us
    ppermute x6, waiting for transfers between devices, body(): lax.ppermute(tile, AXES, [(i, i ^ masks[i % 2]) for i in range(devices)])  13.3 us
    ppermute x4, starting transfers between devices, shifted(): lax.ppermute(value, axis, [(i, (i + by) % count) for i in range(count)])  6.67 us
    pallas_call x1, Pallas kernels, body(): inner(w)  6.58 us
    pallas_call x1, Pallas kernels, body(): inner(w2)  6.58 us
    ppermute x2, starting transfers between devices, exchanged(): lax.ppermute(yf, 'dev', far)  4.51 us
    pallas_call x1, Pallas kernels, body(): kernel(second_kernel, specs, result, buffers, 'second_stage', 1 << 20, ou...  3.64 us
    pallas_call x1, Pallas kernels, body(): kernel(assemble_kernel, [SMEM, VMEM, ANY, ANY], [GRID, GRID] + sides, [pl...  3.19 us
  transfers between devices with their start and end apart: 17, of which 8 were waited for; matrix products, arithmetic and copies ran while one was open for 0% of the time, Pallas kernels for 21%

profile of v7, /device:TPU:0, one launch (start us, length us, event | category | flops | bytes accessed | tf_op | source)
XLA Modules:
  0.0 73.2 jit_solution(13733454521743023370)
XLA Ops:
  0.7 1.7 %outgoing.1 = f32[15,32,8,128]{3,2,1,0:T(8,128)S(1)} custom-call(s32[1]{0:T(128)S(6)} %copy.3.count_ref, f32[31,32,8,128]{3,2,1,0:T(8,128)} %bitcast.7), custom_call_target="tpu_custom_call" | custom-call | flops 1024 | bytes 6291456 | tf_op jit(solution)/shard_map/outgoing/pallas_call | solution.py:510
  2.4 2.6 %collective-permute-start.8 = (f32[15,32,8,128]{3,2,1,0:T(8,128)S(1)}, f32[15,32,8,128]{3,2,1,0:T(8,128)}, u32[]{:S(2)}, u32[]{:S(2)}) collective-permute-start(f32[15,32,8,128]{3,2,1,0:T(8,128)S(1)} %outgoing.1), channel_id=1, source_target_pairs={{0,1},{1,2},{2,3},{3,4},{4,5},{5,6},{6,7},{7,8},{8,9},{9,10},{10,1... | collective-permute-start | bytes 5898248 | tf_op jit(solution)/shard_map/ppermute | solution.py:513
  5.0 2.3 %signal_speed.1 = f32[8,128]{1,0:T(8,128)S(1)} custom-call(s32[1]{0:T(128)S(6)} %copy.3.count_ref, s32[1]{0:T(128)} %bitcast.place_ref, f32[31,32,8,128]{3,2,1,0:T(8,128)} %bitcast.8), custom_call_target="tpu_custom_call" | custom-call | flops 1048576 | bytes 6291456 | tf_op jit(solution)/shard_map/signal_speed/pallas_call | solution.py:514
  7.3 1.2 %collective-permute-start = (f32[8,128]{1,0:T(8,128)S(1)}, f32[8,128]{1,0:T(8,128)S(1)}, u32[]{:S(2)}, u32[]{:S(2)}) collective-permute-start(f32[8,128]{1,0:T(8,128)S(1)} %signal_speed.1), channel_id=1, source_target_pairs={{0,1},{1,0},{2,3},{3,2},{4,5},{5,4},{6,7},{7,6},{8,9},{9,8},{10,11... | collective-permute-start | bytes 12296 | tf_op jit(solution)/shard_map/ppermute | solution.py:525
  8.5 0.8 %collective-permute-done = f32[8,128]{1,0:T(8,128)S(1)} collective-permute-done((f32[8,128]{1,0:T(8,128)S(1)}, f32[8,128]{1,0:T(8,128)S(1)}, u32[]{:S(2)}, u32[]{:S(2)}) %collective-permute-start) | collective-permute-done | bytes 4128 | tf_op jit(solution)/shard_map/ppermute | solution.py:525
  9.3 0.8 %collective-permute-start.1 = (f32[8,128]{1,0:T(8,128)S(1)}, f32[8,128]{1,0:T(8,128)S(1)}, u32[]{:S(2)}, u32[]{:S(2)}) collective-permute-start(f32[8,128]{1,0:T(8,128)S(1)} %max.24), channel_id=1, source_target_pairs={{0,8},{1,33},{2,10},{3,35},{4,12},{5,37},{6,14},{7,39},{8,0},{9,41... | collective-permute-start | bytes 12296 | tf_op jit(solution)/shard_map/ppermute | solution.py:527
  10.0 2.8 %collective-permute-done.1 = f32[8,128]{1,0:T(8,128)S(1)} collective-permute-done((f32[8,128]{1,0:T(8,128)S(1)}, f32[8,128]{1,0:T(8,128)S(1)}, u32[]{:S(2)}, u32[]{:S(2)}) %collective-permute-start.1) | collective-permute-done | bytes 4128 | tf_op jit(solution)/shard_map/ppermute | solution.py:527
  12.9 2.4 %collective-permute-start.2 = (f32[8,128]{1,0:T(8,128)S(1)}, f32[8,128]{1,0:T(8,128)S(1)}, u32[]{:S(2)}, u32[]{:S(2)}) collective-permute-start(f32[8,128]{1,0:T(8,128)S(1)} %max.25), channel_id=1, source_target_pairs={{0,24},{1,97},{2,26},{3,99},{4,28},{5,101},{6,30},{7,103},{8,16},{... | collective-permute-start | bytes 12296 | tf_op jit(solution)/shard_map/ppermute | solution.py:527
  15.3 2.4 %collective-permute-done.2 = f32[8,128]{1,0:T(8,128)S(1)} collective-permute-done((f32[8,128]{1,0:T(8,128)S(1)}, f32[8,128]{1,0:T(8,128)S(1)}, u32[]{:S(2)}, u32[]{:S(2)}) %collective-permute-start.2) | collective-permute-done | bytes 4128 | tf_op jit(solution)/shard_map/ppermute | solution.py:527
  17.7 1.4 %collective-permute-start.3 = (f32[8,128]{1,0:T(8,128)S(1)}, f32[8,128]{1,0:T(8,128)S(1)}, u32[]{:S(2)}, u32[]{:S(2)}) collective-permute-start(f32[8,128]{1,0:T(8,128)S(1)} %max.26), channel_id=1, source_target_pairs={{0,2},{1,33},{2,0},{3,35},{4,6},{5,37},{6,4},{7,39},{8,10},{9,41},... | collective-permute-start | bytes 12296 | tf_op jit(solution)/shard_map/ppermute | solution.py:527
  19.1 2.2 %collective-permute-done.3 = f32[8,128]{1,0:T(8,128)S(1)} collective-permute-done((f32[8,128]{1,0:T(8,128)S(1)}, f32[8,128]{1,0:T(8,128)S(1)}, u32[]{:S(2)}, u32[]{:S(2)}) %collective-permute-start.3) | collective-permute-done | bytes 4128 | tf_op jit(solution)/shard_map/ppermute | solution.py:527
  21.3 2.8 %collective-permute-start.4 = (f32[8,128]{1,0:T(8,128)S(1)}, f32[8,128]{1,0:T(8,128)S(1)}, u32[]{:S(2)}, u32[]{:S(2)}) collective-permute-start(f32[8,128]{1,0:T(8,128)S(1)} %max.27), channel_id=1, source_target_pairs={{0,6},{1,97},{2,4},{3,99},{4,2},{5,101},{6,0},{7,103},{8,14},{9,10... | collective-permute-start | bytes 12296 | tf_op jit(solution)/shard_map/ppermute | solution.py:527
  24.1 2.4 %collective-permute-done.4 = f32[8,128]{1,0:T(8,128)S(1)} collective-permute-done((f32[8,128]{1,0:T(8,128)S(1)}, f32[8,128]{1,0:T(8,128)S(1)}, u32[]{:S(2)}, u32[]{:S(2)}) %collective-permute-start.4) | collective-permute-done | bytes 4128 | tf_op jit(solution)/shard_map/ppermute | solution.py:527
  26.6 1.8 %collective-permute-start.5 = (f32[8,128]{1,0:T(8,128)S(1)}, f32[8,128]{1,0:T(8,128)S(1)}, u32[]{:S(2)}, u32[]{:S(2)}) collective-permute-start(f32[8,128]{1,0:T(8,128)S(1)} %max.28), channel_id=1, source_target_pairs={{0,32},{1,33},{2,34},{3,35},{4,36},{5,37},{6,38},{7,39},{8,40},{9,... | collective-permute-start | bytes 12296 | tf_op jit(solution)/shard_map/ppermute | solution.py:527
  28.3 1.8 %collective-permute-done.5 = f32[8,128]{1,0:T(8,128)S(1)} collective-permute-done((f32[8,128]{1,0:T(8,128)S(1)}, f32[8,128]{1,0:T(8,128)S(1)}, u32[]{:S(2)}, u32[]{:S(2)}) %collective-permute-start.5) | collective-permute-done | bytes 4128 | tf_op jit(solution)/shard_map/ppermute | solution.py:527
  30.2 6.7 %collective-permute-start.6 = (f32[8,128]{1,0:T(8,128)S(1)}, f32[8,128]{1,0:T(8,128)S(1)}, u32[]{:S(2)}, u32[]{:S(2)}) collective-permute-start(f32[8,128]{1,0:T(8,128)S(1)} %max.29), channel_id=1, source_target_pairs={{0,96},{1,97},{2,98},{3,99},{4,100},{5,101},{6,102},{7,103},{8,104... | collective-permute-start | bytes 12296 | tf_op jit(solution)/shard_map/ppermute | solution.py:527
  36.8 1.6 %collective-permute-done.6 = f32[8,128]{1,0:T(8,128)S(1)} collective-permute-done((f32[8,128]{1,0:T(8,128)S(1)}, f32[8,128]{1,0:T(8,128)S(1)}, u32[]{:S(2)}, u32[]{:S(2)}) %collective-permute-start.6) | collective-permute-done | bytes 4128 | tf_op jit(solution)/shard_map/ppermute | solution.py:527
  38.4 0.0 collective-permute-start.7
  38.4 1.2 %collective-permute-done.7 = f32[8,128]{1,0:T(8,128)S(1)} collective-permute-done((f32[8,128]{1,0:T(8,128)S(1)}, f32[8,128]{1,0:T(8,128)S(1)}, u32[]{:S(2)}, u32[]{:S(2)}) %collective-permute-start.7) | collective-permute-done | bytes 4128 | tf_op jit(solution)/shard_map/ppermute | solution.py:528
  39.6 0.0 collective-permute-done.8.came_ref
  39.6 3.2 %assemble.1 = (f32[16,4,8,8,128]{4,3,2,1,0:T(8,128)S(1)}, f32[16,4,8,8,128]{4,3,2,1,0:T(8,128)S(1)}, f32[2,4,8,8,128]{4,3,2,1,0:T(8,128)S(1)}, f32[2,4,8,8,128]{...) custom-call(s32[1]{0:T(128)} %bitcast.place_ref, f32[8,128]{1,0:T(8,128)S(1)} %max.31.tile_ref, ...), custom_call_target="tpu_custom_call" | custom-call | flops 1048576 | bytes 6291456 | tf_op jit(solution)/shard_map/assemble/pallas_call | solution.py:530
  42.8 0.1 collective-permute-start.9
  42.9 3.3 %collective-permute-start.10 = (f32[2,4,8,8,128]{4,3,2,1,0:T(8,128)S(1)}, f32[2,4,8,8,128]{4,3,2,1,0:T(8,128)S(1)}, u32[]{:S(2)}, u32[]{:S(2)}) collective-permute-start(f32[2,4,8,8,128]{4,3,2,1,0:T(8,128)S(1)} %get-tuple-element.26), channel_id=1, source_target_pairs={{0,96},{32,0},{64,32},{96,64},{1,97},{33,1},{65,33},{97,65},{2,98}... | collective-permute-start | bytes 786440 | tf_op jit(solution)/shard_map/ppermute | solution.py:493
  46.2 0.0 collective-permute-start.11
  46.2 1.5 %collective-permute-start.12 = (f32[2,2,8,8,128]{4,3,2,1,0:T(8,128)S(1)}, f32[2,2,8,8,128]{4,3,2,1,0:T(8,128)S(1)}, u32[]{:S(2)}, u32[]{:S(2)}) collective-permute-start(f32[2,2,8,8,128]{4,3,2,1,0:T(8,128)S(1)} %get-tuple-element.28), channel_id=1, source_target_pairs={{0,31},{1,2},{2,1},{3,4},{4,3},{5,6},{6,5},{7,8},{8,7},{9,10},{10,... | collective-permute-start | bytes 393224 | tf_op jit(solution)/shard_map/ppermute | solution.py:500
  47.7 6.6 %inner_fluxes.2 = (f32[16,4,8,8,128]{4,3,2,1,0:T(8,128)S(1)}, f32[16,4,8,8,128]{4,3,2,1,0:T(8,128)S(1)}) custom-call(f32[16,4,8,8,128]{4,3,2,1,0:T(8,128)S(1)} %get-tuple-element.21.w_ref), custom_call_target="tpu_custom_call" | custom-call | flops 41943040 | bytes 6291456 | tf_op jit(solution)/shard_map/inner_fluxes/pallas_call | solution.py:543
  54.3 0.0 collective-permute-done.11.yn
  54.3 0.0 collective-permute-done.12.yf
  54.3 0.0 collective-permute-done.9.xl
  54.3 0.0 collective-permute-done.10.xh
  54.3 2.1 %first_stage.1 = (f32[16,4,8,8,128]{4,3,2,1,0:T(8,128)S(1)}, f32[16,4,8,8,128]{4,3,2,1,0:T(8,128)S(1)}, f32[2,4,8,8,128]{4,3,2,1,0:T(8,128)S(1)}, f32[2,4,8,8,12...) custom-call(s32[1]{0:T(128)} %bitcast.place_ref, ...), custom_call_target="tpu_custom_call" | custom-call | flops 1048576 | bytes 6291456 | tf_op jit(solution)/shard_map/first_stage/pallas_call | solution.py:542
  56.5 0.1 collective-permute-start.13
  56.6 3.2 %collective-permute-start.14 = (f32[2,4,8,8,128]{4,3,2,1,0:T(8,128)S(1)}, f32[2,4,8,8,128]{4,3,2,1,0:T(8,128)S(1)}, u32[]{:S(2)}, u32[]{:S(2)}) collective-permute-start(f32[2,4,8,8,128]{4,3,2,1,0:T(8,128)S(1)} %get-tuple-element.34), channel_id=1, source_target_pairs={{0,96},{32,0},{64,32},{96,64},{1,97},{33,1},{65,33},{97,65},{2,98}... | collective-permute-start | bytes 786440 | tf_op jit(solution)/shard_map/ppermute | solution.py:493
  59.8 0.0 collective-permute-start.15
  59.8 3.0 %collective-permute-start.16 = (f32[2,2,8,8,128]{4,3,2,1,0:T(8,128)S(1)}, f32[2,2,8,8,128]{4,3,2,1,0:T(8,128)S(1)}, u32[]{:S(2)}, u32[]{:S(2)}) collective-permute-start(f32[2,2,8,8,128]{4,3,2,1,0:T(8,128)S(1)} %get-tuple-element.36), channel_id=1, source_target_pairs={{0,31},{1,2},{2,1},{3,4},{4,3},{5,6},{6,5},{7,8},{8,7},{9,10},{10,... | collective-permute-start | bytes 393224 | tf_op jit(solution)/shard_map/ppermute | solution.py:500
  62.8 6.6 %inner_fluxes.3 = (f32[16,4,8,8,128]{4,3,2,1,0:T(8,128)S(1)}, f32[16,4,8,8,128]{4,3,2,1,0:T(8,128)S(1)}) custom-call(f32[16,4,8,8,128]{4,3,2,1,0:T(8,128)S(1)} %get-tuple-element.29.w_ref), custom_call_target="tpu_custom_call" | custom-call | flops 41943040 | bytes 6291456 | tf_op jit(solution)/shard_map/inner_fluxes/pallas_call | solution.py:549
  69.3 0.0 collective-permute-done.15.yn
  69.4 0.0 collective-permute-done.16.yf
  69.4 0.0 collective-permute-done.13.xl
  69.4 0.0 collective-permute-done.14.xh
  69.4 3.6 %second_stage.1 = f32[16,32,8,128]{3,2,1,0:T(8,128)} custom-call(s32[1]{0:T(128)} %bitcast.place_ref, f32[8,128]{1,0:T(8,128)S(1)} %max.31.tile_ref, f32[16,4,8,8,128]{4,3,2,1,0:T(8,128)S(1)} %get-tuple-element.29.w_ref, f32[16,4,8,8,128]{4,3,2,1,0:T(8,128)S(1)} %get-tuple-element.30.s_ref, f32[16,4,8,8,128]{4,3,2,1,0:T(8,128)S(1)} %get-tuple-element.31.txz, ...), custom_call_target="tpu_custom_call" | custom-call | flops 1048576 | bytes 6291456 | tf_op jit(solution)/shard_map/second_stage/pallas_call | solution.py:548
  (8 shorter events, 0.0 us)
Async XLA Ops:
  2.4 37.2 %collective-permute-start.8 = (f32[15,32,8,128]{3,2,1,0:T(8,128)S(1)}, f32[15,32,8,128]{3,2,1,0:T(8,128)}, u32[]{:S(2)}, u32[]{:S(2)}) collective-permute-start(f32[15,32,8,128]{3,2,1,0:T(8,128)S(1)} %outgoing.1), channel_id=1, source_target_pairs={{0,1},{1,2},{2,3},{3,4},{4,5},{5,6},{6,7},{7,8},{8,9},{9,10},{10,1... | collective-permute-start | bytes 5898248 | tf_op jit(solution)/shard_map/ppermute | solution.py:513
  7.3 2.0 %collective-permute-start = (f32[8,128]{1,0:T(8,128)S(1)}, f32[8,128]{1,0:T(8,128)S(1)}, u32[]{:S(2)}, u32[]{:S(2)}) collective-permute-start(f32[8,128]{1,0:T(8,128)S(1)} %signal_speed.1), channel_id=1, source_target_pairs={{0,1},{1,0},{2,3},{3,2},{4,5},{5,4},{6,7},{7,6},{8,9},{9,8},{10,11... | collective-permute-start | bytes 12296 | tf_op jit(solution)/shard_map/ppermute | solution.py:525
  9.3 3.6 %collective-permute-start.1 = (f32[8,128]{1,0:T(8,128)S(1)}, f32[8,128]{1,0:T(8,128)S(1)}, u32[]{:S(2)}, u32[]{:S(2)}) collective-permute-start(f32[8,128]{1,0:T(8,128)S(1)} %max.24), channel_id=1, source_target_pairs={{0,8},{1,33},{2,10},{3,35},{4,12},{5,37},{6,14},{7,39},{8,0},{9,41... | collective-permute-start | bytes 12296 | tf_op jit(solution)/shard_map/ppermute | solution.py:527
  12.9 4.8 %collective-permute-start.2 = (f32[8,128]{1,0:T(8,128)S(1)}, f32[8,128]{1,0:T(8,128)S(1)}, u32[]{:S(2)}, u32[]{:S(2)}) collective-permute-start(f32[8,128]{1,0:T(8,128)S(1)} %max.25), channel_id=1, source_target_pairs={{0,24},{1,97},{2,26},{3,99},{4,28},{5,101},{6,30},{7,103},{8,16},{... | collective-permute-start | bytes 12296 | tf_op jit(solution)/shard_map/ppermute | solution.py:527
  17.7 3.6 %collective-permute-start.3 = (f32[8,128]{1,0:T(8,128)S(1)}, f32[8,128]{1,0:T(8,128)S(1)}, u32[]{:S(2)}, u32[]{:S(2)}) collective-permute-start(f32[8,128]{1,0:T(8,128)S(1)} %max.26), channel_id=1, source_target_pairs={{0,2},{1,33},{2,0},{3,35},{4,6},{5,37},{6,4},{7,39},{8,10},{9,41},... | collective-permute-start | bytes 12296 | tf_op jit(solution)/shard_map/ppermute | solution.py:527
  21.3 5.2 %collective-permute-start.4 = (f32[8,128]{1,0:T(8,128)S(1)}, f32[8,128]{1,0:T(8,128)S(1)}, u32[]{:S(2)}, u32[]{:S(2)}) collective-permute-start(f32[8,128]{1,0:T(8,128)S(1)} %max.27), channel_id=1, source_target_pairs={{0,6},{1,97},{2,4},{3,99},{4,2},{5,101},{6,0},{7,103},{8,14},{9,10... | collective-permute-start | bytes 12296 | tf_op jit(solution)/shard_map/ppermute | solution.py:527
  26.6 3.6 %collective-permute-start.5 = (f32[8,128]{1,0:T(8,128)S(1)}, f32[8,128]{1,0:T(8,128)S(1)}, u32[]{:S(2)}, u32[]{:S(2)}) collective-permute-start(f32[8,128]{1,0:T(8,128)S(1)} %max.28), channel_id=1, source_target_pairs={{0,32},{1,33},{2,34},{3,35},{4,36},{5,37},{6,38},{7,39},{8,40},{9,... | collective-permute-start | bytes 12296 | tf_op jit(solution)/shard_map/ppermute | solution.py:527
  30.2 8.2 %collective-permute-start.6 = (f32[8,128]{1,0:T(8,128)S(1)}, f32[8,128]{1,0:T(8,128)S(1)}, u32[]{:S(2)}, u32[]{:S(2)}) collective-permute-start(f32[8,128]{1,0:T(8,128)S(1)} %max.29), channel_id=1, source_target_pairs={{0,96},{1,97},{2,98},{3,99},{4,100},{5,101},{6,102},{7,103},{8,104... | collective-permute-start | bytes 12296 | tf_op jit(solution)/shard_map/ppermute | solution.py:527
  38.4 1.2 %collective-permute-start.7 = (f32[8,128]{1,0:T(8,128)S(1)}, f32[8,128]{1,0:T(8,128)S(1)}, u32[]{:S(2)}, u32[]{:S(2)}) collective-permute-start(f32[8,128]{1,0:T(8,128)S(1)} %max.30), channel_id=1, source_target_pairs={{0,1},{1,0},{2,3},{3,2},{4,5},{5,4},{6,7},{7,6},{8,9},{9,8},{10,11... | collective-permute-start | bytes 12296 | tf_op jit(solution)/shard_map/ppermute | solution.py:528
  42.8 11.5 %collective-permute-start.9 = (f32[2,4,8,8,128]{4,3,2,1,0:T(8,128)S(1)}, f32[2,4,8,8,128]{4,3,2,1,0:T(8,128)S(1)}, u32[]{:S(2)}, u32[]{:S(2)}) collective-permute-start(f32[2,4,8,8,128]{4,3,2,1,0:T(8,128)S(1)} %get-tuple-element.25), channel_id=1, source_target_pairs={{0,32},{32,64},{64,96},{96,0},{1,33},{33,65},{65,97},{97,1},{2,34}... | collective-permute-start | bytes 786440 | tf_op jit(solution)/shard_map/ppermute | solution.py:493
  42.9 11.5 %collective-permute-start.10 = (f32[2,4,8,8,128]{4,3,2,1,0:T(8,128)S(1)}, f32[2,4,8,8,128]{4,3,2,1,0:T(8,128)S(1)}, u32[]{:S(2)}, u32[]{:S(2)}) collective-permute-start(f32[2,4,8,8,128]{4,3,2,1,0:T(8,128)S(1)} %get-tuple-element.26), channel_id=1, source_target_pairs={{0,96},{32,0},{64,32},{96,64},{1,97},{33,1},{65,33},{97,65},{2,98}... | collective-permute-start | bytes 786440 | tf_op jit(solution)/shard_map/ppermute | solution.py:493
  46.2 8.1 %collective-permute-start.11 = (f32[2,2,8,8,128]{4,3,2,1,0:T(8,128)S(1)}, f32[2,2,8,8,128]{4,3,2,1,0:T(8,128)S(1)}, u32[]{:S(2)}, u32[]{:S(2)}) collective-permute-start(f32[2,2,8,8,128]{4,3,2,1,0:T(8,128)S(1)} %get-tuple-element.27), channel_id=1, source_target_pairs={{0,1},{1,0},{2,3},{3,2},{4,5},{5,4},{6,7},{7,6},{8,9},{9,8},{10,11... | collective-permute-start | bytes 393224 | tf_op jit(solution)/shard_map/ppermute | solution.py:500
  46.2 8.1 %collective-permute-start.12 = (f32[2,2,8,8,128]{4,3,2,1,0:T(8,128)S(1)}, f32[2,2,8,8,128]{4,3,2,1,0:T(8,128)S(1)}, u32[]{:S(2)}, u32[]{:S(2)}) collective-permute-start(f32[2,2,8,8,128]{4,3,2,1,0:T(8,128)S(1)} %get-tuple-element.28), channel_id=1, source_target_pairs={{0,31},{1,2},{2,1},{3,4},{4,3},{5,6},{6,5},{7,8},{8,7},{9,10},{10,... | collective-permute-start | bytes 393224 | tf_op jit(solution)/shard_map/ppermute | solution.py:500
  56.5 12.9 %collective-permute-start.13 = (f32[2,4,8,8,128]{4,3,2,1,0:T(8,128)S(1)}, f32[2,4,8,8,128]{4,3,2,1,0:T(8,128)S(1)}, u32[]{:S(2)}, u32[]{:S(2)}) collective-permute-start(f32[2,4,8,8,128]{4,3,2,1,0:T(8,128)S(1)} %get-tuple-element.33), channel_id=1, source_target_pairs={{0,32},{32,64},{64,96},{96,0},{1,33},{33,65},{65,97},{97,1},{2,34}... | collective-permute-start | bytes 786440 | tf_op jit(solution)/shard_map/ppermute | solution.py:493
  56.6 12.8 %collective-permute-start.14 = (f32[2,4,8,8,128]{4,3,2,1,0:T(8,128)S(1)}, f32[2,4,8,8,128]{4,3,2,1,0:T(8,128)S(1)}, u32[]{:S(2)}, u32[]{:S(2)}) collective-permute-start(f32[2,4,8,8,128]{4,3,2,1,0:T(8,128)S(1)} %get-tuple-element.34), channel_id=1, source_target_pairs={{0,96},{32,0},{64,32},{96,64},{1,97},{33,1},{65,33},{97,65},{2,98}... | collective-permute-start | bytes 786440 | tf_op jit(solution)/shard_map/ppermute | solution.py:493
  59.8 9.6 %collective-permute-start.15 = (f32[2,2,8,8,128]{4,3,2,1,0:T(8,128)S(1)}, f32[2,2,8,8,128]{4,3,2,1,0:T(8,128)S(1)}, u32[]{:S(2)}, u32[]{:S(2)}) collective-permute-start(f32[2,2,8,8,128]{4,3,2,1,0:T(8,128)S(1)} %get-tuple-element.35), channel_id=1, source_target_pairs={{0,1},{1,0},{2,3},{3,2},{4,5},{5,4},{6,7},{7,6},{8,9},{9,8},{10,11... | collective-permute-start | bytes 393224 | tf_op jit(solution)/shard_map/ppermute | solution.py:500
  59.8 9.6 %collective-permute-start.16 = (f32[2,2,8,8,128]{4,3,2,1,0:T(8,128)S(1)}, f32[2,2,8,8,128]{4,3,2,1,0:T(8,128)S(1)}, u32[]{:S(2)}, u32[]{:S(2)}) collective-permute-start(f32[2,2,8,8,128]{4,3,2,1,0:T(8,128)S(1)} %get-tuple-element.36), channel_id=1, source_target_pairs={{0,31},{1,2},{2,1},{3,4},{4,3},{5,6},{6,5},{7,8},{8,7},{9,10},{10,... | collective-permute-start | bytes 393224 | tf_op jit(solution)/shard_map/ppermute | solution.py:500
